TPU v7x, 32 devices: a whole 2x2x4 slice. The times are simulated.
32 devices in a mesh: doc: 8 (over z, y), leaf: 4 (over x, core).
Axes of the slice: x: 2, y: 2, z: 4, core: 2. Of those that a mesh axis runs over, the one named last changes fastest.
Arguments:
- features: bfloat16 [32768, 256], P(('doc', 'leaf'))
- scores: float32 [32768], P(('doc', 'leaf')), may hold values from -6 to 6
- labels: int32 [32768], P(('doc', 'leaf')), may hold values from 0 to 4
- query_ids: int32 [32768], P(('doc', 'leaf')), may hold values from 0 to 1018, as said below
- ranks: int32 [32768], P(('doc', 'leaf')), may hold values from 1 to 128, as said below
- leaf_ids: int32 [32768], P(('doc', 'leaf')), may hold values from 0 to 15
Outputs:
- gradients: float32 [32768], P(('doc', 'leaf'))
- tree_output: float32 [32768], P(('doc', 'leaf'))
- new_scores: float32 [32768], P(('doc', 'leaf'))
Inputs may be any that keep to these rules, and one draw needn't show every extreme that they name: `query_ids`: the rows of one query are contiguous; ids are 0 on the first row and rise by one at each new query; a query has 1 to 128 rows and some query has exactly 128. Within each query the ranks of its rows are the numbers 1 to its row count, each once.
All inputs are finite; a program needn't handle non-finite values.
Results may differ from a plain program's by a relative error of at most 0.0038.
Values sent between devices are 32-bit elements; how exact they have to be, the bound alone decides.
No kernel may reach another device: no remote copies, remote signals or barrier semaphores. Data moves between devices by JAX's collectives and lax.ppermute only.
A program may use at most 64 MiB of HBM per device.

v0:
```python
import jax
import jax.numpy as jnp
from jax import lax
from jax.sharding import PartitionSpec as P

LEAVES = 16
MAXQ = 128


LAMBDA = 1.0
SHRINKAGE = 0.1


def passed_along(value, axis, by):
    devices = lax.axis_size(axis)
    pairs = [(i, i + by) for i in range(devices) if 0 <= i + by < devices]
    return lax.ppermute(value, axis, pairs)


def discount(rank_values):
    return 1.0 / jnp.log2(1.0 + jnp.maximum(rank_values, 1.0))


def pair_block(own_rows, window):
    same_query = own_rows[0][:, None] == window[0][None, :]
    own_label = own_rows[1][:, None]
    far_label = window[1][None, :]
    counts = jnp.stack(
        [
            jnp.sum(jnp.where(same_query & (far_label >= grade_level), 1.0, 0.0), axis=1)
            for grade_level in (1.0, 2.0, 3.0, 4.0)
        ],
        axis=1,
    )
    positions = jnp.arange(1, MAXQ + 1).astype(jnp.float32)
    prefix = jnp.sum(
        jnp.where(
            positions[None, None, :] <= counts[:, :, None], discount(positions)[None, None, :], 0.0
        ),
        axis=2,
    )
    ideal_gain = jnp.sum(prefix * jnp.array([1.0, 2.0, 4.0, 8.0], jnp.float32)[None, :], axis=1)
    inverse = 1.0 / jnp.maximum(ideal_gain, 1.0)
    gain_gap = jnp.abs(jnp.exp2(own_label) - jnp.exp2(far_label))
    disc_gap = jnp.abs(discount(own_rows[2])[:, None] - discount(window[2])[None, :])
    direction = jnp.sign(own_label - far_label)
    weight = jnp.where(same_query, gain_gap * disc_gap, 0.0)
    pair_prob = jax.nn.sigmoid(-direction * (own_rows[3][:, None] - window[3][None, :]))
    gradient = -inverse * jnp.sum(direction * weight * pair_prob, axis=1)
    hessian = inverse * jnp.sum(weight * pair_prob * (1.0 - pair_prob), axis=1)
    return (gradient, hessian)


def solve_leaf(leaf_block):
    feature_count = leaf_block.shape[1]
    gram_matrix = leaf_block[:feature_count]
    weighted_sum = leaf_block[feature_count]
    moment = leaf_block[feature_count + 1]
    hess_total = leaf_block[feature_count + 2, 0]
    grad_total = leaf_block[feature_count + 2, 1]
    denominator = hess_total + LAMBDA
    system = (
        gram_matrix
        + LAMBDA * jnp.eye(feature_count, dtype=jnp.float32)
        - weighted_sum[:, None] * weighted_sum[None, :] / denominator
    )
    right_side = weighted_sum * grad_total / denominator - moment
    factor = jnp.linalg.cholesky(system)
    middle = lax.linalg.triangular_solve(factor, right_side[:, None], left_side=True, lower=True)
    coefficients = lax.linalg.triangular_solve(
        factor, middle, left_side=True, lower=True, transpose_a=True
    )[:, 0]
    intercept = -(grad_total + jnp.sum(weighted_sum * coefficients)) / denominator
    return (coefficients, intercept)


def body(features, scores, labels, query_ids, ranks, leaf_ids):
    row_count = features.shape[0]
    feature_count = features.shape[1]
    row_info = jnp.stack(
        [
            (query_ids + 1).astype(jnp.float32),
            labels.astype(jnp.float32),
            ranks.astype(jnp.float32),
            scores,
        ]
    )
    leading = passed_along(row_info[:, row_count - MAXQ :], ("doc", "leaf"), 1)
    trailing = passed_along(row_info[:, :MAXQ], ("doc", "leaf"), -1)
    padded = jnp.concatenate([leading, row_info, trailing], axis=1)
    block_rows = min(512, row_count)
    zero_index = jnp.zeros((), jnp.int32)

    def one_block(block_start):
        own_rows = lax.dynamic_slice(padded, (zero_index, block_start + MAXQ), (4, block_rows))
        window = lax.dynamic_slice(padded, (zero_index, block_start), (4, block_rows + 2 * MAXQ))
        return pair_block(own_rows, window)

    starts = jnp.arange(row_count // block_rows) * block_rows
    block_grads, block_hess = lax.map(one_block, starts)
    gradients = block_grads.reshape(-1)
    hessians = block_hess.reshape(-1)

    def leaf_terms(leaf_number):
        in_leaf = (leaf_ids == leaf_number).astype(jnp.float32)
        weighted = ((hessians * in_leaf)[:, None] * features).astype(jnp.bfloat16)
        gram_matrix = lax.dot_general(
            weighted, features, (((0,), (0,)), ((), ())), preferred_element_type=jnp.float32
        )
        weighted_sum = jnp.sum(weighted.astype(jnp.float32), axis=0)
        grad_low = (gradients * in_leaf).astype(jnp.bfloat16)
        moment = jnp.dot(grad_low, features, preferred_element_type=jnp.float32)
        total_rows = jnp.zeros((6, feature_count), jnp.float32)
        total_rows = (
            total_rows.at[0, 0]
            .set(jnp.sum(hessians * in_leaf))
            .at[0, 1]
            .set(jnp.sum(gradients * in_leaf))
        )
        return jnp.concatenate(
            [gram_matrix, weighted_sum[None, :], moment[None, :], total_rows], axis=0
        )

    per_owner = LEAVES // lax.axis_size("leaf")
    owner_part = lax.psum_scatter(
        lax.map(leaf_terms, jnp.arange(lax.axis_size("leaf") * per_owner)),
        "leaf",
        scatter_dimension=0,
        tiled=True,
    )
    owner_sums = lax.psum(owner_part, "doc")
    own_coefs, own_intercepts = jax.vmap(solve_leaf)(owner_sums)
    coefficients, intercepts = (
        lax.all_gather(own_coefs, "leaf", axis=0, tiled=True),
        lax.all_gather(own_intercepts, "leaf", axis=0, tiled=True),
    )
    per_leaf = (
        jnp.dot(features.astype(jnp.float32), coefficients.T, precision=lax.Precision.HIGHEST)
        + intercepts[None, :]
    )
    chosen = leaf_ids[:, None] == jnp.arange(LEAVES)[None, :]
    tree_output = jnp.sum(jnp.where(chosen, per_leaf, 0.0), axis=1)
    new_scores = scores + SHRINKAGE * tree_output
    return (gradients, tree_output, new_scores)


def solution(mesh):
    placed = (
        P(("doc", "leaf"), None),
        P(("doc", "leaf")),
        P(("doc", "leaf")),
        P(("doc", "leaf")),
        P(("doc", "leaf")),
        P(("doc", "leaf")),
    )
    return jax.shard_map(
        body,
        mesh=mesh,
        in_specs=placed,
        out_specs=(P(("doc", "leaf")), P(("doc", "leaf")), P(("doc", "leaf"))),
        check_vma=False,
    )
```

profile of v0, /device:TPU:0, one launch (start us, length us, event | category | flops | bytes accessed | tf_op | source)
XLA Modules:
  0.0 559.9 jit_solution(12895669993256081545)
XLA Ops:
  10.0 2.4 collective-permute-start
  13.7 3.8 collective-permute-done.1
  18.2 18.1 %while.32 = (s32[]{:T(128)}, f32[2,512]{1,0:T(2,128)S(1)}, f32[2,512]{1,0:T(2,128)S(1)}, s32[2]{0:T(128)S(1)}, f32[4,1280]{1,0:T(4,128)S(1)}, /*index=5*/s32[]{:...) while((s32[]{:T(128)}, f32[2,512]{1,0:T(2,128)S(1)}, ...), condition=%wide.region_9.10_spmd.clone, body=%wide.region_0.9_spmd.sunk.clone.sunk | while | flops 14173452 | bytes 159045 | solution.py:100
  22.7 3.0 multiply_reduce_fusion.5
  31.8 3.0 multiply_reduce_fusion.5
  36.4 110.6 %while.30 = (s32[]{:T(128)}, f32[16,264,256]{2,1,0:T(8,128)}, s32[16]{0:T(128)S(1)}, s32[1024]{0:T(1024)S(1)}, f32[1024]{0:T(1024)S(1)}, /*index=5*/bf16[1024,25...) while((s32[]{:T(128)}, f32[16,264,256]{2,1,0:T(8,128)}, s32[16]{0:T(128)S(1)}, ...), condition=%wide.region_14.15_spmd, body=%wide.region_10.14_spmd.sunk | while | flops 137047808 | bytes 2423457 | solution.py:126
  39.6 2.0 scatter.13
  46.5 2.0 scatter.13
  53.4 2.0 scatter.13
  60.4 2.0 scatter.13
  67.3 2.0 scatter.13
  74.2 2.0 scatter.13
  88.0 2.0 scatter.13
  94.9 2.0 scatter.13
  101.8 2.0 scatter.13
  108.8 2.0 scatter.13
  115.7 2.0 scatter.13
  122.6 2.0 scatter.13
  129.5 2.0 scatter.13
  147.0 6.1 %copy.35 = f32[16,264,256]{1,2,0:T(8,128)} copy(f32[16,264,256]{2,1,0:T(8,128)} %get-tuple-element.197) | data formatting | bytes 8650752 | tf_op jit(solution)/shard_map/while | solution.py:126
  153.2 62.5 %reduce-scatter.2.cloned.1.call-done = f32[4,264,256]{1,2,0:T(8,128)} async-done(((f32[16,264,256]{1,2,0:T(8,128)}), f32[4,264,256]{1,2,0:T(8,128)}) %reduce-scatter.2.cloned.1.call-update) | async-done | bytes 1081360 | tf_op jit(solution)/shard_map/reduce_scatter | solution.py:125
  217.1 91.5 %all-reduce.5.cloned.1.call-done = f32[4,264,256]{1,2,0:T(8,128)} async-done(((f32[4,264,256]{1,2,0:T(8,128)}), f32[4,264,256]{1,2,0:T(8,128)}) %all-reduce.5.cloned.1.call-update) | async-done | bytes 1081360 | tf_op jit(solution)/shard_map/psum | solution.py:131
  311.4 2.4 fusion.9
  316.8 47.1 %custom-call.18 = f32[4,128,128]{2,1,0:T(8,128)S(1)} custom-call(f32[4,128,128]{2,1,0:T(8,128)S(1)} %cholesky.122), custom_call_target="Cholesky" | custom-call | tf_op jit(solution)/shard_map/vmap(jit(cholesky))/cholesky | solution.py:68
  364.0 39.3 %custom-call.19 = f32[4,1,128,128]{2,3,1,0:T(8,128)S(1)} custom-call(f32[4,1,128,128]{3,2,1,0:T(8,128)S(1)} %select_bitcast_fusion), custom_call_target="InvertDiagBlocksLowerTriangular" | custom-call | tf_op jit(solution)/shard_map/vmap(jit(cholesky))/cholesky | solution.py:68
  404.4 46.9 %custom-call.20 = f32[4,128,128]{2,1,0:T(8,128)S(1)} custom-call(f32[4,128,128]{2,1,0:T(8,128)S(1)} %convolution_subtract_fusion), custom_call_target="Cholesky" | custom-call | tf_op jit(solution)/shard_map/vmap(jit(cholesky))/cholesky | solution.py:68
  451.8 5.5 while.31
  452.5 2.1 bitcast_dynamic-update-slice_fusion.2
  455.3 2.1 bitcast_dynamic-update-slice_fusion.2
  457.4 79.4 %custom-call.21 = f32[4,2,128,128]{2,3,1,0:T(8,128)S(1)} custom-call(f32[4,2,128,128]{3,2,1,0:T(8,128)} %bitcast.205), custom_call_target="InvertDiagBlocksLowerTriangular" | custom-call | tf_op jit(solution)/shard_map/vmap()/triangular_solve | solution.py:70
  539.7 5.2 all-gather
  544.9 7.0 %all-reduce.2 = f32[16]{0:T(128)S(1)} all-reduce(f32[16]{0:T(128)S(1)} %divide_dynamic-update-slice_fusion), channel_id=1, replica_groups=mesh['doc'=8,'leaf'=4] {'leaf'}, use_global_device_ids=true, to_apply=%add.2 | all-reduce | flops 16 | bytes 128
  (283 shorter events, 106.9 us)
Async XLA Ops:
  7.2 208.5 %reduce-scatter.2.cloned.1.call-start = ((), (), s32[]{:S(2)}) async-start(), calls=%async_computation.1 | async-start | bytes 7864320 | tf_op jit(solution)/shard_map/reduce_scatter | solution.py:125
  10.0 3.7 collective-permute-start
  12.3 5.2 collective-permute-start.1
  18.2 18.2 %copy-start = (bf16[1024,256]{1,0:T(8,128)(2,1)S(1)}, bf16[1024,256]{1,0:T(8,128)(2,1)}, u32[]{:S(2)}) copy-start(bf16[1024,256]{1,0:T(8,128)(2,1)} %param.15) | copy-start | bytes 1572868
  18.2 18.2 %copy-start.5 = (s32[1024]{0:T(1024)S(1)}, s32[1024]{0:T(1024)}, u32[]{:S(2)}) copy-start(s32[1024]{0:T(1024)} %param.20) | copy-start | bytes 12292
  147.0 6.1 %copy-start.4 = (f32[1024]{0:T(1024)}, f32[1024]{0:T(1024)S(1)}, u32[]{:S(2)}) copy-start(f32[1024]{0:T(1024)S(1)} %get-tuple-element.552) | copy-start | bytes 12292
  153.2 62.6 %copy-start.8 = (u32[32]{0:T(128)S(1)}, u32[32]{0:T(128)}, u32[]{:S(2)}) copy-start(u32[32]{0:T(128)} %constant.288) | copy-start | bytes 388
  153.2 155.4 %all-reduce.5.cloned.1.call-start = ((), (), s32[]{:S(2)}) async-start(), calls=%async_computation.2 | async-start | bytes 3145728 | tf_op jit(solution)/shard_map/psum | solution.py:131
  313.8 1.7 copy-start.1
  315.8 1.0 copy-start.2
  316.8 86.5 %copy-start.3 = (f32[4,256,256]{2,1,0:T(8,128)S(1)}, f32[4,256,256]{2,1,0:T(8,128)}, u32[]{:S(2)}) copy-start(f32[4,256,256]{2,1,0:T(8,128)} %copy-done.2) | copy-start | bytes 3145732
  457.4 95.1 %copy-start.6 = (f32[1024]{0:T(1024)S(1)}, f32[1024]{0:T(1024)}, u32[]{:S(2)}) copy-start(f32[1024]{0:T(1024)} %param.16) | copy-start | bytes 12292
  552.5 0.6 copy-start.7
Sparse Core Ops, SparseCore 0:
  153.3 62.3 reduce-scatter.1
  219.6 88.9 all-reduce.4
where the time goes:
time: 561 us; the launch traced here: 560 us
  other arithmetic  268 us (48%)
  waiting for transfers between devices  158 us (28%)
  local copies, waits for them, and re-layouts  80.1 us (14%)
  matrix products  15.6 us (3%)
  between operations  15 us (3%)
  blocking collectives  12.2 us (2%)
  loops' own time  7.77 us (1%)
    another operation x9, other arithmetic, solve_leaf(): factor = jnp.linalg.cholesky(system)  134 us
    psum x1, waiting for transfers between devices, body(): owner_sums = lax.psum(owner_part, 'doc')  91.5 us
    another operation x6, other arithmetic, solve_leaf(): lax.linalg.triangular_solve(factor, middle, left_side=True, lower=True, t...  79.7 us
    reduce_scatter x1, waiting for transfers between devices, body(): lax.psum_scatter(lax.map(leaf_terms, jnp.arange(lax.axis_size('leaf') * p...  62.5 us
    scatter x32, local copies, waits for them, and re-layouts, leaf_terms(): total_rows = total_rows.at[0, 0].set(jnp.sum(hessians * in_leaf)).at[0, 1...  42.9 us
    another operation x38, local copies, waits for them, and re-layouts  14.9 us
    dynamic_update_slice x16, other arithmetic, body(): lax.map(leaf_terms, jnp.arange(lax.axis_size('leaf') * per_owner))  11.9 us
  transfers between devices with their start and end apart: 4, of which 3 were waited for; matrix products, arithmetic and copies ran while one was open for 0% of the time, Pallas kernels for 0%

commit v1 on v0

v1 whole, which is shorter than its diff:
```python
import jax
import jax.numpy as jnp
import numpy as np
from jax import lax
from jax.experimental import pallas as pl
from jax.experimental.pallas import tpu as pltpu
from jax.sharding import PartitionSpec as P

LEAVES = 16
MAXQ = 128
LAMBDA = 1.0
SHRINKAGE = 0.1
AXES = ("doc", "leaf")
LANE = 128
EXTRA = 8
VMEM_LIMIT = 48 * 1024 * 1024
F32 = jnp.float32
BF16 = jnp.bfloat16


def iota(shape, dim):
    return lax.broadcasted_iota(jnp.int32, shape, dim)


def lanes_of(block_rows):
    return jnp.concatenate(
        [block_rows[b : b + 1, :] for b in range(block_rows.shape[0])], axis=1
    )


def pair_gram_kernel(
    where_ref, x_ref, score_ref, label_ref, query_ref, rank_ref, leaf_ref, before_ref, after_ref,
    grad_ref, keep_ref, send_ref,
    rows, cols, packed_cols, hess_rows, weighted, moment_s, hsum_s, total_s,
):
    blocks = score_ref.shape[0]
    n_rows, feats = x_ref.shape
    half = feats // 2
    core = where_ref[0]
    first = where_ref[1]
    last = where_ref[2]

    def with_halo(mid, slot):
        before = before_ref[slot : slot + 1, :]
        after = after_ref[slot : slot + 1, :]
        return jnp.concatenate([before, mid, after], axis=0)

    query = with_halo(query_ref[...].astype(F32), 0)
    block_at = iota(query.shape, 0)
    outside = ((block_at == 0) & (first == 1)) | ((block_at == blocks + 1) & (last == 1))
    query = jnp.where(outside, -1.0, query)
    label = with_halo(label_ref[...].astype(F32), 1)
    rank = with_halo(rank_ref[...].astype(F32), 2)
    score = with_halo(score_ref[...], 3)
    gain = jnp.exp2(label)
    disc = 1.0 / jnp.log2(1.0 + jnp.maximum(rank, 1.0))
    expo = jnp.exp(score)
    for slot, value in enumerate((query, gain, disc, expo)):
        rows[slot, 0 : blocks + 2, :] = value
        turned = value.T
        for b in range(blocks + 2):
            cols[slot, b * LANE : (b + 1) * LANE, :] = jnp.broadcast_to(
                turned[:, b : b + 1], (LANE, LANE)
            )
    grade = label.T
    turned = (
        jnp.where(grade >= 1.0, 1, 0)
        + jnp.where(grade >= 2.0, 1 << 8, 0)
        + jnp.where(grade >= 3.0, 1 << 16, 0)
        + jnp.where(grade >= 4.0, 1 << 24, 0)
    )
    for b in range(blocks + 2):
        packed_cols[b * LANE : (b + 1) * LANE, :] = jnp.broadcast_to(
            turned[:, b : b + 1], (LANE, LANE)
        )

    positions = iota((LANE, LANE), 0).astype(F32) + 1.0
    position_disc = 1.0 / jnp.log2(1.0 + positions)

    def one_block(b, carry):
        own_q = rows[0, pl.ds(b + 1, 1), :]
        own_g = rows[1, pl.ds(b + 1, 1), :]
        own_d = rows[2, pl.ds(b + 1, 1), :]
        own_e = rows[3, pl.ds(b + 1, 1), :]
        grad_sum = jnp.zeros((8, LANE), F32)
        hess_sum = jnp.zeros((8, LANE), F32)
        counts = jnp.zeros((8, LANE), jnp.int32)
        for chunk in range(3 * LANE // 8):
            at = pl.ds(pl.multiple_of(b * LANE + chunk * 8, 8), 8)
            far_e = cols[3, at, :]
            same = cols[0, at, :] == own_q
            gap = own_g - cols[1, at, :]
            signed = jnp.where(same, gap * jnp.abs(own_d - cols[2, at, :]), 0.0)
            inv = 1.0 / (own_e + far_e)
            scaled = signed * inv
            grad_sum = grad_sum + scaled * jnp.where(gap > 0.0, far_e, own_e)
            hess_sum = hess_sum + jnp.abs(scaled) * (far_e * inv)
            counts = counts + jnp.where(same, packed_cols[at, :], 0)
        count = jnp.sum(counts, axis=0, keepdims=True)
        grad = jnp.sum(grad_sum, axis=0, keepdims=True)
        hess = jnp.sum(hess_sum, axis=0, keepdims=True) * own_e
        ideal = jnp.zeros((LANE, LANE), F32)
        for k in range(4):
            count_k = (lax.shift_right_logical(count, 8 * k) & 255).astype(F32)
            ideal = ideal + jnp.where(positions <= count_k, float(1 << k), 0.0)
        ideal = jnp.sum(ideal * position_disc, axis=0, keepdims=True)
        norm = 1.0 / jnp.maximum(ideal, 1.0)
        grad_ref[pl.ds(b, 1), :] = -norm * grad
        hess_rows[pl.ds(b, 1), :] = norm * hess
        return carry

    lax.fori_loop(0, blocks, one_block, 0)

    hess_all = lanes_of(hess_rows[...])
    grad_all = lanes_of(grad_ref[...])
    leaf_all = lanes_of(leaf_ref[...])
    weighted[...] = (x_ref[...].astype(F32).T * hess_all).astype(BF16)
    member = leaf_all == iota((LEAVES, n_rows), 0)
    member_low = jnp.where(member, 1.0, 0.0).astype(BF16)
    grad_low = jnp.where(member, grad_all, 0.0).astype(BF16)
    moment_s[...] = jnp.dot(grad_low, x_ref[...], preferred_element_type=F32)
    hsum_s[...] = lax.dot_general(
        member_low, weighted[...], (((1,), (1,)), ((), ())), preferred_element_type=F32
    )
    htot = jnp.sum(jnp.where(member, hess_all, 0.0), axis=1, keepdims=True)
    gtot = jnp.sum(jnp.where(member, grad_all, 0.0), axis=1, keepdims=True)
    lane_at = iota((LEAVES, LANE), 1)
    total_s[...] = jnp.where(lane_at == 0, htot, jnp.where(lane_at == 1, gtot, 0.0))

    down = iota((half, half), 0)
    across = iota((half, half), 1)

    def one_leaf(leaf, carry):
        mask = jnp.where(leaf_all == leaf, 1.0, 0.0).astype(BF16)
        gram = jnp.dot(weighted[...] * mask, x_ref[...], preferred_element_type=F32)
        corner = gram[half:, :half]
        mixed = jnp.where(down >= across, gram[:half, :half], gram[half:, half:])
        diagonal = jnp.sum(
            jnp.where(down == across, gram[half:, half:], 0.0), axis=0, keepdims=True
        )
        hs = hsum_s[pl.ds(leaf, 1), :]
        mo = moment_s[pl.ds(leaf, 1), :]
        to = total_s[pl.ds(leaf, 1), :]
        rest = jnp.zeros((EXTRA - 4, LANE), F32)
        extra0 = jnp.concatenate([diagonal, hs[:, :half], hs[:, half:], to, rest], axis=0)
        rest = jnp.zeros((EXTRA - 2, LANE), F32)
        extra1 = jnp.concatenate([mo[:, :half], mo[:, half:], rest], axis=0)
        keep_ref[leaf, :half, :] = jnp.where(core == 0, corner, mixed)
        send_ref[leaf, :half, :] = jnp.where(core == 0, mixed, corner)
        keep_ref[leaf, half:, :] = jnp.where(core == 0, extra0, extra1)
        send_ref[leaf, half:, :] = jnp.where(core == 0, extra1, extra0)
        return carry

    lax.fori_loop(0, LEAVES, one_leaf, 0)


def pair_gram(where, x, score, label, query, rank, leaf, before, after):
    blocks = score.shape[0]
    n_rows, feats = x.shape
    vmem = pl.BlockSpec(memory_space=pltpu.VMEM)
    high = feats // 2 + EXTRA
    part = jax.ShapeDtypeStruct((LEAVES, high, LANE), F32)
    return pl.pallas_call(
        pair_gram_kernel,
        out_shape=(jax.ShapeDtypeStruct((blocks, LANE), F32), part, part),
        in_specs=[pl.BlockSpec(memory_space=pltpu.SMEM)] + [vmem] * 8,
        out_specs=(vmem, vmem, vmem),
        scratch_shapes=[
            pltpu.VMEM((4, blocks + 8, LANE), F32),
            pltpu.VMEM((4, (blocks + 2) * LANE, LANE), F32),
            pltpu.VMEM(((blocks + 2) * LANE, LANE), jnp.int32),
            pltpu.VMEM((blocks, LANE), F32),
            pltpu.VMEM((feats, n_rows), BF16),
            pltpu.VMEM((LEAVES, feats), F32),
            pltpu.VMEM((LEAVES, feats), F32),
            pltpu.VMEM((LEAVES, LANE), F32),
        ],
        compiler_params=pltpu.CompilerParams(vmem_limit_bytes=VMEM_LIMIT),
    )(where, x, score, label, query, rank, leaf, before, after)


def block_inverse(block):
    size = block.shape[0]
    down = iota((size, size), 0)
    across = iota((size, size), 1)
    for p in range(size):
        column = jnp.broadcast_to(block[:, p : p + 1], (size, size))
        pivot = column[p : p + 1, :]
        row = jnp.where(across[:1, :] == p, 1.0, block[p : p + 1, :]) / pivot
        column = jnp.where(down == p, -1.0, column)
        rest = jnp.where((down == p) | (across == p), 0.0, block)
        block = rest - column * row
    return block


def exact_dot(a, b):
    return jnp.dot(a, b, precision=lax.Precision.HIGHEST, preferred_element_type=F32)


def solve_kernel(where_ref, own_ref, other_ref, out_ref, work):
    core = where_ref[0]
    high = own_ref.shape[0]
    half = high - EXTRA
    feats = 2 * half
    copies = out_ref.shape[0]
    block = 32
    own = own_ref[...]
    other = other_ref[...]
    part0 = jnp.where(core == 0, own, other)
    part1 = jnp.where(core == 0, other, own)
    corner = part0[:half]
    mixed = part1[:half]
    turned = mixed.T
    down = iota((half, half), 0)
    across = iota((half, half), 1)
    diag_row = part0[half : half + 1]
    upper_left = jnp.where(down >= across, mixed, turned)
    lower_right = jnp.where(down < across, mixed, jnp.where(down > across, turned, diag_row))
    hs0 = part0[half + 1 : half + 2]
    hs1 = part0[half + 2 : half + 3]
    htot = part0[half + 3 : half + 4, 0:1]
    gtot = part0[half + 3 : half + 4, 1:2]
    inv_den = 1.0 / (htot + LAMBDA)
    rhs0 = hs0 * (gtot * inv_den) - part1[half : half + 1]
    rhs1 = hs1 * (gtot * inv_den) - part1[half + 1 : half + 2]
    columns = jnp.concatenate(
        [hs0, hs1, rhs0, rhs1, jnp.zeros((4, LANE), F32)], axis=0
    ).T
    hc0 = columns[:, 0:1] * inv_den
    hc1 = columns[:, 1:2] * inv_den
    eye = jnp.where(down == across, LAMBDA, 0.0)
    work[0:half, 0:half] = upper_left + eye - hc0 * hs0
    work[0:half, half:feats] = corner.T - hc0 * hs1
    work[half:feats, 0:half] = corner - hc1 * hs0
    work[half:feats, half:feats] = lower_right + eye - hc1 * hs1
    work[0:half, feats:] = jnp.where(across == 0, columns[:, 2:3], 0.0)
    work[half:feats, feats:] = jnp.where(across == 0, columns[:, 3:4], 0.0)

    for start in range(0, feats, block):
        stop = start + block
        tile = (start // LANE) * LANE
        inverse = block_inverse(work[start:stop, start:stop])
        scaled = exact_dot(inverse, work[start:stop, tile:])
        if start > 0:
            work[0:start, tile:] = work[0:start, tile:] - exact_dot(
                work[0:start, start:stop], scaled
            )
        if stop < feats:
            work[stop:feats, tile:] = work[stop:feats, tile:] - exact_dot(
                work[stop:feats, start:stop], scaled
            )
        work[start:stop, tile:] = scaled

    w0 = work[0:half, feats:].T[0:1, :]
    w1 = work[half:feats, feats:].T[0:1, :]
    dotted = jnp.sum(hs0 * w0 + hs1 * w1, axis=1, keepdims=True)
    intercept = -(gtot + dotted) * inv_den
    result = jnp.concatenate(
        [w0, w1, jnp.broadcast_to(intercept, (1, LANE)), jnp.zeros((1, LANE), F32)], axis=0
    )
    out_ref[...] = jnp.broadcast_to(result[None], (copies, 4, LANE))


def solve_leaf(where, own, other, copies):
    high = own.shape[0]
    feats = 2 * (high - EXTRA)
    vmem = pl.BlockSpec(memory_space=pltpu.VMEM)
    return pl.pallas_call(
        solve_kernel,
        out_shape=jax.ShapeDtypeStruct((copies, 4, LANE), F32),
        in_specs=[pl.BlockSpec(memory_space=pltpu.SMEM), vmem, vmem],
        out_specs=vmem,
        scratch_shapes=[pltpu.VMEM((feats, feats + LANE), F32)],
        compiler_params=pltpu.CompilerParams(vmem_limit_bytes=VMEM_LIMIT),
    )(where, own, other)


def output_kernel(owners, x_ref, coef_ref, score_ref, leaf_ref, tree_ref, new_ref):
    low = jnp.concatenate([coef_ref[d, 0:1, :] for d in owners], axis=0)
    high = jnp.concatenate([coef_ref[d, 1:2, :] for d in owners], axis=0)
    shift = jnp.concatenate([coef_ref[d, 2:3, :] for d in owners], axis=0)[:, 0:1]
    coefs = jnp.concatenate([low, high], axis=1)
    top = coefs.astype(BF16)
    left = coefs - top.astype(F32)
    middle = left.astype(BF16)
    bottom = (left - middle.astype(F32)).astype(BF16)
    stacked = jnp.concatenate([top, middle, bottom], axis=0)
    parts = lax.dot_general(
        stacked, x_ref[...], (((1,), (1,)), ((), ())), preferred_element_type=F32
    )
    per_leaf = (
        parts[:LEAVES] + (parts[LEAVES : 2 * LEAVES] + parts[2 * LEAVES :])
    ) + shift
    leaf_all = lanes_of(leaf_ref[...])
    chosen = jnp.sum(
        jnp.where(leaf_all == iota(per_leaf.shape, 0), per_leaf, 0.0), axis=0, keepdims=True
    )
    for b in range(score_ref.shape[0]):
        piece = chosen[:, b * LANE : (b + 1) * LANE]
        tree_ref[b : b + 1, :] = piece
        new_ref[b : b + 1, :] = score_ref[b : b + 1, :] + SHRINKAGE * piece


def row_outputs(owners, x, coefs, score, leaf):
    vmem = pl.BlockSpec(memory_space=pltpu.VMEM)
    shape = jax.ShapeDtypeStruct(score.shape, F32)
    return pl.pallas_call(
        lambda *refs: output_kernel(owners, *refs),
        out_shape=(shape, shape),
        in_specs=[vmem] * 4,
        out_specs=(vmem, vmem),
        compiler_params=pltpu.CompilerParams(vmem_limit_bytes=VMEM_LIMIT),
    )(x, coefs, score, leaf)


def split_plan(docs, leaf_devices):
    cores = 2
    spread = leaf_devices // cores
    low_docs = 2 if docs % 2 == 0 else 1
    high_docs = docs // low_docs

    def device(high, low, across, core):
        return (high * low_docs + low) * leaf_devices + across * cores + core

    near = [
        [device(h, l, a, c) for l in range(low_docs) for a in range(spread)]
        for h in range(high_docs)
        for c in range(cores)
    ]
    far = [
        [device(h, l, a, c) for h in range(high_docs)]
        for l in range(low_docs)
        for a in range(spread)
        for c in range(cores)
    ]
    return near, far


def reduce_groups(parts, groups, leaf_of):
    size = len(groups[0])
    held = parts.shape[0]
    if held % size == 0:
        own = held // size
        arrived = lax.all_to_all(parts, AXES, 0, 0, axis_index_groups=groups, tiled=True)
        total = jnp.sum(arrived.reshape((size, own) + parts.shape[1:]), axis=0)
        for group in groups:
            for place, device in enumerate(group):
                leaf_of[device] = leaf_of[device][place * own : (place + 1) * own]
        return total
    return lax.psum(parts, AXES, axis_index_groups=groups)


def body(features, scores, labels, query_ids, ranks, leaf_ids):
    docs = lax.axis_size("doc")
    leaf_devices = lax.axis_size("leaf")
    devices = docs * leaf_devices
    n_rows = features.shape[0]
    me = lax.axis_index(AXES)
    where = jnp.stack(
        [me % 2, (me == 0).astype(jnp.int32), (me == devices - 1).astype(jnp.int32)]
    ).astype(jnp.int32)
    blocked = [
        v.reshape(n_rows // LANE, LANE) for v in (scores, labels, query_ids, ranks, leaf_ids)
    ]
    score, label, query, rank, leaf = blocked

    def edge(block):
        return jnp.stack(
            [
                query[block].astype(F32),
                label[block].astype(F32),
                rank[block].astype(F32),
                score[block],
            ]
        )

    ahead = [(i, i + 1) for i in range(devices - 1)]
    behind = [(i + 1, i) for i in range(devices - 1)]
    before = lax.ppermute(edge(n_rows // LANE - 1), AXES, ahead)
    after = lax.ppermute(edge(0), AXES, behind)

    grad, keep, send = pair_gram(
        where, features, score, label, query, rank, leaf, before, after
    )
    swap = [(i, i ^ 1) for i in range(devices)]
    mine = keep + lax.ppermute(send, AXES, swap)

    near, far = split_plan(docs, leaf_devices)
    leaf_of = [list(range(LEAVES)) for _ in range(devices)]
    mine = reduce_groups(mine, near, leaf_of)
    mine = reduce_groups(mine, far, leaf_of)
    mine = mine[0]
    other = lax.ppermute(mine, AXES, swap)
    coefs = solve_leaf(where, mine, other, devices)
    coefs = lax.all_to_all(coefs, AXES, 0, 0, tiled=True)
    owners = [leaf_of.index([l]) for l in range(LEAVES)]
    tree, fresh = row_outputs(owners, features, coefs, score, leaf)
    return grad.reshape(-1), tree.reshape(-1), fresh.reshape(-1)


def solution(mesh):
    rows = P(AXES)
    return jax.shard_map(
        body,
        mesh=mesh,
        in_specs=(P(AXES, None), rows, rows, rows, rows, rows),
        out_specs=(rows, rows, rows),
        check_vma=False,
    )
```

time: 561 us -> 101 us (0.18)
  other arithmetic: 268 us -> 1.84 us
  waiting for transfers between devices: 158 us -> 7.39 us
  local copies, waits for them, and re-layouts: 80.1 us -> 5.25 us
  Pallas kernels: 0 us -> 36.1 us
  blocking collectives: 12.2 us -> 42.5 us
  matrix products: 15.6 us -> 0 us
  between operations: 15 us -> 0.71 us
  loops' own time: 7.77 us -> 0 us
    another operation x20 -> x3, other arithmetic: 213 us -> 0.1 us  [the longest x1 0.08 us: body(): jnp.stack([me % 2, (me == 0).astype(jnp.int32), (me == devices - 1).astyp...]
    psum x1 -> x0, waiting for transfers between devices: 91.5 us -> none  [body(): owner_sums = lax.psum(owner_part, 'doc')]
    reduce_scatter x1 -> x0, waiting for transfers between devices: 62.5 us -> none  [body(): lax.psum_scatter(lax.map(leaf_terms, jnp.arange(lax.axis_size('leaf') * p...]
    scatter x32 -> x0, local copies, waits for them, and re-layouts: 42.9 us -> none  [leaf_terms(): total_rows = total_rows.at[0, 0].set(jnp.sum(hessians * in_leaf)).at[0, 1...]
    all_to_all x0 -> x3, blocking collectives: none -> 42.5 us  [the longest x2 32.8 us: reduce_groups(): lax.all_to_all(parts, AXES, 0, 0, axis_index_groups=groups, tiled=True)]
    pallas_call x0 -> x3, Pallas kernels: none -> 36.1 us  [the longest x1 26.4 us: solve_leaf(): pl.pallas_call(solve_kernel, out_shape=jax.ShapeDtypeStruct((copies, 4, L...]
    reduce_sum x39 -> x2, other arithmetic: 23.4 us -> 0.09 us  [reduce_groups(): total = jnp.sum(arrived.reshape((size, own) + parts.shape[1:]), axis=0)]
    another operation x43 -> x0, local copies, waits for them, and re-layouts: 15.1 us -> none
where the time goes in v1:
time: 101 us; the launch traced here: 99.9 us
  blocking collectives  42.5 us (42%)
  Pallas kernels  36.1 us (36%)
  waiting for transfers between devices  7.39 us (7%)
  starting transfers between devices  6.07 us (6%)
  local copies, waits for them, and re-layouts  5.25 us (5%)
  other arithmetic  1.84 us (2%)
    all_to_all x2, blocking collectives, reduce_groups(): lax.all_to_all(parts, AXES, 0, 0, axis_index_groups=groups, tiled=True)  32.8 us
    pallas_call x1, Pallas kernels, solve_leaf(): pl.pallas_call(solve_kernel, out_shape=jax.ShapeDtypeStruct((copies, 4, L...  26.4 us
    all_to_all x1, blocking collectives, body(): coefs = lax.all_to_all(coefs, AXES, 0, 0, tiled=True)  9.7 us
    pallas_call x1, Pallas kernels, pair_gram(): pl.pallas_call(pair_gram_kernel, out_shape=(jax.ShapeDtypeStruct((blocks,...  8.89 us
    unnamed x18, local copies, waits for them, and re-layouts  4.48 us
    ppermute x1, waiting for transfers between devices, body(): after = lax.ppermute(edge(0), AXES, behind)  3.76 us
    ppermute x1, waiting for transfers between devices, body(): mine = keep + lax.ppermute(send, AXES, swap)  2.38 us
    ppermute x1, starting transfers between devices, body(): before = lax.ppermute(edge(n_rows // LANE - 1), AXES, ahead)  2.36 us
  transfers between devices with their start and end apart: 4, of which 3 were waited for; matrix products, arithmetic and copies ran while one was open for 0% of the time, Pallas kernels for 0%

profile of v1, /device:TPU:0, one launch (start us, length us, event | category | flops | bytes accessed | tf_op | source)
XLA Modules:
  0.0 99.9 jit_solution(13416006153042224770)
XLA Ops:
  0.6 0.8 slice_bitcast_fusion
  1.4 0.8 convert_bitcast_fusion.2
  2.2 0.8 convert_bitcast_fusion
  2.9 2.4 %collective-permute-start = (f32[4,128]{1,0:T(4,128)S(1)}, f32[4,128]{1,0:T(4,128)S(1)}, u32[]{:S(2)}, u32[]{:S(2)}) collective-permute-start(f32[4,128]{1,0:T(4,128)S(1)} %pad_maximum_fusion), channel_id=1, source_target_pairs={{0,1},{1,2},{2,3},{3,4},{4,5},{5,6},{6,7},{7,8},{8,9},{9,10},{10,1... | collective-permute-start | bytes 6152 | tf_op jit(solution)/shard_map/ppermute | solution.py:379
  5.3 1.3 %collective-permute-start.1 = (f32[4,128]{1,0:T(4,128)S(1)}, f32[4,128]{1,0:T(4,128)S(1)}, u32[]{:S(2)}, u32[]{:S(2)}) collective-permute-start(f32[4,128]{1,0:T(4,128)S(1)} %pad_maximum_fusion.1), channel_id=1, source_target_pairs={{1,0},{2,1},{3,2},{4,3},{5,4},{6,5},{7,6},{8,7},{9,8},{10,9},{11,1... | collective-permute-start | bytes 6152 | tf_op jit(solution)/shard_map/ppermute | solution.py:380
  6.6 0.1 pad_add_fusion.where_ref
  6.7 0.0 collective-permute-done.before_ref
  6.7 3.8 %collective-permute-done.1.after_ref = f32[4,128]{1,0:T(4,128)S(1)} collective-permute-done((f32[4,128]{1,0:T(4,128)S(1)}, f32[4,128]{1,0:T(4,128)S(1)}, u32[]{:S(2)}, u32[]{:S(2)}) %collective-permute-start.1) | collective-permute-done | bytes 2080 | tf_op jit(solution)/shard_map/ppermute | solution.py:380
  10.5 0.0 copy-start
  10.5 1.0 %copy-done = bf16[1024,256]{1,0:T(8,128)(2,1)S(1)} copy-done((bf16[1024,256]{1,0:T(8,128)(2,1)S(1)}, bf16[1024,256]{1,0:T(8,128)(2,1)}, u32[]{:S(2)}) %copy-start) | copy-done | bytes 524312
  11.5 0.0 copy-start.2
  11.5 0.7 copy-done.2
  12.2 0.0 copy-start.4
  12.2 0.7 copy-done.4
  12.9 0.7 copy-done.6
  13.6 0.7 copy-done.7
  14.3 0.7 copy-done.8
  15.0 8.9 %shard_map.85 = (f32[8,128]{1,0:T(8,128)}, f32[16,136,128]{2,1,0:T(8,128)S(1)}, f32[16,136,128]{2,1,0:T(8,128)S(1)}) custom-call(s32[3]{0:T(128)S(1)} %pad_add_fusion.where_ref, bf16[1024,256]{1,0:T(8,128)(2,1)S(1)} %copy-done, f32[8,128]{1,0:T(8,128)S(1)} %bitcast.28, s32[8,128]{1,0:T(8,128)S(1)} %bitcast.33, s32[8,128]{1,0:T(8,128)S(1)} %bitcast.32, ...), custom_call_target="tpu_custom_call" | custom-call | tf_op jit(solution)/shard_map/pallas_call | solution.py:163
  23.9 2.4 %collective-permute-start.2 = (f32[16,136,128]{2,1,0:T(8,128)S(1)}, f32[16,136,128]{2,1,0:T(8,128)S(1)}, u32[]{:S(2)}, u32[]{:S(2)}) collective-permute-start(f32[16,136,128]{2,1,0:T(8,128)S(1)} %get-tuple-element.10), channel_id=1, source_target_pairs={{0,1},{1,0},{2,3},{3,2},{4,5},{5,4},{6,7},{7,6},{8,9},{9,8},{10,11... | collective-permute-start | bytes 3342344 | tf_op jit(solution)/shard_map/ppermute | solution.py:386
  26.2 2.4 %collective-permute-done.2 = f32[16,136,128]{2,1,0:T(8,128)S(1)} collective-permute-done((f32[16,136,128]{2,1,0:T(8,128)S(1)}, f32[16,136,128]{2,1,0:T(8,128)S(1)}, u32[]{:S(2)}, u32[]{:S(2)}) %collective-permute-start.2) | collective-permute-done | bytes 1114144 | tf_op jit(solution)/shard_map/ppermute | solution.py:386
  28.6 0.1 add.12
  28.7 20.9 %all_to_all.15 = f32[16,136,128]{2,1,0:T(8,128)S(1)} all-to-all(f32[16,136,128]{2,1,0:T(8,128)S(1)} %add.12), channel_id=1, replica_groups={{0,2,4,6},{1,3,5,7},{8,10,12,14},{9,11,13,15},{16,18,20,22},{17,19,21,2..., dimensions={0} | all-to-all | bytes 2228224 | tf_op jit(solution)/shard_map/all_to_all | solution.py:344
  49.6 0.1 reduce_sum.18
  49.7 11.9 %all_to_all.16 = f32[4,136,128]{2,1,0:T(8,128)S(1)} all-to-all(f32[4,136,128]{2,1,0:T(8,128)S(1)} %reduce_sum.18), channel_id=1, replica_groups={{0,8,16,24},{1,9,17,25},{2,10,18,26},{3,11,19,27},{4,12,20,28},{5,13,21..., dimensions={0} | all-to-all | bytes 557056 | tf_op jit(solution)/shard_map/all_to_all | solution.py:344
  61.6 0.1 collective-permute-start.3
  61.7 1.2 %collective-permute-done.3.other_ref = f32[136,128]{1,0:T(8,128)S(1)} collective-permute-done((f32[136,128]{1,0:T(8,128)S(1)}, f32[136,128]{1,0:T(8,128)S(1)}, u32[]{:S(2)}, u32[]{:S(2)}) %collective-permute-start.3) | collective-permute-done | bytes 69664 | tf_op jit(solution)/shard_map/ppermute | solution.py:393
  63.0 26.4 %shard_map.86 = f32[32,4,128]{2,1,0:T(4,128)S(1)} custom-call(s32[3]{0:T(128)S(1)} %pad_add_fusion.where_ref, f32[136,128]{1,0:T(8,128)S(1)} %reduce_sum.19.own_ref, f32[136,128]{1,0:T(8,128)S(1)} %collective-permute-done.3.other_ref), custom_call_target="tpu_custom_call" | custom-call | tf_op jit(solution)/shard_map/pallas_call | solution.py:268
  89.3 9.7 %all_to_all.17.refs_1_ = f32[32,4,128]{2,1,0:T(4,128)S(1)} all-to-all(f32[32,4,128]{2,1,0:T(4,128)S(1)} %shard_map.86), channel_id=1, replica_groups=mesh['doc'=8,'leaf'=4] {'doc','leaf'}, dimensions={0} | all-to-all | bytes 131072 | tf_op jit(solution)/shard_map/all_to_all | solution.py:395
  99.0 0.0 copy-done.1
  99.0 0.0 copy-done.3
  99.0 0.0 copy-done.5
  99.0 0.9 shard_map.87
  (9 shorter events, 0.0 us)
Async XLA Ops:
  2.9 3.8 %collective-permute-start = (f32[4,128]{1,0:T(4,128)S(1)}, f32[4,128]{1,0:T(4,128)S(1)}, u32[]{:S(2)}, u32[]{:S(2)}) collective-permute-start(f32[4,128]{1,0:T(4,128)S(1)} %pad_maximum_fusion), channel_id=1, source_target_pairs={{0,1},{1,2},{2,3},{3,4},{4,5},{5,6},{6,7},{7,8},{8,9},{9,10},{10,1... | collective-permute-start | bytes 6152 | tf_op jit(solution)/shard_map/ppermute | solution.py:379
  5.3 5.2 %collective-permute-start.1 = (f32[4,128]{1,0:T(4,128)S(1)}, f32[4,128]{1,0:T(4,128)S(1)}, u32[]{:S(2)}, u32[]{:S(2)}) collective-permute-start(f32[4,128]{1,0:T(4,128)S(1)} %pad_maximum_fusion.1), channel_id=1, source_target_pairs={{1,0},{2,1},{3,2},{4,3},{5,4},{6,5},{7,6},{8,7},{9,8},{10,9},{11,1... | collective-permute-start | bytes 6152 | tf_op jit(solution)/shard_map/ppermute | solution.py:380
  10.5 1.0 %copy-start = (bf16[1024,256]{1,0:T(8,128)(2,1)S(1)}, bf16[1024,256]{1,0:T(8,128)(2,1)}, u32[]{:S(2)}) copy-start(bf16[1024,256]{1,0:T(8,128)(2,1)} %refs_0_.1) | copy-start | bytes 1572868
  11.5 0.7 copy-start.2
  12.2 0.7 copy-start.4
  12.9 0.7 copy-start.6
  13.6 0.7 copy-start.7
  14.3 0.7 copy-start.8
  23.9 4.7 %collective-permute-start.2 = (f32[16,136,128]{2,1,0:T(8,128)S(1)}, f32[16,136,128]{2,1,0:T(8,128)S(1)}, u32[]{:S(2)}, u32[]{:S(2)}) collective-permute-start(f32[16,136,128]{2,1,0:T(8,128)S(1)} %get-tuple-element.10), channel_id=1, source_target_pairs={{0,1},{1,0},{2,3},{3,2},{4,5},{5,4},{6,7},{7,6},{8,9},{9,8},{10,11... | collective-permute-start | bytes 3342344 | tf_op jit(solution)/shard_map/ppermute | solution.py:386
  49.6 49.5 %copy-start.1 = (bf16[1024,256]{1,0:T(8,128)(2,1)S(1)}, bf16[1024,256]{1,0:T(8,128)(2,1)}, u32[]{:S(2)}) copy-start(bf16[1024,256]{1,0:T(8,128)(2,1)} %refs_0_.1) | copy-start | bytes 1572868
  49.6 49.5 %copy-start.3 = (f32[1024]{0:T(1024)S(1)}, f32[1024]{0:T(1024)}, u32[]{:S(2)}) copy-start(f32[1024]{0:T(1024)} %param.7) | copy-start | bytes 12292
  49.6 49.5 %copy-start.5 = (s32[1024]{0:T(1024)S(1)}, s32[1024]{0:T(1024)}, u32[]{:S(2)}) copy-start(s32[1024]{0:T(1024)} %param.11) | copy-start | bytes 12292
  61.6 1.3 %collective-permute-start.3 = (f32[136,128]{1,0:T(8,128)S(1)}, f32[136,128]{1,0:T(8,128)S(1)}, u32[]{:S(2)}, u32[]{:S(2)}) collective-permute-start(f32[136,128]{1,0:T(8,128)S(1)} %reduce_sum.19.own_ref), channel_id=1, source_target_pairs={{0,1},{1,0},{2,3},{3,2},{4,5},{5,4},{6,7},{7,6},{8,9},{9,8},{10,11... | collective-permute-start | bytes 208904 | tf_op jit(solution)/shard_map/ppermute | solution.py:393

commit v2 on v1

--- a/solution.py
+++ b/solution.py
@@ -13,6 +13,8 @@
 AXES = ("doc", "leaf")
 LANE = 128
 EXTRA = 8
+STRIP = 32
+GROUP = 16
 VMEM_LIMIT = 48 * 1024 * 1024
 F32 = jnp.float32
 BF16 = jnp.bfloat16
@@ -179,31 +181,37 @@
     )(where, x, score, label, query, rank, leaf, before, after)
 
 
-def block_inverse(block):
-    size = block.shape[0]
-    down = iota((size, size), 0)
-    across = iota((size, size), 1)
-    for p in range(size):
-        column = jnp.broadcast_to(block[:, p : p + 1], (size, size))
-        pivot = column[p : p + 1, :]
-        row = jnp.where(across[:1, :] == p, 1.0, block[p : p + 1, :]) / pivot
-        column = jnp.where(down == p, -1.0, column)
-        rest = jnp.where((down == p) | (across == p), 0.0, block)
-        block = rest - column * row
-    return block
+def eliminate(tiles, at, offset):
+    size = tiles[at].shape[0]
+    down = iota((size, LANE), 0)
+    scale = jnp.ones((size, LANE), F32)
+    for base in range(0, size, GROUP):
+        first = offset + base
+        columns = [
+            jnp.broadcast_to(tiles[at][:, first + j : first + j + 1], (size, LANE))
+            for j in range(GROUP)
+        ]
+        for j in range(GROUP):
+            p = base + j
+            inverse = 1.0 / columns[j][p : p + 1, :]
+            scale = jnp.where(down == p, inverse, scale)
+            factor = jnp.where(down == p, 0.0, columns[j]) * inverse
+            for k in range(j + 1, GROUP):
+                columns[k] = columns[k] - factor * columns[k][p : p + 1, :]
+            tiles = [t if t is None else t - factor * t[p : p + 1, :] for t in tiles]
+    return [t if t is None else t * scale for t in tiles]
 
 
 def exact_dot(a, b):
     return jnp.dot(a, b, precision=lax.Precision.HIGHEST, preferred_element_type=F32)
 
 
-def solve_kernel(where_ref, own_ref, other_ref, out_ref, work):
+def solve_kernel(where_ref, own_ref, other_ref, out_ref):
     core = where_ref[0]
     high = own_ref.shape[0]
     half = high - EXTRA
     feats = 2 * half
     copies = out_ref.shape[0]
-    block = 32
     own = own_ref[...]
     other = other_ref[...]
     part0 = jnp.where(core == 0, own, other)
@@ -229,30 +237,46 @@
     hc0 = columns[:, 0:1] * inv_den
     hc1 = columns[:, 1:2] * inv_den
     eye = jnp.where(down == across, LAMBDA, 0.0)
-    work[0:half, 0:half] = upper_left + eye - hc0 * hs0
-    work[0:half, half:feats] = corner.T - hc0 * hs1
-    work[half:feats, 0:half] = corner - hc1 * hs0
-    work[half:feats, half:feats] = lower_right + eye - hc1 * hs1
-    work[0:half, feats:] = jnp.where(across == 0, columns[:, 2:3], 0.0)
-    work[half:feats, feats:] = jnp.where(across == 0, columns[:, 3:4], 0.0)
-
-    for start in range(0, feats, block):
-        stop = start + block
-        tile = (start // LANE) * LANE
-        inverse = block_inverse(work[start:stop, start:stop])
-        scaled = exact_dot(inverse, work[start:stop, tile:])
-        if start > 0:
-            work[0:start, tile:] = work[0:start, tile:] - exact_dot(
-                work[0:start, start:stop], scaled
+    top = [
+        upper_left + eye - hc0 * hs0,
+        corner.T - hc0 * hs1,
+        jnp.where(across == 0, columns[:, 2:3], 0.0),
+    ]
+    low = [
+        corner - hc1 * hs0,
+        lower_right + eye - hc1 * hs1,
+        jnp.where(across == 0, columns[:, 3:4], 0.0),
+    ]
+    per_tile = LANE // STRIP
+    count = feats // STRIP
+    strips = []
+    for s in range(count):
+        source = top if s < per_tile else low
+        start = (s % per_tile) * STRIP
+        strips.append([t[start : start + STRIP] for t in source])
+    for s in range(count):
+        tile, offset = s // per_tile, (s % per_tile) * STRIP
+        done = eliminate([None] * tile + strips[s][tile:], tile, offset)
+        strips[s] = done
+        solved = jnp.concatenate(done[tile:], axis=1)
+        later = [s + 1] if s + 1 < count else []
+        others = [i for i in range(count) if i not in (s, s + 1)]
+        for group in (later, others):
+            if not group:
+                continue
+            left = jnp.concatenate(
+                [strips[i][tile][:, offset : offset + STRIP] for i in group], axis=0
             )
-        if stop < feats:
-            work[stop:feats, tile:] = work[stop:feats, tile:] - exact_dot(
-                work[stop:feats, start:stop], scaled
-            )
-        work[start:stop, tile:] = scaled
-
-    w0 = work[0:half, feats:].T[0:1, :]
-    w1 = work[half:feats, feats:].T[0:1, :]
+            change = exact_dot(left, solved)
+            for q, i in enumerate(group):
+                part = change[q * STRIP : (q + 1) * STRIP]
+                strips[i] = [
+                    t if n < tile else t - part[:, (n - tile) * LANE : (n - tile + 1) * LANE]
+                    for n, t in enumerate(strips[i])
+                ]
+    right = [strips[s][2] for s in range(count)]
+    w0 = jnp.concatenate(right[:per_tile], axis=0).T[0:1, :]
+    w1 = jnp.concatenate(right[per_tile:], axis=0).T[0:1, :]
     dotted = jnp.sum(hs0 * w0 + hs1 * w1, axis=1, keepdims=True)
     intercept = -(gtot + dotted) * inv_den
     result = jnp.concatenate(
@@ -263,14 +287,12 @@
 
 def solve_leaf(where, own, other, copies):
     high = own.shape[0]
-    feats = 2 * (high - EXTRA)
     vmem = pl.BlockSpec(memory_space=pltpu.VMEM)
     return pl.pallas_call(
         solve_kernel,
         out_shape=jax.ShapeDtypeStruct((copies, 4, LANE), F32),
         in_specs=[pl.BlockSpec(memory_space=pltpu.SMEM), vmem, vmem],
         out_specs=vmem,
-        scratch_shapes=[pltpu.VMEM((feats, feats + LANE), F32)],
         compiler_params=pltpu.CompilerParams(vmem_limit_bytes=VMEM_LIMIT),
     )(where, own, other)
 

time: 101 us -> 82.7 us (0.82)
  Pallas kernels: 36.1 us -> 18.3 us
    pallas_call x1, Pallas kernels: 26.4 us -> 8.56 us  [solve_leaf(): pl.pallas_call(solve_kernel, out_shape=jax.ShapeDtypeStruct((copies, 4, L...]
where the time goes in v2:
time: 82.7 us; the launch traced here: 82.1 us
  blocking collectives  42.5 us (51%)
  Pallas kernels  18.3 us (22%)
  waiting for transfers between devices  7.39 us (9%)
  starting transfers between devices  6.07 us (7%)
  local copies, waits for them, and re-layouts  5.25 us (6%)
  other arithmetic  1.84 us (2%)
    all_to_all x2, blocking collectives, reduce_groups(): lax.all_to_all(parts, AXES, 0, 0, axis_index_groups=groups, tiled=True)  32.8 us
    all_to_all x1, blocking collectives, body(): coefs = lax.all_to_all(coefs, AXES, 0, 0, tiled=True)  9.72 us
    pallas_call x1, Pallas kernels, pair_gram(): pl.pallas_call(pair_gram_kernel, out_shape=(jax.ShapeDtypeStruct((blocks,...  8.89 us
    pallas_call x1, Pallas kernels, solve_leaf(): pl.pallas_call(solve_kernel, out_shape=jax.ShapeDtypeStruct((copies, 4, L...  8.56 us
    unnamed x18, local copies, waits for them, and re-layouts  4.48 us
    ppermute x1, waiting for transfers between devices, body(): after = lax.ppermute(edge(0), AXES, behind)  3.76 us
    ppermute x1, waiting for transfers between devices, body(): mine = keep + lax.ppermute(send, AXES, swap)  2.38 us
    ppermute x1, starting transfers between devices, body(): before = lax.ppermute(edge(n_rows // LANE - 1), AXES, ahead)  2.36 us
  transfers between devices with their start and end apart: 4, of which 3 were waited for; matrix products, arithmetic and copies ran while one was open for 0% of the time, Pallas kernels for 0%

profile of v2, /device:TPU:0, one launch (start us, length us, event | category | flops | bytes accessed | tf_op | source)
XLA Modules:
  0.0 82.1 jit_solution(13570889833108449035)
XLA Ops:
  0.6 0.8 slice_bitcast_fusion
  1.4 0.8 convert_bitcast_fusion.2
  2.2 0.8 convert_bitcast_fusion
  2.9 2.4 %collective-permute-start = (f32[4,128]{1,0:T(4,128)S(1)}, f32[4,128]{1,0:T(4,128)S(1)}, u32[]{:S(2)}, u32[]{:S(2)}) collective-permute-start(f32[4,128]{1,0:T(4,128)S(1)} %pad_maximum_fusion), channel_id=1, source_target_pairs={{0,1},{1,2},{2,3},{3,4},{4,5},{5,6},{6,7},{7,8},{8,9},{9,10},{10,1... | collective-permute-start | bytes 6152 | tf_op jit(solution)/shard_map/ppermute | solution.py:401
  5.3 1.3 %collective-permute-start.1 = (f32[4,128]{1,0:T(4,128)S(1)}, f32[4,128]{1,0:T(4,128)S(1)}, u32[]{:S(2)}, u32[]{:S(2)}) collective-permute-start(f32[4,128]{1,0:T(4,128)S(1)} %pad_maximum_fusion.1), channel_id=1, source_target_pairs={{1,0},{2,1},{3,2},{4,3},{5,4},{6,5},{7,6},{8,7},{9,8},{10,9},{11,1... | collective-permute-start | bytes 6152 | tf_op jit(solution)/shard_map/ppermute | solution.py:402
  6.6 0.1 pad_add_fusion.where_ref
  6.7 0.0 collective-permute-done.before_ref
  6.7 3.8 %collective-permute-done.1.after_ref = f32[4,128]{1,0:T(4,128)S(1)} collective-permute-done((f32[4,128]{1,0:T(4,128)S(1)}, f32[4,128]{1,0:T(4,128)S(1)}, u32[]{:S(2)}, u32[]{:S(2)}) %collective-permute-start.1) | collective-permute-done | bytes 2080 | tf_op jit(solution)/shard_map/ppermute | solution.py:402
  10.5 0.0 copy-start
  10.5 1.0 %copy-done = bf16[1024,256]{1,0:T(8,128)(2,1)S(1)} copy-done((bf16[1024,256]{1,0:T(8,128)(2,1)S(1)}, bf16[1024,256]{1,0:T(8,128)(2,1)}, u32[]{:S(2)}) %copy-start) | copy-done | bytes 524312
  11.5 0.0 copy-start.2
  11.5 0.7 copy-done.2
  12.2 0.0 copy-start.4
  12.2 0.7 copy-done.4
  12.9 0.7 copy-done.6
  13.6 0.7 copy-done.7
  14.3 0.7 copy-done.8
  15.0 8.9 %shard_map.85 = (f32[8,128]{1,0:T(8,128)}, f32[16,136,128]{2,1,0:T(8,128)S(1)}, f32[16,136,128]{2,1,0:T(8,128)S(1)}) custom-call(s32[3]{0:T(128)S(1)} %pad_add_fusion.where_ref, bf16[1024,256]{1,0:T(8,128)(2,1)S(1)} %copy-done, f32[8,128]{1,0:T(8,128)S(1)} %bitcast.28, s32[8,128]{1,0:T(8,128)S(1)} %bitcast.33, s32[8,128]{1,0:T(8,128)S(1)} %bitcast.32, ...), custom_call_target="tpu_custom_call" | custom-call | tf_op jit(solution)/shard_map/pallas_call | solution.py:165
  23.9 2.4 %collective-permute-start.2 = (f32[16,136,128]{2,1,0:T(8,128)S(1)}, f32[16,136,128]{2,1,0:T(8,128)S(1)}, u32[]{:S(2)}, u32[]{:S(2)}) collective-permute-start(f32[16,136,128]{2,1,0:T(8,128)S(1)} %get-tuple-element.10), channel_id=1, source_target_pairs={{0,1},{1,0},{2,3},{3,2},{4,5},{5,4},{6,7},{7,6},{8,9},{9,8},{10,11... | collective-permute-start | bytes 3342344 | tf_op jit(solution)/shard_map/ppermute | solution.py:408
  26.2 2.4 %collective-permute-done.2 = f32[16,136,128]{2,1,0:T(8,128)S(1)} collective-permute-done((f32[16,136,128]{2,1,0:T(8,128)S(1)}, f32[16,136,128]{2,1,0:T(8,128)S(1)}, u32[]{:S(2)}, u32[]{:S(2)}) %collective-permute-start.2) | collective-permute-done | bytes 1114144 | tf_op jit(solution)/shard_map/ppermute | solution.py:408
  28.6 0.1 add.12
  28.7 20.9 %all_to_all.15 = f32[16,136,128]{2,1,0:T(8,128)S(1)} all-to-all(f32[16,136,128]{2,1,0:T(8,128)S(1)} %add.12), channel_id=1, replica_groups={{0,2,4,6},{1,3,5,7},{8,10,12,14},{9,11,13,15},{16,18,20,22},{17,19,21,2..., dimensions={0} | all-to-all | bytes 2228224 | tf_op jit(solution)/shard_map/all_to_all | solution.py:366
  49.6 0.1 reduce_sum.18
  49.7 11.9 %all_to_all.16 = f32[4,136,128]{2,1,0:T(8,128)S(1)} all-to-all(f32[4,136,128]{2,1,0:T(8,128)S(1)} %reduce_sum.18), channel_id=1, replica_groups={{0,8,16,24},{1,9,17,25},{2,10,18,26},{3,11,19,27},{4,12,20,28},{5,13,21..., dimensions={0} | all-to-all | bytes 557056 | tf_op jit(solution)/shard_map/all_to_all | solution.py:366
  61.6 0.1 collective-permute-start.3
  61.7 1.2 %collective-permute-done.3.other_ref = f32[136,128]{1,0:T(8,128)S(1)} collective-permute-done((f32[136,128]{1,0:T(8,128)S(1)}, f32[136,128]{1,0:T(8,128)S(1)}, u32[]{:S(2)}, u32[]{:S(2)}) %collective-permute-start.3) | collective-permute-done | bytes 69664 | tf_op jit(solution)/shard_map/ppermute | solution.py:415
  63.0 8.6 %shard_map.86 = f32[32,4,128]{2,1,0:T(4,128)S(1)} custom-call(s32[3]{0:T(128)S(1)} %pad_add_fusion.where_ref, f32[136,128]{1,0:T(8,128)S(1)} %reduce_sum.19.own_ref, f32[136,128]{1,0:T(8,128)S(1)} %collective-permute-done.3.other_ref), custom_call_target="tpu_custom_call" | custom-call | tf_op jit(solution)/shard_map/pallas_call | solution.py:291
  71.5 9.7 %all_to_all.17.refs_1_ = f32[32,4,128]{2,1,0:T(4,128)S(1)} all-to-all(f32[32,4,128]{2,1,0:T(4,128)S(1)} %shard_map.86), channel_id=1, replica_groups=mesh['doc'=8,'leaf'=4] {'doc','leaf'}, dimensions={0} | all-to-all | bytes 131072 | tf_op jit(solution)/shard_map/all_to_all | solution.py:417
  81.3 0.0 copy-done.1
  81.3 0.0 copy-done.3
  81.3 0.0 copy-done.5
  81.3 0.9 %shard_map.87 = (f32[8,128]{1,0:T(8,128)}, f32[8,128]{1,0:T(8,128)}) custom-call(bf16[1024,256]{1,0:T(8,128)(2,1)S(1)} %copy-done.1, f32[32,4,128]{2,1,0:T(4,128)S(1)} %all_to_all.17.refs_1_, f32[8,128]{1,0:T(8,128)S(1)} %bitcast.29, s32[8,128]{1,0:T(8,128)S(1)} %bitcast.31), custom_call_target="tpu_custom_call" | custom-call | tf_op jit(solution)/shard_map/pallas_call | solution.py:329
  (9 shorter events, 0.0 us)
Async XLA Ops:
  2.9 3.8 %collective-permute-start = (f32[4,128]{1,0:T(4,128)S(1)}, f32[4,128]{1,0:T(4,128)S(1)}, u32[]{:S(2)}, u32[]{:S(2)}) collective-permute-start(f32[4,128]{1,0:T(4,128)S(1)} %pad_maximum_fusion), channel_id=1, source_target_pairs={{0,1},{1,2},{2,3},{3,4},{4,5},{5,6},{6,7},{7,8},{8,9},{9,10},{10,1... | collective-permute-start | bytes 6152 | tf_op jit(solution)/shard_map/ppermute | solution.py:401
  5.3 5.2 %collective-permute-start.1 = (f32[4,128]{1,0:T(4,128)S(1)}, f32[4,128]{1,0:T(4,128)S(1)}, u32[]{:S(2)}, u32[]{:S(2)}) collective-permute-start(f32[4,128]{1,0:T(4,128)S(1)} %pad_maximum_fusion.1), channel_id=1, source_target_pairs={{1,0},{2,1},{3,2},{4,3},{5,4},{6,5},{7,6},{8,7},{9,8},{10,9},{11,1... | collective-permute-start | bytes 6152 | tf_op jit(solution)/shard_map/ppermute | solution.py:402
  10.5 1.0 %copy-start = (bf16[1024,256]{1,0:T(8,128)(2,1)S(1)}, bf16[1024,256]{1,0:T(8,128)(2,1)}, u32[]{:S(2)}) copy-start(bf16[1024,256]{1,0:T(8,128)(2,1)} %refs_0_.1) | copy-start | bytes 1572868
  11.5 0.7 copy-start.2
  12.2 0.7 copy-start.4
  12.9 0.7 copy-start.6
  13.6 0.7 copy-start.7
  14.3 0.7 copy-start.8
  23.9 4.7 %collective-permute-start.2 = (f32[16,136,128]{2,1,0:T(8,128)S(1)}, f32[16,136,128]{2,1,0:T(8,128)S(1)}, u32[]{:S(2)}, u32[]{:S(2)}) collective-permute-start(f32[16,136,128]{2,1,0:T(8,128)S(1)} %get-tuple-element.10), channel_id=1, source_target_pairs={{0,1},{1,0},{2,3},{3,2},{4,5},{5,4},{6,7},{7,6},{8,9},{9,8},{10,11... | collective-permute-start | bytes 3342344 | tf_op jit(solution)/shard_map/ppermute | solution.py:408
  49.6 31.7 %copy-start.1 = (bf16[1024,256]{1,0:T(8,128)(2,1)S(1)}, bf16[1024,256]{1,0:T(8,128)(2,1)}, u32[]{:S(2)}) copy-start(bf16[1024,256]{1,0:T(8,128)(2,1)} %refs_0_.1) | copy-start | bytes 1572868
  49.6 31.7 %copy-start.3 = (f32[1024]{0:T(1024)S(1)}, f32[1024]{0:T(1024)}, u32[]{:S(2)}) copy-start(f32[1024]{0:T(1024)} %param.7) | copy-start | bytes 12292
  49.6 31.7 %copy-start.5 = (s32[1024]{0:T(1024)S(1)}, s32[1024]{0:T(1024)}, u32[]{:S(2)}) copy-start(s32[1024]{0:T(1024)} %param.11) | copy-start | bytes 12292
  61.6 1.3 %collective-permute-start.3 = (f32[136,128]{1,0:T(8,128)S(1)}, f32[136,128]{1,0:T(8,128)S(1)}, u32[]{:S(2)}, u32[]{:S(2)}) collective-permute-start(f32[136,128]{1,0:T(8,128)S(1)} %reduce_sum.19.own_ref), channel_id=1, source_target_pairs={{0,1},{1,0},{2,3},{3,2},{4,5},{5,4},{6,7},{7,6},{8,9},{9,8},{10,11... | collective-permute-start | bytes 208904 | tf_op jit(solution)/shard_map/ppermute | solution.py:415

commit v3 on v2

v3 whole, which is shorter than its diff:
```python
import jax
import jax.numpy as jnp
import numpy as np
from jax import lax
from jax.experimental import pallas as pl
from jax.experimental.pallas import tpu as pltpu
from jax.sharding import PartitionSpec as P

LEAVES = 16
MAXQ = 128
LAMBDA = 1.0
SHRINKAGE = 0.1
AXES = ("doc", "leaf")
LANE = 128
EXTRA = 8
STRIP = 32
GROUP = 16
NEAR = tuple(range(0, 16, 2))
GATHER = ((0, 2, 1, 3), (0, 4, 8, 12))
UNROLL = 2
VMEM_LIMIT = 48 * 1024 * 1024
F32 = jnp.float32
BF16 = jnp.bfloat16


def iota(shape, dim):
    return lax.broadcasted_iota(jnp.int32, shape, dim)


def lanes_of(block_rows):
    return jnp.concatenate(
        [block_rows[b : b + 1, :] for b in range(block_rows.shape[0])], axis=1
    )


def position():
    return lax.axis_index("doc") * lax.axis_size("leaf") + lax.axis_index("leaf")


def slot_mask(me):
    return (me & 1) * 8 + ((me >> 2) & 3) * 2 + ((me >> 1) & 1)


def fetch(sources, places, sems):
    copies = [
        pltpu.make_async_copy(src, dst, sems.at[n])
        for n, (src, dst) in enumerate(zip(sources, places))
    ]
    for copy in copies:
        copy.start()
    return copies


def edge_kernel(
    query_hbm, label_hbm, rank_hbm, score_hbm, leaf_hbm,
    inner_ref, outer_ref, table_ref, query, label, rank, score, leaf, sems,
):
    odd = (position() & 1) == 1
    copies = fetch(
        (query_hbm, label_hbm, rank_hbm, score_hbm, leaf_hbm),
        (query, label, rank, score, leaf),
        sems,
    )
    blocks = query.shape[0]
    for copy in copies:
        copy.wait()
    for n, ref in enumerate((query, label, rank, score, leaf)):
        value = ref[...].astype(F32)
        table_ref[n] = value
        if n < 4:
            first, last = value[0:1, :], value[blocks - 1 : blocks, :]
            inner_ref[n : n + 1, :] = jnp.where(odd, first, last)
            outer_ref[n : n + 1, :] = jnp.where(odd, last, first)


def edges(query, label, rank, score, leaf):
    blocks = score.shape[0]
    anywhere = pl.BlockSpec(memory_space=pltpu.HBM)
    vmem = pl.BlockSpec(memory_space=pltpu.VMEM)
    edge = jax.ShapeDtypeStruct((4, LANE), F32)
    whole = pltpu.VMEM((blocks, LANE), jnp.int32)
    return pl.pallas_call(
        edge_kernel,
        out_shape=(edge, edge, jax.ShapeDtypeStruct((5, blocks, LANE), F32)),
        in_specs=[anywhere] * 5,
        out_specs=(vmem,) * 3,
        scratch_shapes=[whole, whole, whole, pltpu.VMEM((blocks, LANE), F32), whole]
        + [pltpu.SemaphoreType.DMA((5,))],
    )(query, label, rank, score, leaf)


def pair_tables(query, label, rank, score, rows, cols, packed_cols):
    count = query.shape[0]
    gain = jnp.exp2(label)
    disc = 1.0 / jnp.log2(1.0 + jnp.maximum(rank, 1.0))
    expo = jnp.exp(score)
    for slot, value in enumerate((query, gain, disc, expo)):
        rows[slot, 0:count, :] = value
        turned = value.T
        for b in range(count):
            cols[slot, b * LANE : (b + 1) * LANE, :] = jnp.broadcast_to(
                turned[:, b : b + 1], (LANE, LANE)
            )
    grade = label.T
    turned = (
        jnp.where(grade >= 1.0, 1, 0)
        + jnp.where(grade >= 2.0, 1 << 8, 0)
        + jnp.where(grade >= 3.0, 1 << 16, 0)
        + jnp.where(grade >= 4.0, 1 << 24, 0)
    )
    for b in range(count):
        packed_cols[b * LANE : (b + 1) * LANE, :] = jnp.broadcast_to(
            turned[:, b : b + 1], (LANE, LANE)
        )


def pair_block(own, start, rows, cols, packed_cols):
    positions = iota((LANE, LANE), 0).astype(F32) + 1.0
    position_disc = 1.0 / jnp.log2(1.0 + positions)
    own_q = rows[0, pl.ds(own, 1), :]
    own_g = rows[1, pl.ds(own, 1), :]
    own_d = rows[2, pl.ds(own, 1), :]
    own_e = rows[3, pl.ds(own, 1), :]
    grad_sum = jnp.zeros((8, LANE), F32)
    hess_sum = jnp.zeros((8, LANE), F32)
    counts = jnp.zeros((8, LANE), jnp.int32)
    for chunk in range(3 * LANE // 8):
        at = pl.ds(pl.multiple_of(start * LANE + chunk * 8, 8), 8)
        far_e = cols[3, at, :]
        same = cols[0, at, :] == own_q
        gap = own_g - cols[1, at, :]
        signed = jnp.where(same, gap * jnp.abs(own_d - cols[2, at, :]), 0.0)
        inv = 1.0 / (own_e + far_e)
        scaled = signed * inv
        grad_sum = grad_sum + scaled * jnp.where(gap > 0.0, far_e, own_e)
        hess_sum = hess_sum + jnp.abs(scaled) * (far_e * inv)
        counts = counts + jnp.where(same, packed_cols[at, :], 0)
    count = jnp.sum(counts, axis=0, keepdims=True)
    grad = jnp.sum(grad_sum, axis=0, keepdims=True)
    hess = jnp.sum(hess_sum, axis=0, keepdims=True) * own_e
    ideal = jnp.zeros((LANE, LANE), F32)
    for k in range(4):
        count_k = (lax.shift_right_logical(count, 8 * k) & 255).astype(F32)
        ideal = ideal + jnp.where(positions <= count_k, float(1 << k), 0.0)
    ideal = jnp.sum(ideal * position_disc, axis=0, keepdims=True)
    norm = 1.0 / jnp.maximum(ideal, 1.0)
    return -norm * grad, norm * hess


def leaf_sums(x, turned, hess_all, grad_all, leaf_all, weighted, moment_s, hsum_s, total_s):
    n_rows = leaf_all.shape[1]
    weighted[...] = (turned * hess_all).astype(BF16)
    member = leaf_all == iota((LEAVES, n_rows), 0)
    member_low = jnp.where(member, 1.0, 0.0).astype(BF16)
    grad_low = jnp.where(member, grad_all, 0.0).astype(BF16)
    moment_s[...] = jnp.dot(grad_low, x, preferred_element_type=F32)
    hsum_s[...] = lax.dot_general(
        member_low, weighted[...], (((1,), (1,)), ((), ())), preferred_element_type=F32
    )
    htot = jnp.sum(jnp.where(member, hess_all, 0.0), axis=1, keepdims=True)
    gtot = jnp.sum(jnp.where(member, grad_all, 0.0), axis=1, keepdims=True)
    lane_at = iota((LEAVES, LANE), 1)
    total_s[...] = jnp.where(lane_at == 0, htot, jnp.where(lane_at == 1, gtot, 0.0))


def pack_grams(x_ref, leaf_all, weighted, moment_s, hsum_s, total_s, out_ref, base):
    half = x_ref.shape[1] // 2
    mask = slot_mask(position())
    down = iota((half, half), 0)
    across = iota((half, half), 1)

    def one_slot(slot, carry):
        leaf = (slot + base) ^ mask
        chosen = jnp.where(leaf_all == leaf.astype(F32), 1.0, 0.0).astype(BF16)
        gram = jnp.dot(weighted[...] * chosen, x_ref[...], preferred_element_type=F32)
        out_ref[slot, 0:half, :] = gram[half:, :half]
        out_ref[slot, half : 2 * half, :] = jnp.where(
            down >= across, gram[:half, :half], gram[half:, half:]
        )
        diagonal = jnp.sum(
            jnp.where(down == across, gram[half:, half:], 0.0), axis=0, keepdims=True
        )
        hs = hsum_s[pl.ds(leaf, 1), :]
        mo = moment_s[pl.ds(leaf, 1), :]
        to = total_s[pl.ds(leaf, 1), :]
        out_ref[slot, 2 * half :, :] = jnp.concatenate(
            [diagonal, hs[:, :half], hs[:, half:], mo[:, :half], mo[:, half:], to]
            + [jnp.zeros((EXTRA - 6, LANE), F32)],
            axis=0,
        )
        return carry

    lax.fori_loop(0, out_ref.shape[0], one_slot, 0, unroll=UNROLL)


def interior_kernel(table, grad_ref, hess_ref, rows, cols, packed_cols):
    blocks = grad_ref.shape[0]
    pair_tables(table[0], table[1], table[2], table[3], rows, cols, packed_cols)
    nothing = jnp.zeros((1, LANE), F32)
    for ref in (grad_ref, hess_ref):
        ref[0:1, :] = nothing
        ref[blocks - 1 : blocks, :] = nothing

    def one_block(b, carry):
        grad, hess = pair_block(b, b - 1, rows, cols, packed_cols)
        grad_ref[pl.ds(b, 1), :] = grad
        hess_ref[pl.ds(b, 1), :] = hess
        return carry

    lax.fori_loop(1, blocks - 1, one_block, 0)


def boundary_kernel(
    table, x_ref, inner, outer, grad_part, hess_part,
    grad_ref, send_ref, weighted, moment_s, hsum_s, total_s, x_out,
    rows, cols, packed_cols,
):
    blocks = grad_ref.shape[0]
    final = blocks - 1
    me = position()
    devices = lax.axis_size("doc") * lax.axis_size("leaf")

    odd = (me & 1) == 1

    def window(slot):
        near = inner[slot : slot + 1, :]
        far = outer[slot : slot + 1, :]
        return jnp.concatenate(
            [
                jnp.where(odd, near, far),
                table[slot, 0:2, :],
                table[slot, final - 1 :, :],
                jnp.where(odd, far, near),
            ],
            axis=0,
        )

    ids = window(0)
    at = iota(ids.shape, 0)
    outside = ((at == 0) & (me == 0)) | ((at == 5) & (me == devices - 1))
    pair_tables(
        jnp.where(outside, -1.0, ids), window(1), window(2), window(3), rows, cols, packed_cols
    )
    head_grad, head_hess = pair_block(1, 0, rows, cols, packed_cols)
    tail_grad, tail_hess = pair_block(4, 3, rows, cols, packed_cols)
    grads = jnp.concatenate([head_grad, grad_part[1:final, :], tail_grad], axis=0)
    hesses = jnp.concatenate([head_hess, hess_part[1:final, :], tail_hess], axis=0)
    grad_ref[...] = grads
    x_out[...] = x_ref[...]
    leaf_all = lanes_of(table[4])
    leaf_sums(
        x_ref[...], x_ref[...].astype(F32).T, lanes_of(hesses), lanes_of(grads), leaf_all,
        weighted, moment_s, hsum_s, total_s,
    )
    pack_grams(x_ref, leaf_all, weighted, moment_s, hsum_s, total_s, send_ref, LEAVES // 2)


def keep_kernel(table, x_ref, weighted, moment_s, hsum_s, total_s, keep_ref):
    pack_grams(
        x_ref, lanes_of(table[4]), weighted, moment_s, hsum_s, total_s, keep_ref, 0
    )


def table_scratch(count):
    return [
        pltpu.VMEM((4, 8 * pl.cdiv(count, 8), LANE), F32),
        pltpu.VMEM((4, count * LANE, LANE), F32),
        pltpu.VMEM((count * LANE, LANE), jnp.int32),
    ]


def on_chip(kernel, outs, scratch, args, cost=None):
    vmem = pl.BlockSpec(memory_space=pltpu.VMEM)
    return pl.pallas_call(
        kernel,
        out_shape=tuple(jax.ShapeDtypeStruct(shape, kind) for shape, kind in outs),
        in_specs=[vmem] * len(args),
        out_specs=(vmem,) * len(outs),
        scratch_shapes=scratch,
        compiler_params=pltpu.CompilerParams(vmem_limit_bytes=VMEM_LIMIT),
        cost_estimate=cost,
    )(*args)


def interior(table):
    _, blocks, _ = table.shape
    cost = pl.CostEstimate(
        flops=20000 * blocks * LANE * LANE, bytes_accessed=blocks * LANE * LANE, transcendentals=0
    )
    row = ((blocks, LANE), F32)
    return on_chip(interior_kernel, (row, row), table_scratch(blocks), (table,), cost)


def boundary(table, x, inner, outer, grad, hess):
    n_rows, feats = x.shape
    outs = (
        (grad.shape, F32),
        ((LEAVES // 2, feats + EXTRA, LANE), F32),
        ((feats, n_rows), BF16),
        ((LEAVES, feats), F32),
        ((LEAVES, feats), F32),
        ((LEAVES, LANE), F32),
        (x.shape, x.dtype),
    )
    return on_chip(
        boundary_kernel, outs, table_scratch(6), (table, x, inner, outer, grad, hess)
    )


def keep_part(table, x, weighted, moment, hsum, totals):
    n_rows, feats = x.shape
    cost = pl.CostEstimate(
        flops=LEAVES * n_rows * feats * feats, bytes_accessed=4 * n_rows * feats, transcendentals=0
    )
    outs = (((LEAVES // 2, feats + EXTRA, LANE), F32),)
    return on_chip(keep_kernel, outs, [], (table, x, weighted, moment, hsum, totals), cost)[0]


def fold_kernel(keep_ref, other_ref, *outs):
    for n, out in enumerate(outs):
        out[...] = keep_ref[n] + other_ref[n]


def fold(keep, other):
    return on_chip(fold_kernel, ((keep.shape[1:], F32),) * keep.shape[0], [], (keep, other))


def tree_sum(values):
    while len(values) > 1:
        values = [a + b for a, b in zip(values[::2], values[1::2])]
    return values[0]


def total_kernel(*refs):
    refs[-1][...] = tree_sum([ref[...] for ref in refs[:-1]])


def total(parts):
    return on_chip(total_kernel, ((parts[0].shape, F32),), [], parts)[0]


def eliminate(tiles, at, offset):
    size = tiles[at].shape[0]
    down = iota((size, LANE), 0)
    scale = jnp.ones((size, LANE), F32)
    for base in range(0, size, GROUP):
        first = offset + base
        columns = [
            jnp.broadcast_to(tiles[at][:, first + j : first + j + 1], (size, LANE))
            for j in range(GROUP)
        ]
        for j in range(GROUP):
            p = base + j
            inverse = 1.0 / columns[j][p : p + 1, :]
            scale = jnp.where(down == p, inverse, scale)
            factor = jnp.where(down == p, 0.0, columns[j]) * inverse
            for k in range(j + 1, GROUP):
                columns[k] = columns[k] - factor * columns[k][p : p + 1, :]
            tiles = [t if t is None else t - factor * t[p : p + 1, :] for t in tiles]
    return [t if t is None else t * scale for t in tiles]


def exact_dot(a, b):
    return jnp.dot(a, b, precision=lax.Precision.HIGHEST, preferred_element_type=F32)


def solve_kernel(*refs):
    ins, out_ref = refs[:-1], refs[-1]
    summed = tree_sum([ref[...] for ref in ins])
    feats = summed.shape[0] - EXTRA
    half = feats // 2
    corner = summed[:half]
    mixed = summed[half:feats]
    extra = [summed[feats + n : feats + n + 1] for n in range(6)]
    turned = mixed.T
    down = iota((half, half), 0)
    across = iota((half, half), 1)
    diag_row, hs0, hs1, mo0, mo1, totals = extra
    upper_left = jnp.where(down >= across, mixed, turned)
    lower_right = jnp.where(down < across, mixed, jnp.where(down > across, turned, diag_row))
    htot = totals[:, 0:1]
    gtot = totals[:, 1:2]
    inv_den = 1.0 / (htot + LAMBDA)
    rhs0 = hs0 * (gtot * inv_den) - mo0
    rhs1 = hs1 * (gtot * inv_den) - mo1
    columns = jnp.concatenate(
        [hs0, hs1, rhs0, rhs1, jnp.zeros((4, LANE), F32)], axis=0
    ).T
    hc0 = columns[:, 0:1] * inv_den
    hc1 = columns[:, 1:2] * inv_den
    eye = jnp.where(down == across, LAMBDA, 0.0)
    top = [
        upper_left + eye - hc0 * hs0,
        corner.T - hc0 * hs1,
        jnp.where(across == 0, columns[:, 2:3], 0.0),
    ]
    low = [
        corner - hc1 * hs0,
        lower_right + eye - hc1 * hs1,
        jnp.where(across == 0, columns[:, 3:4], 0.0),
    ]
    per_tile = LANE // STRIP
    count = feats // STRIP
    strips = []
    for s in range(count):
        source = top if s < per_tile else low
        start = (s % per_tile) * STRIP
        strips.append([t[start : start + STRIP] for t in source])
    for s in range(count):
        tile, offset = s // per_tile, (s % per_tile) * STRIP
        done = eliminate([None] * tile + strips[s][tile:], tile, offset)
        strips[s] = done
        solved = jnp.concatenate(done[tile:], axis=1)
        later = [s + 1] if s + 1 < count else []
        others = [i for i in range(count) if i not in (s, s + 1)]
        for group in (later, others):
            if not group:
                continue
            left = jnp.concatenate(
                [strips[i][tile][:, offset : offset + STRIP] for i in group], axis=0
            )
            change = exact_dot(left, solved)
            for q, i in enumerate(group):
                part = change[q * STRIP : (q + 1) * STRIP]
                strips[i] = [
                    t if n < tile else t - part[:, (n - tile) * LANE : (n - tile + 1) * LANE]
                    for n, t in enumerate(strips[i])
                ]
    right = [strips[s][2] for s in range(count)]
    w0 = jnp.concatenate(right[:per_tile], axis=0).T[0:1, :]
    w1 = jnp.concatenate(right[per_tile:], axis=0).T[0:1, :]
    dotted = jnp.sum(hs0 * w0 + hs1 * w1, axis=1, keepdims=True)
    intercept = -(gtot + dotted) * inv_den
    out_ref[...] = jnp.concatenate(
        [w0, w1, jnp.broadcast_to(intercept, (1, LANE)), jnp.zeros((1, LANE), F32)], axis=0
    )


def solve_leaf(parts):
    return on_chip(solve_kernel, (((4, LANE), F32),), [], parts)[0]


def output_kernel(table, x_ref, c0, c1, c2, c3, tree_ref, new_ref):
    groups = (c0, c1, c2, c3)
    slots = [groups[n >> 1 & 3][(n >> 3) * 2 + (n & 1)] for n in range(LEAVES)]
    low = jnp.concatenate([c[0:1, :] for c in slots], axis=0)
    high = jnp.concatenate([c[1:2, :] for c in slots], axis=0)
    shift = jnp.concatenate([c[2:3, :] for c in slots], axis=0)[:, 0:1]
    coefs = jnp.concatenate([low, high], axis=1)
    top = coefs.astype(BF16)
    left = coefs - top.astype(F32)
    middle = left.astype(BF16)
    bottom = (left - middle.astype(F32)).astype(BF16)
    stacked = jnp.concatenate([top, middle, bottom], axis=0)
    parts = lax.dot_general(
        stacked, x_ref[...], (((1,), (1,)), ((), ())), preferred_element_type=F32
    )
    per_leaf = (
        parts[:LEAVES] + (parts[LEAVES : 2 * LEAVES] + parts[2 * LEAVES :])
    ) + shift
    leaf_all = lanes_of(table[4])
    leaf_at = (iota(per_leaf.shape, 0) ^ slot_mask(position())).astype(F32)
    chosen = jnp.sum(jnp.where(leaf_all == leaf_at, per_leaf, 0.0), axis=0, keepdims=True)
    for b in range(tree_ref.shape[0]):
        piece = chosen[:, b * LANE : (b + 1) * LANE]
        tree_ref[b : b + 1, :] = piece
        new_ref[b : b + 1, :] = table[3, b : b + 1, :] + SHRINKAGE * piece


def row_outputs(table, x, coefs):
    row = (table.shape[1:], F32)
    return on_chip(output_kernel, (row, row), [], (table, x, *coefs))


def body(features, scores, labels, query_ids, ranks, leaf_ids):
    devices = lax.axis_size("doc") * lax.axis_size("leaf")
    n_rows = features.shape[0]
    score, label, query, rank, leaf = [
        v.reshape(n_rows // LANE, LANE) for v in (scores, labels, query_ids, ranks, leaf_ids)
    ]

    def swapped(value, flip):
        return lax.ppermute(value, AXES, [(i, i ^ flip) for i in range(devices)])

    x = features
    inner, outer, table = edges(query, label, rank, score, leaf)
    inner = swapped(inner, 1)
    outer = lax.ppermute(
        outer, AXES, [p for i in range(1, devices - 1, 2) for p in ((i, i + 1), (i + 1, i))]
    )
    grad, hess = interior(table)
    grad, send, *sums, held = boundary(table, x, inner, outer, grad, hess)
    other = swapped(send, 1)
    chunks = fold(keep_part(table, held, *sums), other)
    mine = total([swapped(c, flip) if flip else c for c, flip in zip(chunks, NEAR)])
    parts = [mine, swapped(mine, 16)]
    bit = 32
    while bit < devices:
        mine = parts[0] + parts[1]
        parts = [mine, swapped(mine, bit)]
        bit *= 2
    coefs = solve_leaf(parts)
    group = jnp.stack([swapped(coefs, flip) if flip else coefs for flip in GATHER[0]])
    coefs = [swapped(group, flip) if flip else group for flip in GATHER[1]]
    tree, fresh = row_outputs(table, x, coefs)
    return grad.reshape(-1), tree.reshape(-1), fresh.reshape(-1)


def solution(mesh):
    rows = P(AXES)
    return jax.shard_map(
        body,
        mesh=mesh,
        in_specs=(P(AXES, None), rows, rows, rows, rows, rows),
        out_specs=(rows, rows, rows),
        check_vma=False,
    )
```

time: 82.7 us -> 63.5 us (0.77)
  blocking collectives: 42.5 us -> 0 us
  starting transfers between devices: 6.07 us -> 26.1 us
  waiting for transfers between devices: 7.39 us -> 18 us
  local copies, waits for them, and re-layouts: 5.25 us -> 0.73 us
  other arithmetic: 1.84 us -> 0.01 us
    all_to_all x3 -> x0, blocking collectives: 42.5 us -> none  [the longest x2 32.8 us: reduce_groups(): lax.all_to_all(parts, AXES, 0, 0, axis_index_groups=groups, tiled=True)]
    ppermute x4 -> x17, starting transfers between devices: 6.07 us -> 26.1 us  [the longest x16 25.5 us: swapped(): return lax.ppermute(value, AXES, [(i, i ^ flip) for i in range(devices)])]
    ppermute x4 -> x17, waiting for transfers between devices: 7.39 us -> 18 us  [the longest x16 18 us: swapped(): return lax.ppermute(value, AXES, [(i, i ^ flip) for i in range(devices)])]
    unnamed x18 -> x6, local copies, waits for them, and re-layouts: 4.48 us -> 0.73 us
    convert_element_type x2 -> x0, other arithmetic: 1.53 us -> none  [the longest x1 0.77 us: edge(): rank[block].astype(F32)]
    pallas_call x3 -> x8, Pallas kernels: 18.3 us -> 17.7 us  [the longest x7 16.3 us: on_chip(): pl.pallas_call(kernel, out_shape=tuple((jax.ShapeDtypeStruct(shape, kind)...]
  transfers between devices with their start and end apart: 4 -> 17, of which waited for: 3 -> 10; matrix products, arithmetic and copies ran while one was open for 0% -> 0% of each run, Pallas kernels for 0% -> 6%
where the time goes in v3:
time: 63.5 us; the launch traced here: 63.3 us
  starting transfers between devices  26.1 us (41%)
  waiting for transfers between devices  18 us (28%)
  Pallas kernels  17.7 us (28%)
  local copies, waits for them, and re-layouts  0.73 us (1%)
  between operations  0.72 us (1%)
    ppermute x16, starting transfers between devices, swapped(): return lax.ppermute(value, AXES, [(i, i ^ flip) for i in range(devices)])  25.5 us
    ppermute x16, waiting for transfers between devices, swapped(): return lax.ppermute(value, AXES, [(i, i ^ flip) for i in range(devices)])  18 us
    pallas_call x7, Pallas kernels, on_chip(): pl.pallas_call(kernel, out_shape=tuple((jax.ShapeDtypeStruct(shape, kind)...  16.3 us
    pallas_call x1, Pallas kernels, edges(): pl.pallas_call(edge_kernel, out_shape=(edge, edge, jax.ShapeDtypeStruct((...  1.41 us
  transfers between devices with their start and end apart: 17, of which 10 were waited for; matrix products, arithmetic and copies ran while one was open for 0% of the time, Pallas kernels for 6%

profile of v3, /device:TPU:0, one launch (start us, length us, event | category | flops | bytes accessed | tf_op | source)
XLA Modules:
  0.0 63.3 jit_solution(10913210370142060783)
XLA Ops:
  0.6 1.4 %shard_map.85 = (f32[4,128]{1,0:T(4,128)}, f32[4,128]{1,0:T(4,128)}, f32[5,8,128]{2,1,0:T(8,128)}) custom-call(s32[8,128]{1,0:T(8,128)} %bitcast.13, s32[8,128]{1,0:T(8,128)} %bitcast.14, s32[8,128]{1,0:T(8,128)} %bitcast.15, f32[8,128]{1,0:T(8,128)} %bitcast.16, s32[8,128]{1,0:T(8,128)} %bitcast.17), custom_call_target="tpu_custom_call" | custom-call | tf_op jit(solution)/shard_map/pallas_call | solution.py:82
  2.0 0.5 collective-permute-start
  2.6 0.6 %collective-permute-start.1 = (f32[4,128]{1,0:T(4,128)}, f32[4,128]{1,0:T(4,128)S(1)}, u32[]{:S(2)}, u32[]{:S(2)}) collective-permute-start(f32[4,128]{1,0:T(4,128)} %get-tuple-element.27), channel_id=1, source_target_pairs={{1,2},{2,1},{3,4},{4,3},{5,6},{6,5},{7,8},{8,7},{9,10},{10,9},{11,... | collective-permute-start | bytes 6152 | tf_op jit(solution)/shard_map/ppermute | solution.py:488
  3.2 0.7 %copy-done.1 = f32[5,8,128]{2,1,0:T(8,128)S(1)} copy-done((f32[5,8,128]{2,1,0:T(8,128)S(1)}, f32[5,8,128]{2,1,0:T(8,128)}, u32[]{:S(2)}) %copy-start.1) | copy-done | bytes 20504
  4.0 2.1 %shard_map.86 = (f32[8,128]{1,0:T(8,128)S(1)}, f32[8,128]{1,0:T(8,128)S(1)}) custom-call(f32[5,8,128]{2,1,0:T(8,128)S(1)} %copy-done.1), custom_call_target="tpu_custom_call" | custom-call | flops 2621440000 | bytes 131072 | tf_op jit(solution)/shard_map/pallas_call | solution.py:274
  6.1 3.3 %shard_map.87 = (f32[8,128]{1,0:T(8,128)}, f32[8,264,128]{2,1,0:T(8,128)S(1)}, bf16[256,1024]{1,0:T(8,128)(2,1)S(1)}, f32[16,256]{1,0:T(8,128)S(1)}, f32[16,256]...) custom-call(f32[5,8,128]{2,1,0:T(8,128)S(1)} %copy-done.1, bf16[1024,256]{1,0:T(8,128)(2,1)S(1)} %copy-done, ...), custom_call_target="tpu_custom_call" | custom-call | tf_op jit(solution)/shard_map/pallas_call | solution.py:274
  9.4 3.9 %collective-permute-start.2 = (f32[8,264,128]{2,1,0:T(8,128)S(1)}, f32[8,264,128]{2,1,0:T(8,128)S(1)}, u32[]{:S(2)}, u32[]{:S(2)}) collective-permute-start(f32[8,264,128]{2,1,0:T(8,128)S(1)} %get-tuple-element.36), channel_id=1, source_target_pairs={{0,1},{1,0},{2,3},{3,2},{4,5},{5,4},{6,7},{7,6},{8,9},{9,8},{10,11... | collective-permute-start | bytes 3244040 | tf_op jit(solution)/shard_map/ppermute | solution.py:483
  13.3 1.8 %shard_map.88.keep_ref = f32[8,264,128]{2,1,0:T(8,128)S(1)} custom-call(f32[5,8,128]{2,1,0:T(8,128)S(1)} %copy-done.1, bf16[1024,256]{1,0:T(8,128)(2,1)S(1)} %get-tuple-element.31.x_ref, bf16[256,1024]{1,0:T(8,128)(2,1)S(1)} %get-tuple-element.32.weighted, f32[16,256]{1,0:T(8,128)S(1)} %get-tuple-element.33.moment_s, ...), custom_call_target="tpu_custom_call" | custom-call | flops 1073741824 | bytes 1048576 | tf_op jit(solution)/shard_map/pallas_call | solution.py:274
  15.1 0.5 collective-permute-done.2.other_ref
  15.7 0.1 shard_map.89
  15.8 1.6 %collective-permute-start.3 = (f32[264,128]{1,0:T(8,128)S(1)}, f32[264,128]{1,0:T(8,128)S(1)}, u32[]{:S(2)}, u32[]{:S(2)}) collective-permute-start(f32[264,128]{1,0:T(8,128)S(1)} %get-tuple-element.38), channel_id=1, source_target_pairs={{0,2},{1,3},{2,0},{3,1},{4,6},{5,7},{6,4},{7,5},{8,10},{9,11},{10,... | collective-permute-start | bytes 405512 | tf_op jit(solution)/shard_map/ppermute | solution.py:483
  17.4 2.4 %collective-permute-start.4 = (f32[264,128]{1,0:T(8,128)S(1)}, f32[264,128]{1,0:T(8,128)S(1)}, u32[]{:S(2)}, u32[]{:S(2)}) collective-permute-start(f32[264,128]{1,0:T(8,128)S(1)} %get-tuple-element.39), channel_id=1, source_target_pairs={{0,4},{1,5},{2,6},{3,7},{4,0},{5,1},{6,2},{7,3},{8,12},{9,13},{10,... | collective-permute-start | bytes 405512 | tf_op jit(solution)/shard_map/ppermute | solution.py:483
  19.8 2.3 %collective-permute-start.6 = (f32[264,128]{1,0:T(8,128)S(1)}, f32[264,128]{1,0:T(8,128)S(1)}, u32[]{:S(2)}, u32[]{:S(2)}) collective-permute-start(f32[264,128]{1,0:T(8,128)S(1)} %get-tuple-element.41), channel_id=1, source_target_pairs={{0,8},{1,9},{2,10},{3,11},{4,12},{5,13},{6,14},{7,15},{8,0},{9,1},... | collective-permute-start | bytes 405512 | tf_op jit(solution)/shard_map/ppermute | solution.py:483
  22.1 0.7 %collective-permute-start.7 = (f32[264,128]{1,0:T(8,128)S(1)}, f32[264,128]{1,0:T(8,128)S(1)}, u32[]{:S(2)}, u32[]{:S(2)}) collective-permute-start(f32[264,128]{1,0:T(8,128)S(1)} %get-tuple-element.42), channel_id=1, source_target_pairs={{0,10},{1,11},{2,8},{3,9},{4,14},{5,15},{6,12},{7,13},{8,2},{9,3},... | collective-permute-start | bytes 405512 | tf_op jit(solution)/shard_map/ppermute | solution.py:483
  22.8 3.0 %collective-permute-start.8 = (f32[264,128]{1,0:T(8,128)S(1)}, f32[264,128]{1,0:T(8,128)S(1)}, u32[]{:S(2)}, u32[]{:S(2)}) collective-permute-start(f32[264,128]{1,0:T(8,128)S(1)} %get-tuple-element.43), channel_id=1, source_target_pairs={{0,12},{1,13},{2,14},{3,15},{4,8},{5,9},{6,10},{7,11},{8,4},{9,5},... | collective-permute-start | bytes 405512 | tf_op jit(solution)/shard_map/ppermute | solution.py:483
  25.8 0.4 collective-permute-done.4.refs_2_
  26.2 2.7 %collective-permute-start.9 = (f32[264,128]{1,0:T(8,128)S(1)}, f32[264,128]{1,0:T(8,128)S(1)}, u32[]{:S(2)}, u32[]{:S(2)}) collective-permute-start(f32[264,128]{1,0:T(8,128)S(1)} %get-tuple-element.44), channel_id=1, source_target_pairs={{0,14},{1,15},{2,12},{3,13},{4,10},{5,11},{6,8},{7,9},{8,6},{9,7},... | collective-permute-start | bytes 405512 | tf_op jit(solution)/shard_map/ppermute | solution.py:483
  28.9 1.2 %collective-permute-done.7.refs_5_ = f32[264,128]{1,0:T(8,128)S(1)} collective-permute-done((f32[264,128]{1,0:T(8,128)S(1)}, f32[264,128]{1,0:T(8,128)S(1)}, u32[]{:S(2)}, u32[]{:S(2)}) %collective-permute-start.7) | collective-permute-done | bytes 135200 | tf_op jit(solution)/shard_map/ppermute | solution.py:483
  30.1 3.1 %collective-permute-done.8.refs_6_ = f32[264,128]{1,0:T(8,128)S(1)} collective-permute-done((f32[264,128]{1,0:T(8,128)S(1)}, f32[264,128]{1,0:T(8,128)S(1)}, u32[]{:S(2)}, u32[]{:S(2)}) %collective-permute-start.8) | collective-permute-done | bytes 135200 | tf_op jit(solution)/shard_map/ppermute | solution.py:483
  33.3 2.6 %collective-permute-done.9.refs_7_ = f32[264,128]{1,0:T(8,128)S(1)} collective-permute-done((f32[264,128]{1,0:T(8,128)S(1)}, f32[264,128]{1,0:T(8,128)S(1)}, u32[]{:S(2)}, u32[]{:S(2)}) %collective-permute-start.9) | collective-permute-done | bytes 135200 | tf_op jit(solution)/shard_map/ppermute | solution.py:483
  36.0 2.6 %collective-permute-start.10 = (f32[264,128]{1,0:T(8,128)S(1)}, f32[264,128]{1,0:T(8,128)S(1)}, u32[]{:S(2)}, u32[]{:S(2)}) collective-permute-start(f32[264,128]{1,0:T(8,128)S(1)} %shard_map.90.refs_0_), channel_id=1, source_target_pairs={{0,16},{1,17},{2,18},{3,19},{4,20},{5,21},{6,22},{7,23},{8,24},{9,... | collective-permute-start | bytes 405512 | tf_op jit(solution)/shard_map/ppermute | solution.py:483
  38.6 5.0 %collective-permute-done.10.refs_1_ = f32[264,128]{1,0:T(8,128)S(1)} collective-permute-done((f32[264,128]{1,0:T(8,128)S(1)}, f32[264,128]{1,0:T(8,128)S(1)}, u32[]{:S(2)}, u32[]{:S(2)}) %collective-permute-start.10) | collective-permute-done | bytes 135200 | tf_op jit(solution)/shard_map/ppermute | solution.py:483
  43.6 8.0 %shard_map.91 = f32[4,128]{1,0:T(4,128)S(1)} custom-call(f32[264,128]{1,0:T(8,128)S(1)} %shard_map.90.refs_0_, f32[264,128]{1,0:T(8,128)S(1)} %collective-permute-done.10.refs_1_), custom_call_target="tpu_custom_call" | custom-call | tf_op jit(solution)/shard_map/pallas_call | solution.py:274
  51.6 1.1 %collective-permute-start.12 = (f32[4,128]{1,0:T(4,128)S(1)}, f32[4,128]{1,0:T(4,128)S(1)}, u32[]{:S(2)}, u32[]{:S(2)}) collective-permute-start(f32[4,128]{1,0:T(4,128)S(1)} %shard_map.91), channel_id=1, source_target_pairs={{0,1},{1,0},{2,3},{3,2},{4,5},{5,4},{6,7},{7,6},{8,9},{9,8},{10,11... | collective-permute-start | bytes 6152 | tf_op jit(solution)/shard_map/ppermute | solution.py:483
  52.7 1.1 %collective-permute-start.11 = (f32[4,128]{1,0:T(4,128)S(1)}, f32[4,128]{1,0:T(4,128)S(1)}, u32[]{:S(2)}, u32[]{:S(2)}) collective-permute-start(f32[4,128]{1,0:T(4,128)S(1)} %shard_map.91), channel_id=1, source_target_pairs={{0,2},{1,3},{2,0},{3,1},{4,6},{5,7},{6,4},{7,5},{8,10},{9,11},{10,... | collective-permute-start | bytes 6152 | tf_op jit(solution)/shard_map/ppermute | solution.py:483
  53.8 0.9 %collective-permute-done.13 = f32[4,128]{1,0:T(4,128)S(1)} collective-permute-done((f32[4,128]{1,0:T(4,128)S(1)}, f32[4,128]{1,0:T(4,128)S(1)}, u32[]{:S(2)}, u32[]{:S(2)}) %collective-permute-start.13) | collective-permute-done | bytes 2080 | tf_op jit(solution)/shard_map/ppermute | solution.py:483
  54.7 1.6 %collective-permute-done.11 = f32[4,128]{1,0:T(4,128)S(1)} collective-permute-done((f32[4,128]{1,0:T(4,128)S(1)}, f32[4,128]{1,0:T(4,128)S(1)}, u32[]{:S(2)}, u32[]{:S(2)}) %collective-permute-start.11) | collective-permute-done | bytes 2080 | tf_op jit(solution)/shard_map/ppermute | solution.py:483
  56.4 2.4 %collective-permute-start.15 = (f32[4,4,128]{2,1,0:T(4,128)S(1)}, f32[4,4,128]{2,1,0:T(4,128)S(1)}, u32[]{:S(2)}, u32[]{:S(2)}) collective-permute-start(f32[4,4,128]{2,1,0:T(4,128)S(1)} %pad_maximum_fusion.c0), channel_id=1, source_target_pairs={{0,8},{1,9},{2,10},{3,11},{4,12},{5,13},{6,14},{7,15},{8,0},{9,1},... | collective-permute-start | bytes 24584 | tf_op jit(solution)/shard_map/ppermute | solution.py:483
  58.7 1.0 %collective-permute-start.14 = (f32[4,4,128]{2,1,0:T(4,128)S(1)}, f32[4,4,128]{2,1,0:T(4,128)S(1)}, u32[]{:S(2)}, u32[]{:S(2)}) collective-permute-start(f32[4,4,128]{2,1,0:T(4,128)S(1)} %pad_maximum_fusion.c0), channel_id=1, source_target_pairs={{0,4},{1,5},{2,6},{3,7},{4,0},{5,1},{6,2},{7,3},{8,12},{9,13},{10,... | collective-permute-start | bytes 24584 | tf_op jit(solution)/shard_map/ppermute | solution.py:483
  59.8 1.1 %collective-permute-done.16.c3 = f32[4,4,128]{2,1,0:T(4,128)S(1)} collective-permute-done((f32[4,4,128]{2,1,0:T(4,128)S(1)}, f32[4,4,128]{2,1,0:T(4,128)S(1)}, u32[]{:S(2)}, u32[]{:S(2)}) %collective-permute-start.16) | collective-permute-done | bytes 8224 | tf_op jit(solution)/shard_map/ppermute | solution.py:483
  60.8 1.6 %collective-permute-done.14.c1 = f32[4,4,128]{2,1,0:T(4,128)S(1)} collective-permute-done((f32[4,4,128]{2,1,0:T(4,128)S(1)}, f32[4,4,128]{2,1,0:T(4,128)S(1)}, u32[]{:S(2)}, u32[]{:S(2)}) %collective-permute-start.14) | collective-permute-done | bytes 8224 | tf_op jit(solution)/shard_map/ppermute | solution.py:483
  62.4 0.9 %shard_map.92 = (f32[8,128]{1,0:T(8,128)}, f32[8,128]{1,0:T(8,128)}) custom-call(f32[5,8,128]{2,1,0:T(8,128)S(1)} %copy-done.2, bf16[1024,256]{1,0:T(8,128)(2,1)S(1)} %copy-done, f32[4,4,128]{2,1,0:T(4,128)S(1)} %pad_maximum_fusion.c0, f32[4,4,128]{2,1,0:T(4,128)S(1)} %collective-permute-done.14.c1, f32[4,4,128]{2,1,0:T(4,128)S(1)} %collective-permute-done.15.c2, ...), custom_call_target="tpu_custom_call" | custom-call | tf_op jit(solution)/shard_map/pallas_call | solution.py:274
  (17 shorter events, 0.2 us)
Async XLA Ops:
  2.0 4.0 %collective-permute-start = (f32[4,128]{1,0:T(4,128)}, f32[4,128]{1,0:T(4,128)S(1)}, u32[]{:S(2)}, u32[]{:S(2)}) collective-permute-start(f32[4,128]{1,0:T(4,128)} %get-tuple-element.26), channel_id=1, source_target_pairs={{0,1},{1,0},{2,3},{3,2},{4,5},{5,4},{6,7},{7,6},{8,9},{9,8},{10,11... | collective-permute-start | bytes 6152 | tf_op jit(solution)/shard_map/ppermute | solution.py:483
  2.6 3.5 %collective-permute-start.1 = (f32[4,128]{1,0:T(4,128)}, f32[4,128]{1,0:T(4,128)S(1)}, u32[]{:S(2)}, u32[]{:S(2)}) collective-permute-start(f32[4,128]{1,0:T(4,128)} %get-tuple-element.27), channel_id=1, source_target_pairs={{1,2},{2,1},{3,4},{4,3},{5,6},{6,5},{7,8},{8,7},{9,10},{10,9},{11,... | collective-permute-start | bytes 6152 | tf_op jit(solution)/shard_map/ppermute | solution.py:488
  3.2 0.7 %copy-start.1 = (f32[5,8,128]{2,1,0:T(8,128)S(1)}, f32[5,8,128]{2,1,0:T(8,128)}, u32[]{:S(2)}) copy-start(f32[5,8,128]{2,1,0:T(8,128)} %get-tuple-element.25.table) | copy-start | bytes 61444
  4.0 2.2 %copy-start = (bf16[1024,256]{1,0:T(8,128)(2,1)S(1)}, bf16[1024,256]{1,0:T(8,128)(2,1)}, u32[]{:S(2)}) copy-start(bf16[1024,256]{1,0:T(8,128)(2,1)} %x_ref.3) | copy-start | bytes 1572868
  9.4 6.2 %collective-permute-start.2 = (f32[8,264,128]{2,1,0:T(8,128)S(1)}, f32[8,264,128]{2,1,0:T(8,128)S(1)}, u32[]{:S(2)}, u32[]{:S(2)}) collective-permute-start(f32[8,264,128]{2,1,0:T(8,128)S(1)} %get-tuple-element.36), channel_id=1, source_target_pairs={{0,1},{1,0},{2,3},{3,2},{4,5},{5,4},{6,7},{7,6},{8,9},{9,8},{10,11... | collective-permute-start | bytes 3244040 | tf_op jit(solution)/shard_map/ppermute | solution.py:483
  15.8 46.6 %copy-start.2 = (f32[5,8,128]{2,1,0:T(8,128)S(1)}, f32[5,8,128]{2,1,0:T(8,128)}, u32[]{:S(2)}) copy-start(f32[5,8,128]{2,1,0:T(8,128)} %get-tuple-element.25.table) | copy-start | bytes 61444
  15.8 7.0 %collective-permute-start.3 = (f32[264,128]{1,0:T(8,128)S(1)}, f32[264,128]{1,0:T(8,128)S(1)}, u32[]{:S(2)}, u32[]{:S(2)}) collective-permute-start(f32[264,128]{1,0:T(8,128)S(1)} %get-tuple-element.38), channel_id=1, source_target_pairs={{0,2},{1,3},{2,0},{3,1},{4,6},{5,7},{6,4},{7,5},{8,10},{9,11},{10,... | collective-permute-start | bytes 405512 | tf_op jit(solution)/shard_map/ppermute | solution.py:483
  17.4 8.8 %collective-permute-start.4 = (f32[264,128]{1,0:T(8,128)S(1)}, f32[264,128]{1,0:T(8,128)S(1)}, u32[]{:S(2)}, u32[]{:S(2)}) collective-permute-start(f32[264,128]{1,0:T(8,128)S(1)} %get-tuple-element.39), channel_id=1, source_target_pairs={{0,4},{1,5},{2,6},{3,7},{4,0},{5,1},{6,2},{7,3},{8,12},{9,13},{10,... | collective-permute-start | bytes 405512 | tf_op jit(solution)/shard_map/ppermute | solution.py:483
  19.8 9.1 %collective-permute-start.5 = (f32[264,128]{1,0:T(8,128)S(1)}, f32[264,128]{1,0:T(8,128)S(1)}, u32[]{:S(2)}, u32[]{:S(2)}) collective-permute-start(f32[264,128]{1,0:T(8,128)S(1)} %get-tuple-element.40), channel_id=1, source_target_pairs={{0,6},{1,7},{2,4},{3,5},{4,2},{5,3},{6,0},{7,1},{8,14},{9,15},{10,... | collective-permute-start | bytes 405512 | tf_op jit(solution)/shard_map/ppermute | solution.py:483
  19.8 9.1 %collective-permute-start.6 = (f32[264,128]{1,0:T(8,128)S(1)}, f32[264,128]{1,0:T(8,128)S(1)}, u32[]{:S(2)}, u32[]{:S(2)}) collective-permute-start(f32[264,128]{1,0:T(8,128)S(1)} %get-tuple-element.41), channel_id=1, source_target_pairs={{0,8},{1,9},{2,10},{3,11},{4,12},{5,13},{6,14},{7,15},{8,0},{9,1},... | collective-permute-start | bytes 405512 | tf_op jit(solution)/shard_map/ppermute | solution.py:483
  22.1 8.0 %collective-permute-start.7 = (f32[264,128]{1,0:T(8,128)S(1)}, f32[264,128]{1,0:T(8,128)S(1)}, u32[]{:S(2)}, u32[]{:S(2)}) collective-permute-start(f32[264,128]{1,0:T(8,128)S(1)} %get-tuple-element.42), channel_id=1, source_target_pairs={{0,10},{1,11},{2,8},{3,9},{4,14},{5,15},{6,12},{7,13},{8,2},{9,3},... | collective-permute-start | bytes 405512 | tf_op jit(solution)/shard_map/ppermute | solution.py:483
  22.8 10.5 %collective-permute-start.8 = (f32[264,128]{1,0:T(8,128)S(1)}, f32[264,128]{1,0:T(8,128)S(1)}, u32[]{:S(2)}, u32[]{:S(2)}) collective-permute-start(f32[264,128]{1,0:T(8,128)S(1)} %get-tuple-element.43), channel_id=1, source_target_pairs={{0,12},{1,13},{2,14},{3,15},{4,8},{5,9},{6,10},{7,11},{8,4},{9,5},... | collective-permute-start | bytes 405512 | tf_op jit(solution)/shard_map/ppermute | solution.py:483
  26.2 9.7 %collective-permute-start.9 = (f32[264,128]{1,0:T(8,128)S(1)}, f32[264,128]{1,0:T(8,128)S(1)}, u32[]{:S(2)}, u32[]{:S(2)}) collective-permute-start(f32[264,128]{1,0:T(8,128)S(1)} %get-tuple-element.44), channel_id=1, source_target_pairs={{0,14},{1,15},{2,12},{3,13},{4,10},{5,11},{6,8},{7,9},{8,6},{9,7},... | collective-permute-start | bytes 405512 | tf_op jit(solution)/shard_map/ppermute | solution.py:483
  36.0 7.7 %collective-permute-start.10 = (f32[264,128]{1,0:T(8,128)S(1)}, f32[264,128]{1,0:T(8,128)S(1)}, u32[]{:S(2)}, u32[]{:S(2)}) collective-permute-start(f32[264,128]{1,0:T(8,128)S(1)} %shard_map.90.refs_0_), channel_id=1, source_target_pairs={{0,16},{1,17},{2,18},{3,19},{4,20},{5,21},{6,22},{7,23},{8,24},{9,... | collective-permute-start | bytes 405512 | tf_op jit(solution)/shard_map/ppermute | solution.py:483
  51.6 3.0 %collective-permute-start.13 = (f32[4,128]{1,0:T(4,128)S(1)}, f32[4,128]{1,0:T(4,128)S(1)}, u32[]{:S(2)}, u32[]{:S(2)}) collective-permute-start(f32[4,128]{1,0:T(4,128)S(1)} %shard_map.91), channel_id=1, source_target_pairs={{0,3},{1,2},{2,1},{3,0},{4,7},{5,6},{6,5},{7,4},{8,11},{9,10},{10,... | collective-permute-start | bytes 6152 | tf_op jit(solution)/shard_map/ppermute | solution.py:483
  51.6 3.0 %collective-permute-start.12 = (f32[4,128]{1,0:T(4,128)S(1)}, f32[4,128]{1,0:T(4,128)S(1)}, u32[]{:S(2)}, u32[]{:S(2)}) collective-permute-start(f32[4,128]{1,0:T(4,128)S(1)} %shard_map.91), channel_id=1, source_target_pairs={{0,1},{1,0},{2,3},{3,2},{4,5},{5,4},{6,7},{7,6},{8,9},{9,8},{10,11... | collective-permute-start | bytes 6152 | tf_op jit(solution)/shard_map/ppermute | solution.py:483
  52.7 3.6 %collective-permute-start.11 = (f32[4,128]{1,0:T(4,128)S(1)}, f32[4,128]{1,0:T(4,128)S(1)}, u32[]{:S(2)}, u32[]{:S(2)}) collective-permute-start(f32[4,128]{1,0:T(4,128)S(1)} %shard_map.91), channel_id=1, source_target_pairs={{0,2},{1,3},{2,0},{3,1},{4,6},{5,7},{6,4},{7,5},{8,10},{9,11},{10,... | collective-permute-start | bytes 6152 | tf_op jit(solution)/shard_map/ppermute | solution.py:483
  56.3 4.5 %collective-permute-start.16 = (f32[4,4,128]{2,1,0:T(4,128)S(1)}, f32[4,4,128]{2,1,0:T(4,128)S(1)}, u32[]{:S(2)}, u32[]{:S(2)}) collective-permute-start(f32[4,4,128]{2,1,0:T(4,128)S(1)} %pad_maximum_fusion.c0), channel_id=1, source_target_pairs={{0,12},{1,13},{2,14},{3,15},{4,8},{5,9},{6,10},{7,11},{8,4},{9,5},... | collective-permute-start | bytes 24584 | tf_op jit(solution)/shard_map/ppermute | solution.py:483
  56.4 4.5 %collective-permute-start.15 = (f32[4,4,128]{2,1,0:T(4,128)S(1)}, f32[4,4,128]{2,1,0:T(4,128)S(1)}, u32[]{:S(2)}, u32[]{:S(2)}) collective-permute-start(f32[4,4,128]{2,1,0:T(4,128)S(1)} %pad_maximum_fusion.c0), channel_id=1, source_target_pairs={{0,8},{1,9},{2,10},{3,11},{4,12},{5,13},{6,14},{7,15},{8,0},{9,1},... | collective-permute-start | bytes 24584 | tf_op jit(solution)/shard_map/ppermute | solution.py:483
  58.7 3.7 %collective-permute-start.14 = (f32[4,4,128]{2,1,0:T(4,128)S(1)}, f32[4,4,128]{2,1,0:T(4,128)S(1)}, u32[]{:S(2)}, u32[]{:S(2)}) collective-permute-start(f32[4,4,128]{2,1,0:T(4,128)S(1)} %pad_maximum_fusion.c0), channel_id=1, source_target_pairs={{0,4},{1,5},{2,6},{3,7},{4,0},{5,1},{6,2},{7,3},{8,12},{9,13},{10,... | collective-permute-start | bytes 24584 | tf_op jit(solution)/shard_map/ppermute | solution.py:483

commit v4 on v3

--- a/solution.py
+++ b/solution.py
@@ -1,3 +1,5 @@
+import functools
+
 import jax
 import jax.numpy as jnp
 import numpy as np
@@ -15,9 +17,9 @@
 EXTRA = 8
 STRIP = 32
 GROUP = 16
-NEAR = tuple(range(0, 16, 2))
+NEAR = ((0, 4, 2, 1), (7, 6, 5, 3))
 GATHER = ((0, 2, 1, 3), (0, 4, 8, 12))
-UNROLL = 2
+PART = 4
 VMEM_LIMIT = 48 * 1024 * 1024
 F32 = jnp.float32
 BF16 = jnp.bfloat16
@@ -39,6 +41,10 @@
 
 def slot_mask(me):
     return (me & 1) * 8 + ((me >> 2) & 3) * 2 + ((me >> 1) & 1)
+
+
+def other_core(codes):
+    return tuple(code + LEAVES // 2 for code in codes)
 
 
 def fetch(sources, places, sems):
@@ -163,14 +169,14 @@
     total_s[...] = jnp.where(lane_at == 0, htot, jnp.where(lane_at == 1, gtot, 0.0))
 
 
-def pack_grams(x_ref, leaf_all, weighted, moment_s, hsum_s, total_s, out_ref, base):
+def pack_grams(x_ref, leaf_all, weighted, moment_s, hsum_s, total_s, out_ref, codes):
     half = x_ref.shape[1] // 2
     mask = slot_mask(position())
     down = iota((half, half), 0)
     across = iota((half, half), 1)
 
-    def one_slot(slot, carry):
-        leaf = (slot + base) ^ mask
+    for slot, code in enumerate(codes):
+        leaf = mask ^ code
         chosen = jnp.where(leaf_all == leaf.astype(F32), 1.0, 0.0).astype(BF16)
         gram = jnp.dot(weighted[...] * chosen, x_ref[...], preferred_element_type=F32)
         out_ref[slot, 0:half, :] = gram[half:, :half]
@@ -188,9 +194,6 @@
             + [jnp.zeros((EXTRA - 6, LANE), F32)],
             axis=0,
         )
-        return carry
-
-    lax.fori_loop(0, out_ref.shape[0], one_slot, 0, unroll=UNROLL)
 
 
 def interior_kernel(table, grad_ref, hess_ref, rows, cols, packed_cols):
@@ -252,12 +255,12 @@
         x_ref[...], x_ref[...].astype(F32).T, lanes_of(hesses), lanes_of(grads), leaf_all,
         weighted, moment_s, hsum_s, total_s,
     )
-    pack_grams(x_ref, leaf_all, weighted, moment_s, hsum_s, total_s, send_ref, LEAVES // 2)
-
-
-def keep_kernel(table, x_ref, weighted, moment_s, hsum_s, total_s, keep_ref):
+    pack_grams(x_ref, leaf_all, weighted, moment_s, hsum_s, total_s, send_ref, other_core(NEAR[0]))
+
+
+def gram_kernel(codes, table, x_ref, weighted, moment_s, hsum_s, total_s, out_ref):
     pack_grams(
-        x_ref, lanes_of(table[4]), weighted, moment_s, hsum_s, total_s, keep_ref, 0
+        x_ref, lanes_of(table[4]), weighted, moment_s, hsum_s, total_s, out_ref, codes
     )
 
 
@@ -295,7 +298,7 @@
     n_rows, feats = x.shape
     outs = (
         (grad.shape, F32),
-        ((LEAVES // 2, feats + EXTRA, LANE), F32),
+        ((PART, feats + EXTRA, LANE), F32),
         ((feats, n_rows), BF16),
         ((LEAVES, feats), F32),
         ((LEAVES, feats), F32),
@@ -307,13 +310,14 @@
     )
 
 
-def keep_part(table, x, weighted, moment, hsum, totals):
+def gram_part(codes, table, x, weighted, moment, hsum, totals):
     n_rows, feats = x.shape
     cost = pl.CostEstimate(
-        flops=LEAVES * n_rows * feats * feats, bytes_accessed=4 * n_rows * feats, transcendentals=0
-    )
-    outs = (((LEAVES // 2, feats + EXTRA, LANE), F32),)
-    return on_chip(keep_kernel, outs, [], (table, x, weighted, moment, hsum, totals), cost)[0]
+        flops=8 * PART * n_rows * feats * feats, bytes_accessed=n_rows * feats, transcendentals=0
+    )
+    outs = (((PART, feats + EXTRA, LANE), F32),)
+    kernel = functools.partial(gram_kernel, codes)
+    return on_chip(kernel, outs, [], (table, x, weighted, moment, hsum, totals), cost)[0]
 
 
 def fold_kernel(keep_ref, other_ref, *outs):
@@ -360,8 +364,21 @@
     return [t if t is None else t * scale for t in tiles]
 
 
-def exact_dot(a, b):
-    return jnp.dot(a, b, precision=lax.Precision.HIGHEST, preferred_element_type=F32)
+def three(value):
+    top = value.astype(BF16)
+    left = value - top.astype(F32)
+    middle = left.astype(BF16)
+    return top, middle, (left - middle.astype(F32)).astype(BF16)
+
+
+def left_parts(value):
+    top, middle, bottom = three(value)
+    return jnp.concatenate([top, top, middle, top, middle, bottom], axis=1)
+
+
+def right_parts(value):
+    top, middle, bottom = three(value)
+    return jnp.concatenate([top, middle, top, bottom, middle, top], axis=0)
 
 
 def solve_kernel(*refs):
@@ -410,7 +427,7 @@
         tile, offset = s // per_tile, (s % per_tile) * STRIP
         done = eliminate([None] * tile + strips[s][tile:], tile, offset)
         strips[s] = done
-        solved = jnp.concatenate(done[tile:], axis=1)
+        solved = right_parts(jnp.concatenate(done[tile:], axis=1))
         later = [s + 1] if s + 1 < count else []
         others = [i for i in range(count) if i not in (s, s + 1)]
         for group in (later, others):
@@ -419,7 +436,7 @@
             left = jnp.concatenate(
                 [strips[i][tile][:, offset : offset + STRIP] for i in group], axis=0
             )
-            change = exact_dot(left, solved)
+            change = jnp.dot(left_parts(left), solved, preferred_element_type=F32)
             for q, i in enumerate(group):
                 part = change[q * STRIP : (q + 1) * STRIP]
                 strips[i] = [
@@ -447,11 +464,7 @@
     high = jnp.concatenate([c[1:2, :] for c in slots], axis=0)
     shift = jnp.concatenate([c[2:3, :] for c in slots], axis=0)[:, 0:1]
     coefs = jnp.concatenate([low, high], axis=1)
-    top = coefs.astype(BF16)
-    left = coefs - top.astype(F32)
-    middle = left.astype(BF16)
-    bottom = (left - middle.astype(F32)).astype(BF16)
-    stacked = jnp.concatenate([top, middle, bottom], axis=0)
+    stacked = jnp.concatenate(three(coefs), axis=0)
     parts = lax.dot_general(
         stacked, x_ref[...], (((1,), (1,)), ((), ())), preferred_element_type=F32
     )
@@ -490,9 +503,14 @@
     )
     grad, hess = interior(table)
     grad, send, *sums, held = boundary(table, x, inner, outer, grad, hess)
-    other = swapped(send, 1)
-    chunks = fold(keep_part(table, held, *sums), other)
-    mine = total([swapped(c, flip) if flip else c for c, flip in zip(chunks, NEAR)])
+    chunks = []
+    for codes in NEAR:
+        if chunks:
+            send = gram_part(other_core(codes), table, held, *sums)
+        other = swapped(send, 1)
+        folded = fold(gram_part(codes, table, held, *sums), other)
+        chunks += [swapped(c, 2 * code) if code else c for c, code in zip(folded, codes)]
+    mine = total(chunks)
     parts = [mine, swapped(mine, 16)]
     bit = 32
     while bit < devices:

time: 63.5 us -> 61 us (0.961)
  starting transfers between devices: 26.1 us -> 22.5 us
  waiting for transfers between devices: 18 us -> 19.8 us
  Pallas kernels: 17.7 us -> 16.8 us
    ppermute x16 -> x17, starting transfers between devices: 25.5 us -> 21.9 us  [swapped(): return lax.ppermute(value, AXES, [(i, i ^ flip) for i in range(devices)])]
    ppermute x16 -> x17, waiting for transfers between devices: 18 us -> 19.8 us  [swapped(): return lax.ppermute(value, AXES, [(i, i ^ flip) for i in range(devices)])]
    pallas_call x7 -> x10, Pallas kernels: 16.3 us -> 15.3 us  [on_chip(): pl.pallas_call(kernel, out_shape=tuple((jax.ShapeDtypeStruct(shape, kind)...]
  transfers between devices with their start and end apart: 17 -> 18, of which waited for: 10 -> 11; matrix products, arithmetic and copies ran while one was open for 0% -> 0% of each run, Pallas kernels for 6% -> 7%
where the time goes in v4:
time: 61 us; the launch traced here: 60.7 us
  starting transfers between devices  22.5 us (37%)
  waiting for transfers between devices  19.8 us (32%)
  Pallas kernels  16.8 us (28%)
  local copies, waits for them, and re-layouts  0.89 us (1%)
  between operations  0.74 us (1%)
    ppermute x17, starting transfers between devices, swapped(): return lax.ppermute(value, AXES, [(i, i ^ flip) for i in range(devices)])  21.9 us
    ppermute x17, waiting for transfers between devices, swapped(): return lax.ppermute(value, AXES, [(i, i ^ flip) for i in range(devices)])  19.8 us
    pallas_call x10, Pallas kernels, on_chip(): pl.pallas_call(kernel, out_shape=tuple((jax.ShapeDtypeStruct(shape, kind)...  15.3 us
    pallas_call x1, Pallas kernels, edges(): pl.pallas_call(edge_kernel, out_shape=(edge, edge, jax.ShapeDtypeStruct((...  1.4 us
  transfers between devices with their start and end apart: 18, of which 11 were waited for; matrix products, arithmetic and copies ran while one was open for 0% of the time, Pallas kernels for 7%

profile of v4, /device:TPU:0, one launch (start us, length us, event | category | flops | bytes accessed | tf_op | source)
XLA Modules:
  0.0 60.7 jit_solution(2917819679150386299)
XLA Ops:
  0.6 1.4 %shard_map.85 = (f32[4,128]{1,0:T(4,128)}, f32[4,128]{1,0:T(4,128)}, f32[5,8,128]{2,1,0:T(8,128)}) custom-call(s32[8,128]{1,0:T(8,128)} %bitcast.13, s32[8,128]{1,0:T(8,128)} %bitcast.14, s32[8,128]{1,0:T(8,128)} %bitcast.15, f32[8,128]{1,0:T(8,128)} %bitcast.16, s32[8,128]{1,0:T(8,128)} %bitcast.17), custom_call_target="tpu_custom_call" | custom-call | tf_op jit(solution)/shard_map/pallas_call | solution.py:88
  2.7 0.6 %collective-permute-start.1 = (f32[4,128]{1,0:T(4,128)S(1)}, f32[4,128]{1,0:T(4,128)S(1)}, u32[]{:S(2)}, u32[]{:S(2)}) collective-permute-start(f32[4,128]{1,0:T(4,128)S(1)} %copy-done.3), channel_id=1, source_target_pairs={{1,2},{2,1},{3,4},{4,3},{5,6},{6,5},{7,8},{8,7},{9,10},{10,9},{11,... | collective-permute-start | bytes 6152 | tf_op jit(solution)/shard_map/ppermute | solution.py:501
  3.4 0.7 %copy-done.1 = f32[5,8,128]{2,1,0:T(8,128)S(1)} copy-done((f32[5,8,128]{2,1,0:T(8,128)S(1)}, f32[5,8,128]{2,1,0:T(8,128)}, u32[]{:S(2)}) %copy-start.1) | copy-done | bytes 20504
  4.1 2.1 %shard_map.86 = (f32[8,128]{1,0:T(8,128)S(1)}, f32[8,128]{1,0:T(8,128)S(1)}) custom-call(f32[5,8,128]{2,1,0:T(8,128)S(1)} %copy-done.1), custom_call_target="tpu_custom_call" | custom-call | flops 2621440000 | bytes 131072 | tf_op jit(solution)/shard_map/pallas_call | solution.py:277
  6.3 2.4 %shard_map.87 = (f32[8,128]{1,0:T(8,128)}, f32[4,264,128]{2,1,0:T(8,128)S(1)}, bf16[256,1024]{1,0:T(8,128)(2,1)S(1)}, f32[16,256]{1,0:T(8,128)S(1)}, f32[16,256]...) custom-call(f32[5,8,128]{2,1,0:T(8,128)S(1)} %copy-done.1, bf16[1024,256]{1,0:T(8,128)(2,1)S(1)} %copy-done, ...), custom_call_target="tpu_custom_call" | custom-call | tf_op jit(solution)/shard_map/pallas_call | solution.py:277
  8.7 4.3 %collective-permute-start.2 = (f32[4,264,128]{2,1,0:T(8,128)S(1)}, f32[4,264,128]{2,1,0:T(8,128)S(1)}, u32[]{:S(2)}, u32[]{:S(2)}) collective-permute-start(f32[4,264,128]{2,1,0:T(8,128)S(1)} %get-tuple-element.36), channel_id=1, source_target_pairs={{0,1},{1,0},{2,3},{3,2},{4,5},{5,4},{6,7},{7,6},{8,9},{9,8},{10,11... | collective-permute-start | bytes 1622024 | tf_op jit(solution)/shard_map/ppermute | solution.py:496
  13.0 0.7 %shard_map.91 = f32[4,264,128]{2,1,0:T(8,128)S(1)} custom-call(f32[5,8,128]{2,1,0:T(8,128)S(1)} %copy-done.1, bf16[1024,256]{1,0:T(8,128)(2,1)S(1)} %get-tuple-element.31.x_ref, bf16[256,1024]{1,0:T(8,128)(2,1)S(1)} %get-tuple-element.32.weighted, f32[16,256]{1,0:T(8,128)S(1)} %get-tuple-element.33.moment_s, f32[16,256]{1,0:T(8,128)S(1)} %get-tuple-element.34.hsum_s, ...), custom_call_target="tpu_custom_call" | custom-call | flops 2147483648 | bytes 262144 | tf_op jit(solution)/shard_map/pallas_call | solution.py:277
  13.8 0.7 %shard_map.88.keep_ref = f32[4,264,128]{2,1,0:T(8,128)S(1)} custom-call(f32[5,8,128]{2,1,0:T(8,128)S(1)} %copy-done.1, bf16[1024,256]{1,0:T(8,128)(2,1)S(1)} %get-tuple-element.31.x_ref, bf16[256,1024]{1,0:T(8,128)(2,1)S(1)} %get-tuple-element.32.weighted, f32[16,256]{1,0:T(8,128)S(1)} %get-tuple-element.33.moment_s, ...), custom_call_target="tpu_custom_call" | custom-call | flops 2147483648 | bytes 262144 | tf_op jit(solution)/shard_map/pallas_call | solution.py:277
  14.6 2.4 %collective-permute-start.3 = (f32[264,128]{1,0:T(8,128)S(1)}, f32[264,128]{1,0:T(8,128)S(1)}, u32[]{:S(2)}, u32[]{:S(2)}) collective-permute-start(f32[264,128]{1,0:T(8,128)S(1)} %get-tuple-element.38), channel_id=1, source_target_pairs={{0,8},{1,9},{2,10},{3,11},{4,12},{5,13},{6,14},{7,15},{8,0},{9,1},... | collective-permute-start | bytes 405512 | tf_op jit(solution)/shard_map/ppermute | solution.py:496
  17.0 0.8 %collective-permute-start.4 = (f32[264,128]{1,0:T(8,128)S(1)}, f32[264,128]{1,0:T(8,128)S(1)}, u32[]{:S(2)}, u32[]{:S(2)}) collective-permute-start(f32[264,128]{1,0:T(8,128)S(1)} %get-tuple-element.39), channel_id=1, source_target_pairs={{0,4},{1,5},{2,6},{3,7},{4,0},{5,1},{6,2},{7,3},{8,12},{9,13},{10,... | collective-permute-start | bytes 405512 | tf_op jit(solution)/shard_map/ppermute | solution.py:496
  17.8 0.7 %shard_map.90.keep_ref = f32[4,264,128]{2,1,0:T(8,128)S(1)} custom-call(f32[5,8,128]{2,1,0:T(8,128)S(1)} %copy-done.1, bf16[1024,256]{1,0:T(8,128)(2,1)S(1)} %get-tuple-element.31.x_ref, bf16[256,1024]{1,0:T(8,128)(2,1)S(1)} %get-tuple-element.32.weighted, f32[16,256]{1,0:T(8,128)S(1)} %get-tuple-element.33.moment_s, ...), custom_call_target="tpu_custom_call" | custom-call | flops 2147483648 | bytes 262144 | tf_op jit(solution)/shard_map/pallas_call | solution.py:277
  18.5 1.7 %collective-permute-start.5 = (f32[264,128]{1,0:T(8,128)S(1)}, f32[264,128]{1,0:T(8,128)S(1)}, u32[]{:S(2)}, u32[]{:S(2)}) collective-permute-start(f32[264,128]{1,0:T(8,128)S(1)} %get-tuple-element.40), channel_id=1, source_target_pairs={{0,2},{1,3},{2,0},{3,1},{4,6},{5,7},{6,4},{7,5},{8,10},{9,11},{10,... | collective-permute-start | bytes 405512 | tf_op jit(solution)/shard_map/ppermute | solution.py:496
  20.3 0.6 %collective-permute-start.7 = (f32[264,128]{1,0:T(8,128)S(1)}, f32[264,128]{1,0:T(8,128)S(1)}, u32[]{:S(2)}, u32[]{:S(2)}) collective-permute-start(f32[264,128]{1,0:T(8,128)S(1)} %get-tuple-element.41), channel_id=1, source_target_pairs={{0,14},{1,15},{2,12},{3,13},{4,10},{5,11},{6,8},{7,9},{8,6},{9,7},... | collective-permute-start | bytes 405512 | tf_op jit(solution)/shard_map/ppermute | solution.py:496
  20.9 2.2 %collective-permute-start.8 = (f32[264,128]{1,0:T(8,128)S(1)}, f32[264,128]{1,0:T(8,128)S(1)}, u32[]{:S(2)}, u32[]{:S(2)}) collective-permute-start(f32[264,128]{1,0:T(8,128)S(1)} %get-tuple-element.42), channel_id=1, source_target_pairs={{0,12},{1,13},{2,14},{3,15},{4,8},{5,9},{6,10},{7,11},{8,4},{9,5},... | collective-permute-start | bytes 405512 | tf_op jit(solution)/shard_map/ppermute | solution.py:496
  23.1 1.6 %collective-permute-start.9 = (f32[264,128]{1,0:T(8,128)S(1)}, f32[264,128]{1,0:T(8,128)S(1)}, u32[]{:S(2)}, u32[]{:S(2)}) collective-permute-start(f32[264,128]{1,0:T(8,128)S(1)} %get-tuple-element.43), channel_id=1, source_target_pairs={{0,10},{1,11},{2,8},{3,9},{4,14},{5,15},{6,12},{7,13},{8,2},{9,3},... | collective-permute-start | bytes 405512 | tf_op jit(solution)/shard_map/ppermute | solution.py:496
  24.6 0.7 %collective-permute-start.10 = (f32[264,128]{1,0:T(8,128)S(1)}, f32[264,128]{1,0:T(8,128)S(1)}, u32[]{:S(2)}, u32[]{:S(2)}) collective-permute-start(f32[264,128]{1,0:T(8,128)S(1)} %get-tuple-element.44), channel_id=1, source_target_pairs={{0,6},{1,7},{2,4},{3,5},{4,2},{5,3},{6,0},{7,1},{8,14},{9,15},{10,... | collective-permute-start | bytes 405512 | tf_op jit(solution)/shard_map/ppermute | solution.py:496
  25.3 2.1 %collective-permute-done.5.refs_3_ = f32[264,128]{1,0:T(8,128)S(1)} collective-permute-done((f32[264,128]{1,0:T(8,128)S(1)}, f32[264,128]{1,0:T(8,128)S(1)}, u32[]{:S(2)}, u32[]{:S(2)}) %collective-permute-start.5) | collective-permute-done | bytes 135200 | tf_op jit(solution)/shard_map/ppermute | solution.py:496
  27.4 2.2 %collective-permute-done.7.refs_4_ = f32[264,128]{1,0:T(8,128)S(1)} collective-permute-done((f32[264,128]{1,0:T(8,128)S(1)}, f32[264,128]{1,0:T(8,128)S(1)}, u32[]{:S(2)}, u32[]{:S(2)}) %collective-permute-start.7) | collective-permute-done | bytes 135200 | tf_op jit(solution)/shard_map/ppermute | solution.py:496
  29.7 1.7 %collective-permute-done.8.refs_5_ = f32[264,128]{1,0:T(8,128)S(1)} collective-permute-done((f32[264,128]{1,0:T(8,128)S(1)}, f32[264,128]{1,0:T(8,128)S(1)}, u32[]{:S(2)}, u32[]{:S(2)}) %collective-permute-start.8) | collective-permute-done | bytes 135200 | tf_op jit(solution)/shard_map/ppermute | solution.py:496
  31.4 0.6 collective-permute-done.9.refs_6_
  32.0 2.2 %collective-permute-done.10.refs_7_ = f32[264,128]{1,0:T(8,128)S(1)} collective-permute-done((f32[264,128]{1,0:T(8,128)S(1)}, f32[264,128]{1,0:T(8,128)S(1)}, u32[]{:S(2)}, u32[]{:S(2)}) %collective-permute-start.10) | collective-permute-done | bytes 135200 | tf_op jit(solution)/shard_map/ppermute | solution.py:496
  34.3 1.4 %collective-permute-start.11 = (f32[264,128]{1,0:T(8,128)S(1)}, f32[264,128]{1,0:T(8,128)S(1)}, u32[]{:S(2)}, u32[]{:S(2)}) collective-permute-start(f32[264,128]{1,0:T(8,128)S(1)} %shard_map.93.refs_0_), channel_id=1, source_target_pairs={{0,16},{1,17},{2,18},{3,19},{4,20},{5,21},{6,22},{7,23},{8,24},{9,... | collective-permute-start | bytes 405512 | tf_op jit(solution)/shard_map/ppermute | solution.py:496
  35.7 7.3 %collective-permute-done.11.refs_1_ = f32[264,128]{1,0:T(8,128)S(1)} collective-permute-done((f32[264,128]{1,0:T(8,128)S(1)}, f32[264,128]{1,0:T(8,128)S(1)}, u32[]{:S(2)}, u32[]{:S(2)}) %collective-permute-start.11) | collective-permute-done | bytes 135200 | tf_op jit(solution)/shard_map/ppermute | solution.py:496
  43.0 7.6 %shard_map.94 = f32[4,128]{1,0:T(4,128)S(1)} custom-call(f32[264,128]{1,0:T(8,128)S(1)} %shard_map.93.refs_0_, f32[264,128]{1,0:T(8,128)S(1)} %collective-permute-done.11.refs_1_), custom_call_target="tpu_custom_call" | custom-call | tf_op jit(solution)/shard_map/pallas_call | solution.py:277
  50.6 2.1 %collective-permute-start.12 = (f32[4,128]{1,0:T(4,128)S(1)}, f32[4,128]{1,0:T(4,128)S(1)}, u32[]{:S(2)}, u32[]{:S(2)}) collective-permute-start(f32[4,128]{1,0:T(4,128)S(1)} %shard_map.94), channel_id=1, source_target_pairs={{0,2},{1,3},{2,0},{3,1},{4,6},{5,7},{6,4},{7,5},{8,10},{9,11},{10,... | collective-permute-start | bytes 6152 | tf_op jit(solution)/shard_map/ppermute | solution.py:496
  52.7 0.9 %collective-permute-done.14 = f32[4,128]{1,0:T(4,128)S(1)} collective-permute-done((f32[4,128]{1,0:T(4,128)S(1)}, f32[4,128]{1,0:T(4,128)S(1)}, u32[]{:S(2)}, u32[]{:S(2)}) %collective-permute-start.14) | collective-permute-done | bytes 2080 | tf_op jit(solution)/shard_map/ppermute | solution.py:496
  53.6 0.7 %collective-permute-done.12 = f32[4,128]{1,0:T(4,128)S(1)} collective-permute-done((f32[4,128]{1,0:T(4,128)S(1)}, f32[4,128]{1,0:T(4,128)S(1)}, u32[]{:S(2)}, u32[]{:S(2)}) %collective-permute-start.12) | collective-permute-done | bytes 2080 | tf_op jit(solution)/shard_map/ppermute | solution.py:496
  54.3 1.0 %collective-permute-start.15 = (f32[4,4,128]{2,1,0:T(4,128)S(1)}, f32[4,4,128]{2,1,0:T(4,128)S(1)}, u32[]{:S(2)}, u32[]{:S(2)}) collective-permute-start(f32[4,4,128]{2,1,0:T(4,128)S(1)} %pad_maximum_fusion.c0), channel_id=1, source_target_pairs={{0,4},{1,5},{2,6},{3,7},{4,0},{5,1},{6,2},{7,3},{8,12},{9,13},{10,... | collective-permute-start | bytes 24584 | tf_op jit(solution)/shard_map/ppermute | solution.py:496
  55.3 2.5 %collective-permute-start.17 = (f32[4,4,128]{2,1,0:T(4,128)S(1)}, f32[4,4,128]{2,1,0:T(4,128)S(1)}, u32[]{:S(2)}, u32[]{:S(2)}) collective-permute-start(f32[4,4,128]{2,1,0:T(4,128)S(1)} %pad_maximum_fusion.c0), channel_id=1, source_target_pairs={{0,12},{1,13},{2,14},{3,15},{4,8},{5,9},{6,10},{7,11},{8,4},{9,5},... | collective-permute-start | bytes 24584 | tf_op jit(solution)/shard_map/ppermute | solution.py:496
  58.0 1.0 %collective-permute-done.16.c2 = f32[4,4,128]{2,1,0:T(4,128)S(1)} collective-permute-done((f32[4,4,128]{2,1,0:T(4,128)S(1)}, f32[4,4,128]{2,1,0:T(4,128)S(1)}, u32[]{:S(2)}, u32[]{:S(2)}) %collective-permute-start.16) | collective-permute-done | bytes 8224 | tf_op jit(solution)/shard_map/ppermute | solution.py:496
  58.9 0.9 %collective-permute-done.17.c3 = f32[4,4,128]{2,1,0:T(4,128)S(1)} collective-permute-done((f32[4,4,128]{2,1,0:T(4,128)S(1)}, f32[4,4,128]{2,1,0:T(4,128)S(1)}, u32[]{:S(2)}, u32[]{:S(2)}) %collective-permute-start.17) | collective-permute-done | bytes 8224 | tf_op jit(solution)/shard_map/ppermute | solution.py:496
  59.8 0.9 %shard_map.95 = (f32[8,128]{1,0:T(8,128)}, f32[8,128]{1,0:T(8,128)}) custom-call(f32[5,8,128]{2,1,0:T(8,128)S(1)} %copy-done.2, bf16[1024,256]{1,0:T(8,128)(2,1)S(1)} %copy-done, f32[4,4,128]{2,1,0:T(4,128)S(1)} %pad_maximum_fusion.c0, f32[4,4,128]{2,1,0:T(4,128)S(1)} %collective-permute-done.15.c1, f32[4,4,128]{2,1,0:T(4,128)S(1)} %collective-permute-done.16.c2, ...), custom_call_target="tpu_custom_call" | custom-call | tf_op jit(solution)/shard_map/pallas_call | solution.py:277
  (24 shorter events, 1.2 us)
Async XLA Ops:
  2.0 0.7 %copy-start.3 = (f32[4,128]{1,0:T(4,128)S(1)}, f32[4,128]{1,0:T(4,128)}, u32[]{:S(2)}) copy-start(f32[4,128]{1,0:T(4,128)} %get-tuple-element.27) | copy-start | bytes 6148
  2.1 4.2 %collective-permute-start = (f32[4,128]{1,0:T(4,128)}, f32[4,128]{1,0:T(4,128)S(1)}, u32[]{:S(2)}, u32[]{:S(2)}) collective-permute-start(f32[4,128]{1,0:T(4,128)} %get-tuple-element.26), channel_id=1, source_target_pairs={{0,1},{1,0},{2,3},{3,2},{4,5},{5,4},{6,7},{7,6},{8,9},{9,8},{10,11... | collective-permute-start | bytes 6152 | tf_op jit(solution)/shard_map/ppermute | solution.py:496
  2.7 3.5 %collective-permute-start.1 = (f32[4,128]{1,0:T(4,128)S(1)}, f32[4,128]{1,0:T(4,128)S(1)}, u32[]{:S(2)}, u32[]{:S(2)}) collective-permute-start(f32[4,128]{1,0:T(4,128)S(1)} %copy-done.3), channel_id=1, source_target_pairs={{1,2},{2,1},{3,4},{4,3},{5,6},{6,5},{7,8},{8,7},{9,10},{10,9},{11,... | collective-permute-start | bytes 6152 | tf_op jit(solution)/shard_map/ppermute | solution.py:501
  3.4 0.7 %copy-start.1 = (f32[5,8,128]{2,1,0:T(8,128)S(1)}, f32[5,8,128]{2,1,0:T(8,128)}, u32[]{:S(2)}) copy-start(f32[5,8,128]{2,1,0:T(8,128)} %get-tuple-element.25.table) | copy-start | bytes 61444
  4.1 2.2 %copy-start = (bf16[1024,256]{1,0:T(8,128)(2,1)S(1)}, bf16[1024,256]{1,0:T(8,128)(2,1)}, u32[]{:S(2)}) copy-start(bf16[1024,256]{1,0:T(8,128)(2,1)} %x_ref.3) | copy-start | bytes 1572868
  8.7 5.9 %collective-permute-start.2 = (f32[4,264,128]{2,1,0:T(8,128)S(1)}, f32[4,264,128]{2,1,0:T(8,128)S(1)}, u32[]{:S(2)}, u32[]{:S(2)}) collective-permute-start(f32[4,264,128]{2,1,0:T(8,128)S(1)} %get-tuple-element.36), channel_id=1, source_target_pairs={{0,1},{1,0},{2,3},{3,2},{4,5},{5,4},{6,7},{7,6},{8,9},{9,8},{10,11... | collective-permute-start | bytes 1622024 | tf_op jit(solution)/shard_map/ppermute | solution.py:496
  13.7 6.5 %collective-permute-start.6 = (f32[4,264,128]{2,1,0:T(8,128)S(1)}, f32[4,264,128]{2,1,0:T(8,128)S(1)}, u32[]{:S(2)}, u32[]{:S(2)}) collective-permute-start(f32[4,264,128]{2,1,0:T(8,128)S(1)} %shard_map.91), channel_id=1, source_target_pairs={{0,1},{1,0},{2,3},{3,2},{4,5},{5,4},{6,7},{7,6},{8,9},{9,8},{10,11... | collective-permute-start | bytes 1622024 | tf_op jit(solution)/shard_map/ppermute | solution.py:496
  14.6 8.5 %collective-permute-start.3 = (f32[264,128]{1,0:T(8,128)S(1)}, f32[264,128]{1,0:T(8,128)S(1)}, u32[]{:S(2)}, u32[]{:S(2)}) collective-permute-start(f32[264,128]{1,0:T(8,128)S(1)} %get-tuple-element.38), channel_id=1, source_target_pairs={{0,8},{1,9},{2,10},{3,11},{4,12},{5,13},{6,14},{7,15},{8,0},{9,1},... | collective-permute-start | bytes 405512 | tf_op jit(solution)/shard_map/ppermute | solution.py:496
  17.0 7.6 %collective-permute-start.4 = (f32[264,128]{1,0:T(8,128)S(1)}, f32[264,128]{1,0:T(8,128)S(1)}, u32[]{:S(2)}, u32[]{:S(2)}) collective-permute-start(f32[264,128]{1,0:T(8,128)S(1)} %get-tuple-element.39), channel_id=1, source_target_pairs={{0,4},{1,5},{2,6},{3,7},{4,0},{5,1},{6,2},{7,3},{8,12},{9,13},{10,... | collective-permute-start | bytes 405512 | tf_op jit(solution)/shard_map/ppermute | solution.py:496
  18.5 8.9 %collective-permute-start.5 = (f32[264,128]{1,0:T(8,128)S(1)}, f32[264,128]{1,0:T(8,128)S(1)}, u32[]{:S(2)}, u32[]{:S(2)}) collective-permute-start(f32[264,128]{1,0:T(8,128)S(1)} %get-tuple-element.40), channel_id=1, source_target_pairs={{0,2},{1,3},{2,0},{3,1},{4,6},{5,7},{6,4},{7,5},{8,10},{9,11},{10,... | collective-permute-start | bytes 405512 | tf_op jit(solution)/shard_map/ppermute | solution.py:496
  20.3 9.4 %collective-permute-start.7 = (f32[264,128]{1,0:T(8,128)S(1)}, f32[264,128]{1,0:T(8,128)S(1)}, u32[]{:S(2)}, u32[]{:S(2)}) collective-permute-start(f32[264,128]{1,0:T(8,128)S(1)} %get-tuple-element.41), channel_id=1, source_target_pairs={{0,14},{1,15},{2,12},{3,13},{4,10},{5,11},{6,8},{7,9},{8,6},{9,7},... | collective-permute-start | bytes 405512 | tf_op jit(solution)/shard_map/ppermute | solution.py:496
  20.9 10.5 %collective-permute-start.8 = (f32[264,128]{1,0:T(8,128)S(1)}, f32[264,128]{1,0:T(8,128)S(1)}, u32[]{:S(2)}, u32[]{:S(2)}) collective-permute-start(f32[264,128]{1,0:T(8,128)S(1)} %get-tuple-element.42), channel_id=1, source_target_pairs={{0,12},{1,13},{2,14},{3,15},{4,8},{5,9},{6,10},{7,11},{8,4},{9,5},... | collective-permute-start | bytes 405512 | tf_op jit(solution)/shard_map/ppermute | solution.py:496
  23.1 8.9 %collective-permute-start.9 = (f32[264,128]{1,0:T(8,128)S(1)}, f32[264,128]{1,0:T(8,128)S(1)}, u32[]{:S(2)}, u32[]{:S(2)}) collective-permute-start(f32[264,128]{1,0:T(8,128)S(1)} %get-tuple-element.43), channel_id=1, source_target_pairs={{0,10},{1,11},{2,8},{3,9},{4,14},{5,15},{6,12},{7,13},{8,2},{9,3},... | collective-permute-start | bytes 405512 | tf_op jit(solution)/shard_map/ppermute | solution.py:496
  24.6 9.6 %collective-permute-start.10 = (f32[264,128]{1,0:T(8,128)S(1)}, f32[264,128]{1,0:T(8,128)S(1)}, u32[]{:S(2)}, u32[]{:S(2)}) collective-permute-start(f32[264,128]{1,0:T(8,128)S(1)} %get-tuple-element.44), channel_id=1, source_target_pairs={{0,6},{1,7},{2,4},{3,5},{4,2},{5,3},{6,0},{7,1},{8,14},{9,15},{10,... | collective-permute-start | bytes 405512 | tf_op jit(solution)/shard_map/ppermute | solution.py:496
  34.3 8.7 %collective-permute-start.11 = (f32[264,128]{1,0:T(8,128)S(1)}, f32[264,128]{1,0:T(8,128)S(1)}, u32[]{:S(2)}, u32[]{:S(2)}) collective-permute-start(f32[264,128]{1,0:T(8,128)S(1)} %shard_map.93.refs_0_), channel_id=1, source_target_pairs={{0,16},{1,17},{2,18},{3,19},{4,20},{5,21},{6,22},{7,23},{8,24},{9,... | collective-permute-start | bytes 405512 | tf_op jit(solution)/shard_map/ppermute | solution.py:496
  50.6 9.3 %copy-start.2 = (f32[5,8,128]{2,1,0:T(8,128)S(1)}, f32[5,8,128]{2,1,0:T(8,128)}, u32[]{:S(2)}) copy-start(f32[5,8,128]{2,1,0:T(8,128)} %get-tuple-element.25.table) | copy-start | bytes 61444
  50.6 3.0 %collective-permute-start.14 = (f32[4,128]{1,0:T(4,128)S(1)}, f32[4,128]{1,0:T(4,128)S(1)}, u32[]{:S(2)}, u32[]{:S(2)}) collective-permute-start(f32[4,128]{1,0:T(4,128)S(1)} %shard_map.94), channel_id=1, source_target_pairs={{0,3},{1,2},{2,1},{3,0},{4,7},{5,6},{6,5},{7,4},{8,11},{9,10},{10,... | collective-permute-start | bytes 6152 | tf_op jit(solution)/shard_map/ppermute | solution.py:496
  50.6 3.0 %collective-permute-start.13 = (f32[4,128]{1,0:T(4,128)S(1)}, f32[4,128]{1,0:T(4,128)S(1)}, u32[]{:S(2)}, u32[]{:S(2)}) collective-permute-start(f32[4,128]{1,0:T(4,128)S(1)} %shard_map.94), channel_id=1, source_target_pairs={{0,1},{1,0},{2,3},{3,2},{4,5},{5,4},{6,7},{7,6},{8,9},{9,8},{10,11... | collective-permute-start | bytes 6152 | tf_op jit(solution)/shard_map/ppermute | solution.py:496
  50.6 3.7 %collective-permute-start.12 = (f32[4,128]{1,0:T(4,128)S(1)}, f32[4,128]{1,0:T(4,128)S(1)}, u32[]{:S(2)}, u32[]{:S(2)}) collective-permute-start(f32[4,128]{1,0:T(4,128)S(1)} %shard_map.94), channel_id=1, source_target_pairs={{0,2},{1,3},{2,0},{3,1},{4,6},{5,7},{6,4},{7,5},{8,10},{9,11},{10,... | collective-permute-start | bytes 6152 | tf_op jit(solution)/shard_map/ppermute | solution.py:496
  54.3 3.7 %collective-permute-start.15 = (f32[4,4,128]{2,1,0:T(4,128)S(1)}, f32[4,4,128]{2,1,0:T(4,128)S(1)}, u32[]{:S(2)}, u32[]{:S(2)}) collective-permute-start(f32[4,4,128]{2,1,0:T(4,128)S(1)} %pad_maximum_fusion.c0), channel_id=1, source_target_pairs={{0,4},{1,5},{2,6},{3,7},{4,0},{5,1},{6,2},{7,3},{8,12},{9,13},{10,... | collective-permute-start | bytes 24584 | tf_op jit(solution)/shard_map/ppermute | solution.py:496
  55.3 3.7 %collective-permute-start.16 = (f32[4,4,128]{2,1,0:T(4,128)S(1)}, f32[4,4,128]{2,1,0:T(4,128)S(1)}, u32[]{:S(2)}, u32[]{:S(2)}) collective-permute-start(f32[4,4,128]{2,1,0:T(4,128)S(1)} %pad_maximum_fusion.c0), channel_id=1, source_target_pairs={{0,8},{1,9},{2,10},{3,11},{4,12},{5,13},{6,14},{7,15},{8,0},{9,1},... | collective-permute-start | bytes 24584 | tf_op jit(solution)/shard_map/ppermute | solution.py:496
  55.3 4.5 %collective-permute-start.17 = (f32[4,4,128]{2,1,0:T(4,128)S(1)}, f32[4,4,128]{2,1,0:T(4,128)S(1)}, u32[]{:S(2)}, u32[]{:S(2)}) collective-permute-start(f32[4,4,128]{2,1,0:T(4,128)S(1)} %pad_maximum_fusion.c0), channel_id=1, source_target_pairs={{0,12},{1,13},{2,14},{3,15},{4,8},{5,9},{6,10},{7,11},{8,4},{9,5},... | collective-permute-start | bytes 24584 | tf_op jit(solution)/shard_map/ppermute | solution.py:496

commit v5 on v4

--- a/solution.py
+++ b/solution.py
@@ -18,7 +18,6 @@
 STRIP = 32
 GROUP = 16
 NEAR = ((0, 4, 2, 1), (7, 6, 5, 3))
-GATHER = ((0, 2, 1, 3), (0, 4, 8, 12))
 PART = 4
 VMEM_LIMIT = 48 * 1024 * 1024
 F32 = jnp.float32
@@ -120,9 +119,13 @@
         )
 
 
-def pair_block(own, start, rows, cols, packed_cols):
+def rank_table():
     positions = iota((LANE, LANE), 0).astype(F32) + 1.0
-    position_disc = 1.0 / jnp.log2(1.0 + positions)
+    return positions, 1.0 / jnp.log2(1.0 + positions)
+
+
+def pair_block(own, start, rows, cols, packed_cols, ranked):
+    positions, position_disc = ranked
     own_q = rows[0, pl.ds(own, 1), :]
     own_g = rows[1, pl.ds(own, 1), :]
     own_d = rows[2, pl.ds(own, 1), :]
@@ -204,13 +207,15 @@
         ref[0:1, :] = nothing
         ref[blocks - 1 : blocks, :] = nothing
 
+    ranked = rank_table()
+
     def one_block(b, carry):
-        grad, hess = pair_block(b, b - 1, rows, cols, packed_cols)
+        grad, hess = pair_block(b, b - 1, rows, cols, packed_cols, ranked)
         grad_ref[pl.ds(b, 1), :] = grad
         hess_ref[pl.ds(b, 1), :] = hess
         return carry
 
-    lax.fori_loop(1, blocks - 1, one_block, 0)
+    lax.fori_loop(1, blocks - 1, one_block, 0, unroll=6)
 
 
 def boundary_kernel(
@@ -244,8 +249,9 @@
     pair_tables(
         jnp.where(outside, -1.0, ids), window(1), window(2), window(3), rows, cols, packed_cols
     )
-    head_grad, head_hess = pair_block(1, 0, rows, cols, packed_cols)
-    tail_grad, tail_hess = pair_block(4, 3, rows, cols, packed_cols)
+    ranked = rank_table()
+    head_grad, head_hess = pair_block(1, 0, rows, cols, packed_cols, ranked)
+    tail_grad, tail_hess = pair_block(4, 3, rows, cols, packed_cols, ranked)
     grads = jnp.concatenate([head_grad, grad_part[1:final, :], tail_grad], axis=0)
     hesses = jnp.concatenate([head_hess, hess_part[1:final, :], tail_hess], axis=0)
     grad_ref[...] = grads
@@ -448,18 +454,18 @@
     w1 = jnp.concatenate(right[per_tile:], axis=0).T[0:1, :]
     dotted = jnp.sum(hs0 * w0 + hs1 * w1, axis=1, keepdims=True)
     intercept = -(gtot + dotted) * inv_den
-    out_ref[...] = jnp.concatenate(
+    result = jnp.concatenate(
         [w0, w1, jnp.broadcast_to(intercept, (1, LANE)), jnp.zeros((1, LANE), F32)], axis=0
     )
-
-
-def solve_leaf(parts):
-    return on_chip(solve_kernel, (((4, LANE), F32),), [], parts)[0]
-
-
-def output_kernel(table, x_ref, c0, c1, c2, c3, tree_ref, new_ref):
-    groups = (c0, c1, c2, c3)
-    slots = [groups[n >> 1 & 3][(n >> 3) * 2 + (n & 1)] for n in range(LEAVES)]
+    out_ref[...] = jnp.broadcast_to(result[None], out_ref.shape)
+
+
+def solve_leaf(parts, copies):
+    return on_chip(solve_kernel, (((copies, 4, LANE), F32),), [], parts)[0]
+
+
+def output_kernel(table, x_ref, coef_ref, tree_ref, new_ref):
+    slots = [coef_ref[(n >> 3) * 17 + (n & 7) * 2] for n in range(LEAVES)]
     low = jnp.concatenate([c[0:1, :] for c in slots], axis=0)
     high = jnp.concatenate([c[1:2, :] for c in slots], axis=0)
     shift = jnp.concatenate([c[2:3, :] for c in slots], axis=0)[:, 0:1]
@@ -472,7 +478,7 @@
         parts[:LEAVES] + (parts[LEAVES : 2 * LEAVES] + parts[2 * LEAVES :])
     ) + shift
     leaf_all = lanes_of(table[4])
-    leaf_at = (iota(per_leaf.shape, 0) ^ slot_mask(position())).astype(F32)
+    leaf_at = iota(per_leaf.shape, 0).astype(F32)
     chosen = jnp.sum(jnp.where(leaf_all == leaf_at, per_leaf, 0.0), axis=0, keepdims=True)
     for b in range(tree_ref.shape[0]):
         piece = chosen[:, b * LANE : (b + 1) * LANE]
@@ -482,7 +488,7 @@
 
 def row_outputs(table, x, coefs):
     row = (table.shape[1:], F32)
-    return on_chip(output_kernel, (row, row), [], (table, x, *coefs))
+    return on_chip(output_kernel, (row, row), [], (table, x, coefs))
 
 
 def body(features, scores, labels, query_ids, ranks, leaf_ids):
@@ -511,15 +517,14 @@
         folded = fold(gram_part(codes, table, held, *sums), other)
         chunks += [swapped(c, 2 * code) if code else c for c, code in zip(folded, codes)]
     mine = total(chunks)
-    parts = [mine, swapped(mine, 16)]
+    owner = [(d >> 4 & 1) == (d & 1) for d in range(devices)]
+    parts = [mine, lax.ppermute(mine, AXES, [(d, d ^ (1 if o else 16)) for d, o in enumerate(owner)])]
     bit = 32
     while bit < devices:
         mine = parts[0] + parts[1]
         parts = [mine, swapped(mine, bit)]
         bit *= 2
-    coefs = solve_leaf(parts)
-    group = jnp.stack([swapped(coefs, flip) if flip else coefs for flip in GATHER[0]])
-    coefs = [swapped(group, flip) if flip else group for flip in GATHER[1]]
+    coefs = lax.all_to_all(solve_leaf(parts, devices), AXES, 0, 0, tiled=True)
     tree, fresh = row_outputs(table, x, coefs)
     return grad.reshape(-1), tree.reshape(-1), fresh.reshape(-1)
 

time: 61 us -> 59.6 us (0.977)
  blocking collectives: 0 us -> 9.1 us
  starting transfers between devices: 22.5 us -> 16.1 us
  waiting for transfers between devices: 19.8 us -> 16.3 us
    ppermute x17 -> x10, waiting for transfers between devices: 19.8 us -> 8.93 us  [swapped(): return lax.ppermute(value, AXES, [(i, i ^ flip) for i in range(devices)])]
    all_to_all x0 -> x1, blocking collectives: none -> 9.1 us  [body(): coefs = lax.all_to_all(solve_leaf(parts, devices), AXES, 0, 0, tiled=True)]
    ppermute x0 -> x1, waiting for transfers between devices: none -> 7.35 us  [body(): lax.ppermute(mine, AXES, [(d, d ^ (1 if o else 16)) for d, o in enumerate...]
    ppermute x17 -> x10, starting transfers between devices: 21.9 us -> 15.4 us  [swapped(): return lax.ppermute(value, AXES, [(i, i ^ flip) for i in range(devices)])]
  transfers between devices with their start and end apart: 18 -> 12, of which waited for: 11 -> 6; matrix products, arithmetic and copies ran while one was open for 0% -> 0% of each run, Pallas kernels for 7% -> 6%
where the time goes in v5:
time: 59.6 us; the launch traced here: 59.3 us
  waiting for transfers between devices  16.3 us (27%)
  Pallas kernels  16.2 us (27%)
  starting transfers between devices  16.1 us (27%)
  blocking collectives  9.1 us (15%)
  local copies, waits for them, and re-layouts  0.89 us (1%)
  between operations  0.76 us (1%)
    ppermute x10, starting transfers between devices, swapped(): return lax.ppermute(value, AXES, [(i, i ^ flip) for i in range(devices)])  15.4 us
    pallas_call x10, Pallas kernels, on_chip(): pl.pallas_call(kernel, out_shape=tuple((jax.ShapeDtypeStruct(shape, kind)...  14.8 us
    all_to_all x1, blocking collectives, body(): coefs = lax.all_to_all(solve_leaf(parts, devices), AXES, 0, 0, tiled=True)  9.1 us
    ppermute x10, waiting for transfers between devices, swapped(): return lax.ppermute(value, AXES, [(i, i ^ flip) for i in range(devices)])  8.93 us
    ppermute x1, waiting for transfers between devices, body(): lax.ppermute(mine, AXES, [(d, d ^ (1 if o else 16)) for d, o in enumerate...  7.35 us
    pallas_call x1, Pallas kernels, edges(): pl.pallas_call(edge_kernel, out_shape=(edge, edge, jax.ShapeDtypeStruct((...  1.41 us
  transfers between devices with their start and end apart: 12, of which 6 were waited for; matrix products, arithmetic and copies ran while one was open for 0% of the time, Pallas kernels for 6%

profile of v5, /device:TPU:0, one launch (start us, length us, event | category | flops | bytes accessed | tf_op | source)
XLA Modules:
  0.0 59.3 jit_solution(17203472144848935331)
XLA Ops:
  0.6 1.4 %shard_map.85 = (f32[4,128]{1,0:T(4,128)}, f32[4,128]{1,0:T(4,128)}, f32[5,8,128]{2,1,0:T(8,128)}) custom-call(s32[8,128]{1,0:T(8,128)} %bitcast.8, s32[8,128]{1,0:T(8,128)} %bitcast.9, s32[8,128]{1,0:T(8,128)} %bitcast.10, f32[8,128]{1,0:T(8,128)} %bitcast.11, s32[8,128]{1,0:T(8,128)} %bitcast.12), custom_call_target="tpu_custom_call" | custom-call | tf_op jit(solution)/shard_map/pallas_call | solution.py:87
  2.1 0.5 collective-permute-start
  2.6 0.2 copy-done.3
  2.7 0.6 %collective-permute-start.1 = (f32[4,128]{1,0:T(4,128)S(1)}, f32[4,128]{1,0:T(4,128)S(1)}, u32[]{:S(2)}, u32[]{:S(2)}) collective-permute-start(f32[4,128]{1,0:T(4,128)S(1)} %copy-done.3), channel_id=1, source_target_pairs={{1,2},{2,1},{3,4},{4,3},{5,6},{6,5},{7,8},{8,7},{9,10},{10,9},{11,... | collective-permute-start | bytes 6152 | tf_op jit(solution)/shard_map/ppermute | solution.py:507
  3.4 0.7 %copy-done.1 = f32[5,8,128]{2,1,0:T(8,128)S(1)} copy-done((f32[5,8,128]{2,1,0:T(8,128)S(1)}, f32[5,8,128]{2,1,0:T(8,128)}, u32[]{:S(2)}) %copy-start.1) | copy-done | bytes 20504
  4.1 1.6 %shard_map.86 = (f32[8,128]{1,0:T(8,128)S(1)}, f32[8,128]{1,0:T(8,128)S(1)}) custom-call(f32[5,8,128]{2,1,0:T(8,128)S(1)} %copy-done.1), custom_call_target="tpu_custom_call" | custom-call | flops 2621440000 | bytes 131072 | tf_op jit(solution)/shard_map/pallas_call | solution.py:283
  5.7 2.4 %shard_map.87 = (f32[8,128]{1,0:T(8,128)}, f32[4,264,128]{2,1,0:T(8,128)S(1)}, bf16[256,1024]{1,0:T(8,128)(2,1)S(1)}, f32[16,256]{1,0:T(8,128)S(1)}, f32[16,256]...) custom-call(f32[5,8,128]{2,1,0:T(8,128)S(1)} %copy-done.1, bf16[1024,256]{1,0:T(8,128)(2,1)S(1)} %copy-done, ...), custom_call_target="tpu_custom_call" | custom-call | tf_op jit(solution)/shard_map/pallas_call | solution.py:283
  8.1 4.3 %collective-permute-start.2 = (f32[4,264,128]{2,1,0:T(8,128)S(1)}, f32[4,264,128]{2,1,0:T(8,128)S(1)}, u32[]{:S(2)}, u32[]{:S(2)}) collective-permute-start(f32[4,264,128]{2,1,0:T(8,128)S(1)} %get-tuple-element.36), channel_id=1, source_target_pairs={{0,1},{1,0},{2,3},{3,2},{4,5},{5,4},{6,7},{7,6},{8,9},{9,8},{10,11... | collective-permute-start | bytes 1622024 | tf_op jit(solution)/shard_map/ppermute | solution.py:502
  12.4 0.7 %shard_map.91 = f32[4,264,128]{2,1,0:T(8,128)S(1)} custom-call(f32[5,8,128]{2,1,0:T(8,128)S(1)} %copy-done.1, bf16[1024,256]{1,0:T(8,128)(2,1)S(1)} %get-tuple-element.31.x_ref, bf16[256,1024]{1,0:T(8,128)(2,1)S(1)} %get-tuple-element.32.weighted, f32[16,256]{1,0:T(8,128)S(1)} %get-tuple-element.33.moment_s, f32[16,256]{1,0:T(8,128)S(1)} %get-tuple-element.34.hsum_s, ...), custom_call_target="tpu_custom_call" | custom-call | flops 2147483648 | bytes 262144 | tf_op jit(solution)/shard_map/pallas_call | solution.py:283
  13.2 0.1 collective-permute-start.6
  13.2 0.7 %shard_map.88.keep_ref = f32[4,264,128]{2,1,0:T(8,128)S(1)} custom-call(f32[5,8,128]{2,1,0:T(8,128)S(1)} %copy-done.1, bf16[1024,256]{1,0:T(8,128)(2,1)S(1)} %get-tuple-element.31.x_ref, bf16[256,1024]{1,0:T(8,128)(2,1)S(1)} %get-tuple-element.32.weighted, f32[16,256]{1,0:T(8,128)S(1)} %get-tuple-element.33.moment_s, ...), custom_call_target="tpu_custom_call" | custom-call | flops 2147483648 | bytes 262144 | tf_op jit(solution)/shard_map/pallas_call | solution.py:283
  14.0 0.1 shard_map.89
  14.1 3.0 %collective-permute-start.3 = (f32[264,128]{1,0:T(8,128)S(1)}, f32[264,128]{1,0:T(8,128)S(1)}, u32[]{:S(2)}, u32[]{:S(2)}) collective-permute-start(f32[264,128]{1,0:T(8,128)S(1)} %get-tuple-element.38), channel_id=1, source_target_pairs={{0,8},{1,9},{2,10},{3,11},{4,12},{5,13},{6,14},{7,15},{8,0},{9,1},... | collective-permute-start | bytes 405512 | tf_op jit(solution)/shard_map/ppermute | solution.py:502
  17.0 0.6 %collective-permute-start.4 = (f32[264,128]{1,0:T(8,128)S(1)}, f32[264,128]{1,0:T(8,128)S(1)}, u32[]{:S(2)}, u32[]{:S(2)}) collective-permute-start(f32[264,128]{1,0:T(8,128)S(1)} %get-tuple-element.39), channel_id=1, source_target_pairs={{0,4},{1,5},{2,6},{3,7},{4,0},{5,1},{6,2},{7,3},{8,12},{9,13},{10,... | collective-permute-start | bytes 405512 | tf_op jit(solution)/shard_map/ppermute | solution.py:502
  17.6 0.7 %shard_map.90.keep_ref = f32[4,264,128]{2,1,0:T(8,128)S(1)} custom-call(f32[5,8,128]{2,1,0:T(8,128)S(1)} %copy-done.1, bf16[1024,256]{1,0:T(8,128)(2,1)S(1)} %get-tuple-element.31.x_ref, bf16[256,1024]{1,0:T(8,128)(2,1)S(1)} %get-tuple-element.32.weighted, f32[16,256]{1,0:T(8,128)S(1)} %get-tuple-element.33.moment_s, ...), custom_call_target="tpu_custom_call" | custom-call | flops 2147483648 | bytes 262144 | tf_op jit(solution)/shard_map/pallas_call | solution.py:283
  18.4 1.9 %collective-permute-start.5 = (f32[264,128]{1,0:T(8,128)S(1)}, f32[264,128]{1,0:T(8,128)S(1)}, u32[]{:S(2)}, u32[]{:S(2)}) collective-permute-start(f32[264,128]{1,0:T(8,128)S(1)} %get-tuple-element.40), channel_id=1, source_target_pairs={{0,2},{1,3},{2,0},{3,1},{4,6},{5,7},{6,4},{7,5},{8,10},{9,11},{10,... | collective-permute-start | bytes 405512 | tf_op jit(solution)/shard_map/ppermute | solution.py:502
  20.2 0.1 shard_map.92
  20.3 0.6 %collective-permute-start.7 = (f32[264,128]{1,0:T(8,128)S(1)}, f32[264,128]{1,0:T(8,128)S(1)}, u32[]{:S(2)}, u32[]{:S(2)}) collective-permute-start(f32[264,128]{1,0:T(8,128)S(1)} %get-tuple-element.41), channel_id=1, source_target_pairs={{0,14},{1,15},{2,12},{3,13},{4,10},{5,11},{6,8},{7,9},{8,6},{9,7},... | collective-permute-start | bytes 405512 | tf_op jit(solution)/shard_map/ppermute | solution.py:502
  20.9 2.0 %collective-permute-start.8 = (f32[264,128]{1,0:T(8,128)S(1)}, f32[264,128]{1,0:T(8,128)S(1)}, u32[]{:S(2)}, u32[]{:S(2)}) collective-permute-start(f32[264,128]{1,0:T(8,128)S(1)} %get-tuple-element.42), channel_id=1, source_target_pairs={{0,12},{1,13},{2,14},{3,15},{4,8},{5,9},{6,10},{7,11},{8,4},{9,5},... | collective-permute-start | bytes 405512 | tf_op jit(solution)/shard_map/ppermute | solution.py:502
  22.9 1.7 %collective-permute-start.9 = (f32[264,128]{1,0:T(8,128)S(1)}, f32[264,128]{1,0:T(8,128)S(1)}, u32[]{:S(2)}, u32[]{:S(2)}) collective-permute-start(f32[264,128]{1,0:T(8,128)S(1)} %get-tuple-element.43), channel_id=1, source_target_pairs={{0,10},{1,11},{2,8},{3,9},{4,14},{5,15},{6,12},{7,13},{8,2},{9,3},... | collective-permute-start | bytes 405512 | tf_op jit(solution)/shard_map/ppermute | solution.py:502
  24.7 0.7 %collective-permute-start.10 = (f32[264,128]{1,0:T(8,128)S(1)}, f32[264,128]{1,0:T(8,128)S(1)}, u32[]{:S(2)}, u32[]{:S(2)}) collective-permute-start(f32[264,128]{1,0:T(8,128)S(1)} %get-tuple-element.44), channel_id=1, source_target_pairs={{0,6},{1,7},{2,4},{3,5},{4,2},{5,3},{6,0},{7,1},{8,14},{9,15},{10,... | collective-permute-start | bytes 405512 | tf_op jit(solution)/shard_map/ppermute | solution.py:502
  25.3 2.2 %collective-permute-done.5.refs_3_ = f32[264,128]{1,0:T(8,128)S(1)} collective-permute-done((f32[264,128]{1,0:T(8,128)S(1)}, f32[264,128]{1,0:T(8,128)S(1)}, u32[]{:S(2)}, u32[]{:S(2)}) %collective-permute-start.5) | collective-permute-done | bytes 135200 | tf_op jit(solution)/shard_map/ppermute | solution.py:502
  27.5 2.2 %collective-permute-done.7.refs_4_ = f32[264,128]{1,0:T(8,128)S(1)} collective-permute-done((f32[264,128]{1,0:T(8,128)S(1)}, f32[264,128]{1,0:T(8,128)S(1)}, u32[]{:S(2)}, u32[]{:S(2)}) %collective-permute-start.7) | collective-permute-done | bytes 135200 | tf_op jit(solution)/shard_map/ppermute | solution.py:502
  29.7 1.7 %collective-permute-done.8.refs_5_ = f32[264,128]{1,0:T(8,128)S(1)} collective-permute-done((f32[264,128]{1,0:T(8,128)S(1)}, f32[264,128]{1,0:T(8,128)S(1)}, u32[]{:S(2)}, u32[]{:S(2)}) %collective-permute-start.8) | collective-permute-done | bytes 135200 | tf_op jit(solution)/shard_map/ppermute | solution.py:502
  31.4 0.8 %collective-permute-done.9.refs_6_ = f32[264,128]{1,0:T(8,128)S(1)} collective-permute-done((f32[264,128]{1,0:T(8,128)S(1)}, f32[264,128]{1,0:T(8,128)S(1)}, u32[]{:S(2)}, u32[]{:S(2)}) %collective-permute-start.9) | collective-permute-done | bytes 135200 | tf_op jit(solution)/shard_map/ppermute | solution.py:502
  32.2 2.0 %collective-permute-done.10.refs_7_ = f32[264,128]{1,0:T(8,128)S(1)} collective-permute-done((f32[264,128]{1,0:T(8,128)S(1)}, f32[264,128]{1,0:T(8,128)S(1)}, u32[]{:S(2)}, u32[]{:S(2)}) %collective-permute-start.10) | collective-permute-done | bytes 135200 | tf_op jit(solution)/shard_map/ppermute | solution.py:502
  34.2 0.1 shard_map.93.refs_0_
  34.3 0.1 collective-permute-start.11
  34.4 7.3 %collective-permute-done.11.refs_1_ = f32[264,128]{1,0:T(8,128)S(1)} collective-permute-done((f32[264,128]{1,0:T(8,128)S(1)}, f32[264,128]{1,0:T(8,128)S(1)}, u32[]{:S(2)}, u32[]{:S(2)}) %collective-permute-start.11) | collective-permute-done | bytes 135200 | tf_op jit(solution)/shard_map/ppermute | solution.py:521
  41.7 7.6 %shard_map.94 = f32[32,4,128]{2,1,0:T(4,128)S(1)} custom-call(f32[264,128]{1,0:T(8,128)S(1)} %shard_map.93.refs_0_, f32[264,128]{1,0:T(8,128)S(1)} %collective-permute-done.11.refs_1_), custom_call_target="tpu_custom_call" | custom-call | tf_op jit(solution)/shard_map/pallas_call | solution.py:283
  49.3 9.1 %all_to_all.5.coef_ref = f32[32,4,128]{2,1,0:T(4,128)S(1)} all-to-all(f32[32,4,128]{2,1,0:T(4,128)S(1)} %shard_map.94), channel_id=1, replica_groups=mesh['doc'=8,'leaf'=4] {'doc','leaf'}, dimensions={0} | all-to-all | bytes 131072 | tf_op jit(solution)/shard_map/all_to_all | solution.py:527
  58.4 0.9 %shard_map.95 = (f32[8,128]{1,0:T(8,128)}, f32[8,128]{1,0:T(8,128)}) custom-call(f32[5,8,128]{2,1,0:T(8,128)S(1)} %copy-done.2, bf16[1024,256]{1,0:T(8,128)(2,1)S(1)} %copy-done, f32[32,4,128]{2,1,0:T(4,128)S(1)} %all_to_all.5.coef_ref), custom_call_target="tpu_custom_call" | custom-call | tf_op jit(solution)/shard_map/pallas_call | solution.py:283
  (12 shorter events, 0.1 us)
Async XLA Ops:
  2.0 0.7 %copy-start.3 = (f32[4,128]{1,0:T(4,128)S(1)}, f32[4,128]{1,0:T(4,128)}, u32[]{:S(2)}) copy-start(f32[4,128]{1,0:T(4,128)} %get-tuple-element.27) | copy-start | bytes 6148
  2.1 3.6 %collective-permute-start = (f32[4,128]{1,0:T(4,128)}, f32[4,128]{1,0:T(4,128)S(1)}, u32[]{:S(2)}, u32[]{:S(2)}) collective-permute-start(f32[4,128]{1,0:T(4,128)} %get-tuple-element.26), channel_id=1, source_target_pairs={{0,1},{1,0},{2,3},{3,2},{4,5},{5,4},{6,7},{7,6},{8,9},{9,8},{10,11... | collective-permute-start | bytes 6152 | tf_op jit(solution)/shard_map/ppermute | solution.py:502
  2.7 3.0 %collective-permute-start.1 = (f32[4,128]{1,0:T(4,128)S(1)}, f32[4,128]{1,0:T(4,128)S(1)}, u32[]{:S(2)}, u32[]{:S(2)}) collective-permute-start(f32[4,128]{1,0:T(4,128)S(1)} %copy-done.3), channel_id=1, source_target_pairs={{1,2},{2,1},{3,4},{4,3},{5,6},{6,5},{7,8},{8,7},{9,10},{10,9},{11,... | collective-permute-start | bytes 6152 | tf_op jit(solution)/shard_map/ppermute | solution.py:507
  3.4 0.7 %copy-start.1 = (f32[5,8,128]{2,1,0:T(8,128)S(1)}, f32[5,8,128]{2,1,0:T(8,128)}, u32[]{:S(2)}) copy-start(f32[5,8,128]{2,1,0:T(8,128)} %get-tuple-element.25.table) | copy-start | bytes 61444
  4.1 1.6 %copy-start = (bf16[1024,256]{1,0:T(8,128)(2,1)S(1)}, bf16[1024,256]{1,0:T(8,128)(2,1)}, u32[]{:S(2)}) copy-start(bf16[1024,256]{1,0:T(8,128)(2,1)} %x_ref.3) | copy-start | bytes 1572868
  8.1 5.9 %collective-permute-start.2 = (f32[4,264,128]{2,1,0:T(8,128)S(1)}, f32[4,264,128]{2,1,0:T(8,128)S(1)}, u32[]{:S(2)}, u32[]{:S(2)}) collective-permute-start(f32[4,264,128]{2,1,0:T(8,128)S(1)} %get-tuple-element.36), channel_id=1, source_target_pairs={{0,1},{1,0},{2,3},{3,2},{4,5},{5,4},{6,7},{7,6},{8,9},{9,8},{10,11... | collective-permute-start | bytes 1622024 | tf_op jit(solution)/shard_map/ppermute | solution.py:502
  13.2 7.1 %collective-permute-start.6 = (f32[4,264,128]{2,1,0:T(8,128)S(1)}, f32[4,264,128]{2,1,0:T(8,128)S(1)}, u32[]{:S(2)}, u32[]{:S(2)}) collective-permute-start(f32[4,264,128]{2,1,0:T(8,128)S(1)} %shard_map.91), channel_id=1, source_target_pairs={{0,1},{1,0},{2,3},{3,2},{4,5},{5,4},{6,7},{7,6},{8,9},{9,8},{10,11... | collective-permute-start | bytes 1622024 | tf_op jit(solution)/shard_map/ppermute | solution.py:502
  14.1 8.9 %collective-permute-start.3 = (f32[264,128]{1,0:T(8,128)S(1)}, f32[264,128]{1,0:T(8,128)S(1)}, u32[]{:S(2)}, u32[]{:S(2)}) collective-permute-start(f32[264,128]{1,0:T(8,128)S(1)} %get-tuple-element.38), channel_id=1, source_target_pairs={{0,8},{1,9},{2,10},{3,11},{4,12},{5,13},{6,14},{7,15},{8,0},{9,1},... | collective-permute-start | bytes 405512 | tf_op jit(solution)/shard_map/ppermute | solution.py:502
  17.0 7.6 %collective-permute-start.4 = (f32[264,128]{1,0:T(8,128)S(1)}, f32[264,128]{1,0:T(8,128)S(1)}, u32[]{:S(2)}, u32[]{:S(2)}) collective-permute-start(f32[264,128]{1,0:T(8,128)S(1)} %get-tuple-element.39), channel_id=1, source_target_pairs={{0,4},{1,5},{2,6},{3,7},{4,0},{5,1},{6,2},{7,3},{8,12},{9,13},{10,... | collective-permute-start | bytes 405512 | tf_op jit(solution)/shard_map/ppermute | solution.py:502
  18.4 9.2 %collective-permute-start.5 = (f32[264,128]{1,0:T(8,128)S(1)}, f32[264,128]{1,0:T(8,128)S(1)}, u32[]{:S(2)}, u32[]{:S(2)}) collective-permute-start(f32[264,128]{1,0:T(8,128)S(1)} %get-tuple-element.40), channel_id=1, source_target_pairs={{0,2},{1,3},{2,0},{3,1},{4,6},{5,7},{6,4},{7,5},{8,10},{9,11},{10,... | collective-permute-start | bytes 405512 | tf_op jit(solution)/shard_map/ppermute | solution.py:502
  20.3 9.4 %collective-permute-start.7 = (f32[264,128]{1,0:T(8,128)S(1)}, f32[264,128]{1,0:T(8,128)S(1)}, u32[]{:S(2)}, u32[]{:S(2)}) collective-permute-start(f32[264,128]{1,0:T(8,128)S(1)} %get-tuple-element.41), channel_id=1, source_target_pairs={{0,14},{1,15},{2,12},{3,13},{4,10},{5,11},{6,8},{7,9},{8,6},{9,7},... | collective-permute-start | bytes 405512 | tf_op jit(solution)/shard_map/ppermute | solution.py:502
  20.9 10.5 %collective-permute-start.8 = (f32[264,128]{1,0:T(8,128)S(1)}, f32[264,128]{1,0:T(8,128)S(1)}, u32[]{:S(2)}, u32[]{:S(2)}) collective-permute-start(f32[264,128]{1,0:T(8,128)S(1)} %get-tuple-element.42), channel_id=1, source_target_pairs={{0,12},{1,13},{2,14},{3,15},{4,8},{5,9},{6,10},{7,11},{8,4},{9,5},... | collective-permute-start | bytes 405512 | tf_op jit(solution)/shard_map/ppermute | solution.py:502
  22.9 9.2 %collective-permute-start.9 = (f32[264,128]{1,0:T(8,128)S(1)}, f32[264,128]{1,0:T(8,128)S(1)}, u32[]{:S(2)}, u32[]{:S(2)}) collective-permute-start(f32[264,128]{1,0:T(8,128)S(1)} %get-tuple-element.43), channel_id=1, source_target_pairs={{0,10},{1,11},{2,8},{3,9},{4,14},{5,15},{6,12},{7,13},{8,2},{9,3},... | collective-permute-start | bytes 405512 | tf_op jit(solution)/shard_map/ppermute | solution.py:502
  24.7 9.6 %collective-permute-start.10 = (f32[264,128]{1,0:T(8,128)S(1)}, f32[264,128]{1,0:T(8,128)S(1)}, u32[]{:S(2)}, u32[]{:S(2)}) collective-permute-start(f32[264,128]{1,0:T(8,128)S(1)} %get-tuple-element.44), channel_id=1, source_target_pairs={{0,6},{1,7},{2,4},{3,5},{4,2},{5,3},{6,0},{7,1},{8,14},{9,15},{10,... | collective-permute-start | bytes 405512 | tf_op jit(solution)/shard_map/ppermute | solution.py:502
  34.3 7.4 %collective-permute-start.11 = (f32[264,128]{1,0:T(8,128)S(1)}, f32[264,128]{1,0:T(8,128)S(1)}, u32[]{:S(2)}, u32[]{:S(2)}) collective-permute-start(f32[264,128]{1,0:T(8,128)S(1)} %shard_map.93.refs_0_), channel_id=1, source_target_pairs={{0,1},{1,17},{2,3},{3,19},{4,5},{5,21},{6,7},{7,23},{8,9},{9,25},{... | collective-permute-start | bytes 405512 | tf_op jit(solution)/shard_map/ppermute | solution.py:521
  49.3 9.1 %copy-start.2 = (f32[5,8,128]{2,1,0:T(8,128)S(1)}, f32[5,8,128]{2,1,0:T(8,128)}, u32[]{:S(2)}) copy-start(f32[5,8,128]{2,1,0:T(8,128)} %get-tuple-element.25.table) | copy-start | bytes 61444

commit v6 on v5

--- a/solution.py
+++ b/solution.py
@@ -19,7 +19,7 @@
 GROUP = 16
 NEAR = ((0, 4, 2, 1), (7, 6, 5, 3))
 PART = 4
-VMEM_LIMIT = 48 * 1024 * 1024
+VMEM_LIMIT = 32 * 1024 * 1024
 F32 = jnp.float32
 BF16 = jnp.bfloat16
 
@@ -505,7 +505,7 @@
     inner, outer, table = edges(query, label, rank, score, leaf)
     inner = swapped(inner, 1)
     outer = lax.ppermute(
-        outer, AXES, [p for i in range(1, devices - 1, 2) for p in ((i, i + 1), (i + 1, i))]
+        outer, AXES, [(i, (i + (1 if i % 2 else -1)) % devices) for i in range(devices)]
     )
     grad, hess = interior(table)
     grad, send, *sums, held = boundary(table, x, inner, outer, grad, hess)

time: 59.6 us -> 59.4 us (level)
  waiting for transfers between devices: 16.3 us -> 14.8 us
  starting transfers between devices: 16.1 us -> 17.3 us
    ppermute x1, starting transfers between devices: 0.65 us -> 6.44 us  [body(): lax.ppermute(outer, AXES, [(i, (i + (1 if i % 2 else -1)) % devices) for...]
    ppermute x10, starting transfers between devices: 15.4 us -> 10.6 us  [swapped(): return lax.ppermute(value, AXES, [(i, i ^ flip) for i in range(devices)])]
    ppermute x10, waiting for transfers between devices: 8.93 us -> 6.06 us  [swapped(): return lax.ppermute(value, AXES, [(i, i ^ flip) for i in range(devices)])]
    ppermute x1, waiting for transfers between devices: 7.35 us -> 8.72 us  [body(): lax.ppermute(mine, AXES, [(d, d ^ (1 if o else 16)) for d, o in enumerate...]
  transfers between devices with their start and end apart: 12 -> 12, of which waited for: 6 -> 5; matrix products, arithmetic and copies ran while one was open for 0% -> 0% of each run, Pallas kernels for 6% -> 6%
where the time goes in v6:
time: 59.4 us; the launch traced here: 59.1 us
  starting transfers between devices  17.3 us (29%)
  Pallas kernels  16.2 us (27%)
  waiting for transfers between devices  14.8 us (25%)
  blocking collectives  9.1 us (15%)
  local copies, waits for them, and re-layouts  0.89 us (1%)
  between operations  0.76 us (1%)
    pallas_call x10, Pallas kernels, on_chip(): pl.pallas_call(kernel, out_shape=tuple((jax.ShapeDtypeStruct(shape, kind)...  14.8 us
    ppermute x10, starting transfers between devices, swapped(): return lax.ppermute(value, AXES, [(i, i ^ flip) for i in range(devices)])  10.6 us
    all_to_all x1, blocking collectives, body(): coefs = lax.all_to_all(solve_leaf(parts, devices), AXES, 0, 0, tiled=True)  9.1 us
    ppermute x1, waiting for transfers between devices, body(): lax.ppermute(mine, AXES, [(d, d ^ (1 if o else 16)) for d, o in enumerate...  8.72 us
    ppermute x1, starting transfers between devices, body(): lax.ppermute(outer, AXES, [(i, (i + (1 if i % 2 else -1)) % devices) for...  6.44 us
    ppermute x10, waiting for transfers between devices, swapped(): return lax.ppermute(value, AXES, [(i, i ^ flip) for i in range(devices)])  6.06 us
    pallas_call x1, Pallas kernels, edges(): pl.pallas_call(edge_kernel, out_shape=(edge, edge, jax.ShapeDtypeStruct((...  1.41 us
  transfers between devices with their start and end apart: 12, of which 5 were waited for; matrix products, arithmetic and copies ran while one was open for 0% of the time, Pallas kernels for 6%

profile of v6, /device:TPU:0, one launch (start us, length us, event | category | flops | bytes accessed | tf_op | source)
XLA Modules:
  0.0 59.1 jit_solution(4380684884909442880)
XLA Ops:
  0.6 1.4 %shard_map.85 = (f32[4,128]{1,0:T(4,128)}, f32[4,128]{1,0:T(4,128)}, f32[5,8,128]{2,1,0:T(8,128)}) custom-call(s32[8,128]{1,0:T(8,128)} %bitcast.8, s32[8,128]{1,0:T(8,128)} %bitcast.9, s32[8,128]{1,0:T(8,128)} %bitcast.10, f32[8,128]{1,0:T(8,128)} %bitcast.11, s32[8,128]{1,0:T(8,128)} %bitcast.12), custom_call_target="tpu_custom_call" | custom-call | tf_op jit(solution)/shard_map/pallas_call | solution.py:87
  2.0 0.0 copy-start.3
  2.1 0.5 collective-permute-start
  2.6 0.2 copy-done.3
  2.7 6.4 %collective-permute-start.1 = (f32[4,128]{1,0:T(4,128)S(1)}, f32[4,128]{1,0:T(4,128)S(1)}, u32[]{:S(2)}, u32[]{:S(2)}) collective-permute-start(f32[4,128]{1,0:T(4,128)S(1)} %copy-done.3), channel_id=1, source_target_pairs={{0,31},{1,2},{2,1},{3,4},{4,3},{5,6},{6,5},{7,8},{8,7},{9,10},{10,... | collective-permute-start | bytes 6152 | tf_op jit(solution)/shard_map/ppermute | solution.py:507
  9.2 0.7 %copy-done.1 = f32[5,8,128]{2,1,0:T(8,128)S(1)} copy-done((f32[5,8,128]{2,1,0:T(8,128)S(1)}, f32[5,8,128]{2,1,0:T(8,128)}, u32[]{:S(2)}) %copy-start.1) | copy-done | bytes 20504
  9.9 1.6 %shard_map.86 = (f32[8,128]{1,0:T(8,128)S(1)}, f32[8,128]{1,0:T(8,128)S(1)}) custom-call(f32[5,8,128]{2,1,0:T(8,128)S(1)} %copy-done.1), custom_call_target="tpu_custom_call" | custom-call | flops 2621440000 | bytes 131072 | tf_op jit(solution)/shard_map/pallas_call | solution.py:283
  11.5 0.0 collective-permute-done.inner
  11.5 0.0 collective-permute-done.1.outer
  11.5 2.4 %shard_map.87 = (f32[8,128]{1,0:T(8,128)}, f32[4,264,128]{2,1,0:T(8,128)S(1)}, bf16[256,1024]{1,0:T(8,128)(2,1)S(1)}, f32[16,256]{1,0:T(8,128)S(1)}, f32[16,256]...) custom-call(f32[5,8,128]{2,1,0:T(8,128)S(1)} %copy-done.1, bf16[1024,256]{1,0:T(8,128)(2,1)S(1)} %copy-done, ...), custom_call_target="tpu_custom_call" | custom-call | tf_op jit(solution)/shard_map/pallas_call | solution.py:283
  13.9 0.7 %shard_map.91 = f32[4,264,128]{2,1,0:T(8,128)S(1)} custom-call(f32[5,8,128]{2,1,0:T(8,128)S(1)} %copy-done.1, bf16[1024,256]{1,0:T(8,128)(2,1)S(1)} %get-tuple-element.31.x_ref, bf16[256,1024]{1,0:T(8,128)(2,1)S(1)} %get-tuple-element.32.weighted, f32[16,256]{1,0:T(8,128)S(1)} %get-tuple-element.33.moment_s, f32[16,256]{1,0:T(8,128)S(1)} %get-tuple-element.34.hsum_s, ...), custom_call_target="tpu_custom_call" | custom-call | flops 2147483648 | bytes 262144 | tf_op jit(solution)/shard_map/pallas_call | solution.py:283
  14.6 0.6 collective-permute-start.6
  15.2 0.7 %shard_map.88.keep_ref = f32[4,264,128]{2,1,0:T(8,128)S(1)} custom-call(f32[5,8,128]{2,1,0:T(8,128)S(1)} %copy-done.1, bf16[1024,256]{1,0:T(8,128)(2,1)S(1)} %get-tuple-element.31.x_ref, bf16[256,1024]{1,0:T(8,128)(2,1)S(1)} %get-tuple-element.32.weighted, f32[16,256]{1,0:T(8,128)S(1)} %get-tuple-element.33.moment_s, ...), custom_call_target="tpu_custom_call" | custom-call | flops 2147483648 | bytes 262144 | tf_op jit(solution)/shard_map/pallas_call | solution.py:283
  16.0 0.1 shard_map.89
  16.0 0.1 collective-permute-start.3
  16.1 0.1 collective-permute-start.4
  16.2 0.7 %shard_map.90.keep_ref = f32[4,264,128]{2,1,0:T(8,128)S(1)} custom-call(f32[5,8,128]{2,1,0:T(8,128)S(1)} %copy-done.1, bf16[1024,256]{1,0:T(8,128)(2,1)S(1)} %get-tuple-element.31.x_ref, bf16[256,1024]{1,0:T(8,128)(2,1)S(1)} %get-tuple-element.32.weighted, f32[16,256]{1,0:T(8,128)S(1)} %get-tuple-element.33.moment_s, ...), custom_call_target="tpu_custom_call" | custom-call | flops 2147483648 | bytes 262144 | tf_op jit(solution)/shard_map/pallas_call | solution.py:283
  16.9 1.5 %collective-permute-start.5 = (f32[264,128]{1,0:T(8,128)S(1)}, f32[264,128]{1,0:T(8,128)S(1)}, u32[]{:S(2)}, u32[]{:S(2)}) collective-permute-start(f32[264,128]{1,0:T(8,128)S(1)} %get-tuple-element.40), channel_id=1, source_target_pairs={{0,2},{1,3},{2,0},{3,1},{4,6},{5,7},{6,4},{7,5},{8,10},{9,11},{10,... | collective-permute-start | bytes 405512 | tf_op jit(solution)/shard_map/ppermute | solution.py:502
  18.4 0.1 shard_map.92
  18.4 3.5 %collective-permute-start.7 = (f32[264,128]{1,0:T(8,128)S(1)}, f32[264,128]{1,0:T(8,128)S(1)}, u32[]{:S(2)}, u32[]{:S(2)}) collective-permute-start(f32[264,128]{1,0:T(8,128)S(1)} %get-tuple-element.41), channel_id=1, source_target_pairs={{0,14},{1,15},{2,12},{3,13},{4,10},{5,11},{6,8},{7,9},{8,6},{9,7},... | collective-permute-start | bytes 405512 | tf_op jit(solution)/shard_map/ppermute | solution.py:502
  22.0 0.9 %collective-permute-start.9 = (f32[264,128]{1,0:T(8,128)S(1)}, f32[264,128]{1,0:T(8,128)S(1)}, u32[]{:S(2)}, u32[]{:S(2)}) collective-permute-start(f32[264,128]{1,0:T(8,128)S(1)} %get-tuple-element.43), channel_id=1, source_target_pairs={{0,10},{1,11},{2,8},{3,9},{4,14},{5,15},{6,12},{7,13},{8,2},{9,3},... | collective-permute-start | bytes 405512 | tf_op jit(solution)/shard_map/ppermute | solution.py:502
  22.9 3.5 %collective-permute-start.10 = (f32[264,128]{1,0:T(8,128)S(1)}, f32[264,128]{1,0:T(8,128)S(1)}, u32[]{:S(2)}, u32[]{:S(2)}) collective-permute-start(f32[264,128]{1,0:T(8,128)S(1)} %get-tuple-element.44), channel_id=1, source_target_pairs={{0,6},{1,7},{2,4},{3,5},{4,2},{5,3},{6,0},{7,1},{8,14},{9,15},{10,... | collective-permute-start | bytes 405512 | tf_op jit(solution)/shard_map/ppermute | solution.py:502
  26.4 1.1 %collective-permute-done.7.refs_4_ = f32[264,128]{1,0:T(8,128)S(1)} collective-permute-done((f32[264,128]{1,0:T(8,128)S(1)}, f32[264,128]{1,0:T(8,128)S(1)}, u32[]{:S(2)}, u32[]{:S(2)}) %collective-permute-start.7) | collective-permute-done | bytes 135200 | tf_op jit(solution)/shard_map/ppermute | solution.py:502
  27.5 2.5 %collective-permute-done.8.refs_5_ = f32[264,128]{1,0:T(8,128)S(1)} collective-permute-done((f32[264,128]{1,0:T(8,128)S(1)}, f32[264,128]{1,0:T(8,128)S(1)}, u32[]{:S(2)}, u32[]{:S(2)}) %collective-permute-start.8) | collective-permute-done | bytes 135200 | tf_op jit(solution)/shard_map/ppermute | solution.py:502
  29.9 0.7 %collective-permute-done.9.refs_6_ = f32[264,128]{1,0:T(8,128)S(1)} collective-permute-done((f32[264,128]{1,0:T(8,128)S(1)}, f32[264,128]{1,0:T(8,128)S(1)}, u32[]{:S(2)}, u32[]{:S(2)}) %collective-permute-start.9) | collective-permute-done | bytes 135200 | tf_op jit(solution)/shard_map/ppermute | solution.py:502
  30.6 1.8 %collective-permute-done.10.refs_7_ = f32[264,128]{1,0:T(8,128)S(1)} collective-permute-done((f32[264,128]{1,0:T(8,128)S(1)}, f32[264,128]{1,0:T(8,128)S(1)}, u32[]{:S(2)}, u32[]{:S(2)}) %collective-permute-start.10) | collective-permute-done | bytes 135200 | tf_op jit(solution)/shard_map/ppermute | solution.py:502
  32.4 0.1 shard_map.93.refs_0_
  32.5 0.2 collective-permute-start.11
  32.7 8.7 %collective-permute-done.11.refs_1_ = f32[264,128]{1,0:T(8,128)S(1)} collective-permute-done((f32[264,128]{1,0:T(8,128)S(1)}, f32[264,128]{1,0:T(8,128)S(1)}, u32[]{:S(2)}, u32[]{:S(2)}) %collective-permute-start.11) | collective-permute-done | bytes 135200 | tf_op jit(solution)/shard_map/ppermute | solution.py:521
  41.5 7.6 %shard_map.94 = f32[32,4,128]{2,1,0:T(4,128)S(1)} custom-call(f32[264,128]{1,0:T(8,128)S(1)} %shard_map.93.refs_0_, f32[264,128]{1,0:T(8,128)S(1)} %collective-permute-done.11.refs_1_), custom_call_target="tpu_custom_call" | custom-call | tf_op jit(solution)/shard_map/pallas_call | solution.py:283
  49.1 9.1 %all_to_all.5.coef_ref = f32[32,4,128]{2,1,0:T(4,128)S(1)} all-to-all(f32[32,4,128]{2,1,0:T(4,128)S(1)} %shard_map.94), channel_id=1, replica_groups=mesh['doc'=8,'leaf'=4] {'doc','leaf'}, dimensions={0} | all-to-all | bytes 131072 | tf_op jit(solution)/shard_map/all_to_all | solution.py:527
  58.2 0.9 %shard_map.95 = (f32[8,128]{1,0:T(8,128)}, f32[8,128]{1,0:T(8,128)}) custom-call(f32[5,8,128]{2,1,0:T(8,128)S(1)} %copy-done.2, bf16[1024,256]{1,0:T(8,128)(2,1)S(1)} %copy-done, f32[32,4,128]{2,1,0:T(4,128)S(1)} %all_to_all.5.coef_ref), custom_call_target="tpu_custom_call" | custom-call | tf_op jit(solution)/shard_map/pallas_call | solution.py:283
  (12 shorter events, 0.0 us)
Async XLA Ops:
  2.0 0.7 %copy-start.3 = (f32[4,128]{1,0:T(4,128)S(1)}, f32[4,128]{1,0:T(4,128)}, u32[]{:S(2)}) copy-start(f32[4,128]{1,0:T(4,128)} %get-tuple-element.27) | copy-start | bytes 6148
  2.1 9.4 %collective-permute-start = (f32[4,128]{1,0:T(4,128)}, f32[4,128]{1,0:T(4,128)S(1)}, u32[]{:S(2)}, u32[]{:S(2)}) collective-permute-start(f32[4,128]{1,0:T(4,128)} %get-tuple-element.26), channel_id=1, source_target_pairs={{0,1},{1,0},{2,3},{3,2},{4,5},{5,4},{6,7},{7,6},{8,9},{9,8},{10,11... | collective-permute-start | bytes 6152 | tf_op jit(solution)/shard_map/ppermute | solution.py:502
  2.7 8.8 %collective-permute-start.1 = (f32[4,128]{1,0:T(4,128)S(1)}, f32[4,128]{1,0:T(4,128)S(1)}, u32[]{:S(2)}, u32[]{:S(2)}) collective-permute-start(f32[4,128]{1,0:T(4,128)S(1)} %copy-done.3), channel_id=1, source_target_pairs={{0,31},{1,2},{2,1},{3,4},{4,3},{5,6},{6,5},{7,8},{8,7},{9,10},{10,... | collective-permute-start | bytes 6152 | tf_op jit(solution)/shard_map/ppermute | solution.py:507
  9.2 0.7 %copy-start.1 = (f32[5,8,128]{2,1,0:T(8,128)S(1)}, f32[5,8,128]{2,1,0:T(8,128)}, u32[]{:S(2)}) copy-start(f32[5,8,128]{2,1,0:T(8,128)} %get-tuple-element.25.table) | copy-start | bytes 61444
  9.9 1.6 %copy-start = (bf16[1024,256]{1,0:T(8,128)(2,1)S(1)}, bf16[1024,256]{1,0:T(8,128)(2,1)}, u32[]{:S(2)}) copy-start(bf16[1024,256]{1,0:T(8,128)(2,1)} %x_ref.3) | copy-start | bytes 1572868
  13.9 2.0 %collective-permute-start.2 = (f32[4,264,128]{2,1,0:T(8,128)S(1)}, f32[4,264,128]{2,1,0:T(8,128)S(1)}, u32[]{:S(2)}, u32[]{:S(2)}) collective-permute-start(f32[4,264,128]{2,1,0:T(8,128)S(1)} %get-tuple-element.36), channel_id=1, source_target_pairs={{0,1},{1,0},{2,3},{3,2},{4,5},{5,4},{6,7},{7,6},{8,9},{9,8},{10,11... | collective-permute-start | bytes 1622024 | tf_op jit(solution)/shard_map/ppermute | solution.py:502
  14.6 3.7 %collective-permute-start.6 = (f32[4,264,128]{2,1,0:T(8,128)S(1)}, f32[4,264,128]{2,1,0:T(8,128)S(1)}, u32[]{:S(2)}, u32[]{:S(2)}) collective-permute-start(f32[4,264,128]{2,1,0:T(8,128)S(1)} %shard_map.91), channel_id=1, source_target_pairs={{0,1},{1,0},{2,3},{3,2},{4,5},{5,4},{6,7},{7,6},{8,9},{9,8},{10,11... | collective-permute-start | bytes 1622024 | tf_op jit(solution)/shard_map/ppermute | solution.py:502
  16.0 5.9 %collective-permute-start.3 = (f32[264,128]{1,0:T(8,128)S(1)}, f32[264,128]{1,0:T(8,128)S(1)}, u32[]{:S(2)}, u32[]{:S(2)}) collective-permute-start(f32[264,128]{1,0:T(8,128)S(1)} %get-tuple-element.38), channel_id=1, source_target_pairs={{0,8},{1,9},{2,10},{3,11},{4,12},{5,13},{6,14},{7,15},{8,0},{9,1},... | collective-permute-start | bytes 405512 | tf_op jit(solution)/shard_map/ppermute | solution.py:502
  16.1 6.8 %collective-permute-start.4 = (f32[264,128]{1,0:T(8,128)S(1)}, f32[264,128]{1,0:T(8,128)S(1)}, u32[]{:S(2)}, u32[]{:S(2)}) collective-permute-start(f32[264,128]{1,0:T(8,128)S(1)} %get-tuple-element.39), channel_id=1, source_target_pairs={{0,4},{1,5},{2,6},{3,7},{4,0},{5,1},{6,2},{7,3},{8,12},{9,13},{10,... | collective-permute-start | bytes 405512 | tf_op jit(solution)/shard_map/ppermute | solution.py:502
  16.9 9.5 %collective-permute-start.5 = (f32[264,128]{1,0:T(8,128)S(1)}, f32[264,128]{1,0:T(8,128)S(1)}, u32[]{:S(2)}, u32[]{:S(2)}) collective-permute-start(f32[264,128]{1,0:T(8,128)S(1)} %get-tuple-element.40), channel_id=1, source_target_pairs={{0,2},{1,3},{2,0},{3,1},{4,6},{5,7},{6,4},{7,5},{8,10},{9,11},{10,... | collective-permute-start | bytes 405512 | tf_op jit(solution)/shard_map/ppermute | solution.py:502
  18.4 9.1 %collective-permute-start.7 = (f32[264,128]{1,0:T(8,128)S(1)}, f32[264,128]{1,0:T(8,128)S(1)}, u32[]{:S(2)}, u32[]{:S(2)}) collective-permute-start(f32[264,128]{1,0:T(8,128)S(1)} %get-tuple-element.41), channel_id=1, source_target_pairs={{0,14},{1,15},{2,12},{3,13},{4,10},{5,11},{6,8},{7,9},{8,6},{9,7},... | collective-permute-start | bytes 405512 | tf_op jit(solution)/shard_map/ppermute | solution.py:502
  22.0 8.0 %collective-permute-start.8 = (f32[264,128]{1,0:T(8,128)S(1)}, f32[264,128]{1,0:T(8,128)S(1)}, u32[]{:S(2)}, u32[]{:S(2)}) collective-permute-start(f32[264,128]{1,0:T(8,128)S(1)} %get-tuple-element.42), channel_id=1, source_target_pairs={{0,12},{1,13},{2,14},{3,15},{4,8},{5,9},{6,10},{7,11},{8,4},{9,5},... | collective-permute-start | bytes 405512 | tf_op jit(solution)/shard_map/ppermute | solution.py:502
  22.0 8.7 %collective-permute-start.9 = (f32[264,128]{1,0:T(8,128)S(1)}, f32[264,128]{1,0:T(8,128)S(1)}, u32[]{:S(2)}, u32[]{:S(2)}) collective-permute-start(f32[264,128]{1,0:T(8,128)S(1)} %get-tuple-element.43), channel_id=1, source_target_pairs={{0,10},{1,11},{2,8},{3,9},{4,14},{5,15},{6,12},{7,13},{8,2},{9,3},... | collective-permute-start | bytes 405512 | tf_op jit(solution)/shard_map/ppermute | solution.py:502
  22.9 9.5 %collective-permute-start.10 = (f32[264,128]{1,0:T(8,128)S(1)}, f32[264,128]{1,0:T(8,128)S(1)}, u32[]{:S(2)}, u32[]{:S(2)}) collective-permute-start(f32[264,128]{1,0:T(8,128)S(1)} %get-tuple-element.44), channel_id=1, source_target_pairs={{0,6},{1,7},{2,4},{3,5},{4,2},{5,3},{6,0},{7,1},{8,14},{9,15},{10,... | collective-permute-start | bytes 405512 | tf_op jit(solution)/shard_map/ppermute | solution.py:502
  32.5 9.0 %collective-permute-start.11 = (f32[264,128]{1,0:T(8,128)S(1)}, f32[264,128]{1,0:T(8,128)S(1)}, u32[]{:S(2)}, u32[]{:S(2)}) collective-permute-start(f32[264,128]{1,0:T(8,128)S(1)} %shard_map.93.refs_0_), channel_id=1, source_target_pairs={{0,1},{1,17},{2,3},{3,19},{4,5},{5,21},{6,7},{7,23},{8,9},{9,25},{... | collective-permute-start | bytes 405512 | tf_op jit(solution)/shard_map/ppermute | solution.py:521
  49.1 9.1 %copy-start.2 = (f32[5,8,128]{2,1,0:T(8,128)S(1)}, f32[5,8,128]{2,1,0:T(8,128)}, u32[]{:S(2)}) copy-start(f32[5,8,128]{2,1,0:T(8,128)} %get-tuple-element.25.table) | copy-start | bytes 61444

commit v7 on v6

--- a/solution.py
+++ b/solution.py
@@ -124,8 +124,7 @@
     return positions, 1.0 / jnp.log2(1.0 + positions)
 
 
-def pair_block(own, start, rows, cols, packed_cols, ranked):
-    positions, position_disc = ranked
+def pair_sums(own, start, tiles, rows, cols, packed_cols):
     own_q = rows[0, pl.ds(own, 1), :]
     own_g = rows[1, pl.ds(own, 1), :]
     own_d = rows[2, pl.ds(own, 1), :]
@@ -133,7 +132,7 @@
     grad_sum = jnp.zeros((8, LANE), F32)
     hess_sum = jnp.zeros((8, LANE), F32)
     counts = jnp.zeros((8, LANE), jnp.int32)
-    for chunk in range(3 * LANE // 8):
+    for chunk in range(tiles * LANE // 8):
         at = pl.ds(pl.multiple_of(start * LANE + chunk * 8, 8), 8)
         far_e = cols[3, at, :]
         same = cols[0, at, :] == own_q
@@ -144,6 +143,12 @@
         grad_sum = grad_sum + scaled * jnp.where(gap > 0.0, far_e, own_e)
         hess_sum = hess_sum + jnp.abs(scaled) * (far_e * inv)
         counts = counts + jnp.where(same, packed_cols[at, :], 0)
+    return grad_sum, hess_sum, counts
+
+
+def pair_finish(sums, own_e, ranked):
+    positions, position_disc = ranked
+    grad_sum, hess_sum, counts = sums
     count = jnp.sum(counts, axis=0, keepdims=True)
     grad = jnp.sum(grad_sum, axis=0, keepdims=True)
     hess = jnp.sum(hess_sum, axis=0, keepdims=True) * own_e
@@ -199,7 +204,7 @@
         )
 
 
-def interior_kernel(table, grad_ref, hess_ref, rows, cols, packed_cols):
+def interior_kernel(table, grad_ref, hess_ref, part_ref, count_ref, rows, cols, packed_cols):
     blocks = grad_ref.shape[0]
     pair_tables(table[0], table[1], table[2], table[3], rows, cols, packed_cols)
     nothing = jnp.zeros((1, LANE), F32)
@@ -207,10 +212,14 @@
         ref[0:1, :] = nothing
         ref[blocks - 1 : blocks, :] = nothing
 
+    for n, b in enumerate((0, blocks - 1)):
+        sums = pair_sums(b, n * (blocks - 2), 2, rows, cols, packed_cols)
+        part_ref[2 * n], part_ref[2 * n + 1], count_ref[n] = sums
     ranked = rank_table()
 
     def one_block(b, carry):
-        grad, hess = pair_block(b, b - 1, rows, cols, packed_cols, ranked)
+        sums = pair_sums(b, b - 1, 3, rows, cols, packed_cols)
+        grad, hess = pair_finish(sums, rows[3, pl.ds(b, 1), :], ranked)
         grad_ref[pl.ds(b, 1), :] = grad
         hess_ref[pl.ds(b, 1), :] = hess
         return carry
@@ -219,7 +228,7 @@
 
 
 def boundary_kernel(
-    table, x_ref, inner, outer, grad_part, hess_part,
+    table, x_ref, inner, outer, grad_part, hess_part, part_ref, count_ref,
     grad_ref, send_ref, weighted, moment_s, hsum_s, total_s, x_out,
     rows, cols, packed_cols,
 ):
@@ -236,8 +245,8 @@
         return jnp.concatenate(
             [
                 jnp.where(odd, near, far),
-                table[slot, 0:2, :],
-                table[slot, final - 1 :, :],
+                table[slot, 0:1, :],
+                table[slot, final:, :],
                 jnp.where(odd, far, near),
             ],
             axis=0,
@@ -245,13 +254,18 @@
 
     ids = window(0)
     at = iota(ids.shape, 0)
-    outside = ((at == 0) & (me == 0)) | ((at == 5) & (me == devices - 1))
+    outside = ((at == 0) & (me == 0)) | ((at == 3) & (me == devices - 1))
     pair_tables(
         jnp.where(outside, -1.0, ids), window(1), window(2), window(3), rows, cols, packed_cols
     )
     ranked = rank_table()
-    head_grad, head_hess = pair_block(1, 0, rows, cols, packed_cols, ranked)
-    tail_grad, tail_hess = pair_block(4, 3, rows, cols, packed_cols, ranked)
+    ends = []
+    for n in range(2):
+        sums = pair_sums(n + 1, 3 * n, 1, rows, cols, packed_cols)
+        held = (part_ref[2 * n], part_ref[2 * n + 1], count_ref[n])
+        sums = [a + b for a, b in zip(sums, held)]
+        ends.append(pair_finish(sums, rows[3, n + 1 : n + 2, :], ranked))
+    (head_grad, head_hess), (tail_grad, tail_hess) = ends
     grads = jnp.concatenate([head_grad, grad_part[1:final, :], tail_grad], axis=0)
     hesses = jnp.concatenate([head_hess, hess_part[1:final, :], tail_hess], axis=0)
     grad_ref[...] = grads
@@ -297,10 +311,11 @@
         flops=20000 * blocks * LANE * LANE, bytes_accessed=blocks * LANE * LANE, transcendentals=0
     )
     row = ((blocks, LANE), F32)
-    return on_chip(interior_kernel, (row, row), table_scratch(blocks), (table,), cost)
-
-
-def boundary(table, x, inner, outer, grad, hess):
+    parts = (((4, 8, LANE), F32), ((2, 8, LANE), jnp.int32))
+    return on_chip(interior_kernel, (row, row, *parts), table_scratch(blocks), (table,), cost)
+
+
+def boundary(table, x, inner, outer, grad, *parts):
     n_rows, feats = x.shape
     outs = (
         (grad.shape, F32),
@@ -312,7 +327,7 @@
         (x.shape, x.dtype),
     )
     return on_chip(
-        boundary_kernel, outs, table_scratch(6), (table, x, inner, outer, grad, hess)
+        boundary_kernel, outs, table_scratch(4), (table, x, inner, outer, grad, *parts)
     )
 
 
@@ -507,8 +522,8 @@
     outer = lax.ppermute(
         outer, AXES, [(i, (i + (1 if i % 2 else -1)) % devices) for i in range(devices)]
     )
-    grad, hess = interior(table)
-    grad, send, *sums, held = boundary(table, x, inner, outer, grad, hess)
+    grad, *rest = interior(table)
+    grad, send, *sums, held = boundary(table, x, inner, outer, grad, *rest)
     chunks = []
     for codes in NEAR:
         if chunks:

time: 59.4 us -> 58.7 us (0.988)
  transfers between devices with their start and end apart: 12 -> 12, of which waited for: 5 -> 5; matrix products, arithmetic and copies ran while one was open for 0% -> 0% of each run, Pallas kernels for 6% -> 7%
where the time goes in v7:
time: 58.7 us; the launch traced here: 58.4 us
  starting transfers between devices  17.1 us (29%)
  Pallas kernels  15.9 us (27%)
  waiting for transfers between devices  14.7 us (25%)
  blocking collectives  9.1 us (16%)
  local copies, waits for them, and re-layouts  0.89 us (2%)
  between operations  0.76 us (1%)
    pallas_call x10, Pallas kernels, on_chip(): pl.pallas_call(kernel, out_shape=tuple((jax.ShapeDtypeStruct(shape, kind)...  14.5 us
    ppermute x10, starting transfers between devices, swapped(): return lax.ppermute(value, AXES, [(i, i ^ flip) for i in range(devices)])  10.6 us
    all_to_all x1, blocking collectives, body(): coefs = lax.all_to_all(solve_leaf(parts, devices), AXES, 0, 0, tiled=True)  9.1 us
    ppermute x1, waiting for transfers between devices, body(): lax.ppermute(mine, AXES, [(d, d ^ (1 if o else 16)) for d, o in enumerate...  8.66 us
    ppermute x1, starting transfers between devices, body(): lax.ppermute(outer, AXES, [(i, (i + (1 if i % 2 else -1)) % devices) for...  6.44 us
    ppermute x10, waiting for transfers between devices, swapped(): return lax.ppermute(value, AXES, [(i, i ^ flip) for i in range(devices)])  5.99 us
    pallas_call x1, Pallas kernels, edges(): pl.pallas_call(edge_kernel, out_shape=(edge, edge, jax.ShapeDtypeStruct((...  1.41 us
  transfers between devices with their start and end apart: 12, of which 5 were waited for; matrix products, arithmetic and copies ran while one was open for 0% of the time, Pallas kernels for 7%

profile of v7, /device:TPU:0, one launch (start us, length us, event | category | flops | bytes accessed | tf_op | source)
XLA Modules:
  0.0 58.4 jit_solution(14828301964985439516)
XLA Ops:
  0.6 1.4 %shard_map.85 = (f32[4,128]{1,0:T(4,128)}, f32[4,128]{1,0:T(4,128)}, f32[5,8,128]{2,1,0:T(8,128)}) custom-call(s32[8,128]{1,0:T(8,128)} %bitcast.8, s32[8,128]{1,0:T(8,128)} %bitcast.9, s32[8,128]{1,0:T(8,128)} %bitcast.10, f32[8,128]{1,0:T(8,128)} %bitcast.11, s32[8,128]{1,0:T(8,128)} %bitcast.12), custom_call_target="tpu_custom_call" | custom-call | tf_op jit(solution)/shard_map/pallas_call | solution.py:87
  2.0 0.0 copy-start.3
  2.1 0.5 collective-permute-start
  2.6 0.2 copy-done.3
  2.7 6.4 %collective-permute-start.1 = (f32[4,128]{1,0:T(4,128)S(1)}, f32[4,128]{1,0:T(4,128)S(1)}, u32[]{:S(2)}, u32[]{:S(2)}) collective-permute-start(f32[4,128]{1,0:T(4,128)S(1)} %copy-done.3), channel_id=1, source_target_pairs={{0,31},{1,2},{2,1},{3,4},{4,3},{5,6},{6,5},{7,8},{8,7},{9,10},{10,... | collective-permute-start | bytes 6152 | tf_op jit(solution)/shard_map/ppermute | solution.py:522
  9.2 0.7 %copy-done.1 = f32[5,8,128]{2,1,0:T(8,128)S(1)} copy-done((f32[5,8,128]{2,1,0:T(8,128)S(1)}, f32[5,8,128]{2,1,0:T(8,128)}, u32[]{:S(2)}) %copy-start.1) | copy-done | bytes 20504
  9.9 1.7 %shard_map.86 = (f32[8,128]{1,0:T(8,128)S(1)}, f32[8,128]{1,0:T(8,128)S(1)}, f32[4,8,128]{2,1,0:T(8,128)S(1)}, s32[2,8,128]{2,1,0:T(8,128)S(1)}) custom-call(f32[5,8,128]{2,1,0:T(8,128)S(1)} %copy-done.1), custom_call_target="tpu_custom_call" | custom-call | flops 2621440000 | bytes 131072 | tf_op jit(solution)/shard_map/pallas_call | solution.py:297
  11.6 0.0 collective-permute-done.inner
  11.6 2.0 %shard_map.87 = (f32[8,128]{1,0:T(8,128)}, f32[4,264,128]{2,1,0:T(8,128)S(1)}, bf16[256,1024]{1,0:T(8,128)(2,1)S(1)}, f32[16,256]{1,0:T(8,128)S(1)}, f32[16,256]...) custom-call(f32[5,8,128]{2,1,0:T(8,128)S(1)} %copy-done.1, bf16[1024,256]{1,0:T(8,128)(2,1)S(1)} %copy-done, ...), custom_call_target="tpu_custom_call" | custom-call | tf_op jit(solution)/shard_map/pallas_call | solution.py:297
  13.6 0.0 collective-permute-start.2
  13.6 0.7 %shard_map.91 = f32[4,264,128]{2,1,0:T(8,128)S(1)} custom-call(f32[5,8,128]{2,1,0:T(8,128)S(1)} %copy-done.1, bf16[1024,256]{1,0:T(8,128)(2,1)S(1)} %get-tuple-element.35.x_ref, bf16[256,1024]{1,0:T(8,128)(2,1)S(1)} %get-tuple-element.36.weighted, f32[16,256]{1,0:T(8,128)S(1)} %get-tuple-element.37.moment_s, f32[16,256]{1,0:T(8,128)S(1)} %get-tuple-element.38.hsum_s, ...), custom_call_target="tpu_custom_call" | custom-call | flops 2147483648 | bytes 262144 | tf_op jit(solution)/shard_map/pallas_call | solution.py:297
  14.3 0.6 collective-permute-start.6
  14.9 0.7 %shard_map.88.keep_ref = f32[4,264,128]{2,1,0:T(8,128)S(1)} custom-call(f32[5,8,128]{2,1,0:T(8,128)S(1)} %copy-done.1, bf16[1024,256]{1,0:T(8,128)(2,1)S(1)} %get-tuple-element.35.x_ref, bf16[256,1024]{1,0:T(8,128)(2,1)S(1)} %get-tuple-element.36.weighted, f32[16,256]{1,0:T(8,128)S(1)} %get-tuple-element.37.moment_s, ...), custom_call_target="tpu_custom_call" | custom-call | flops 2147483648 | bytes 262144 | tf_op jit(solution)/shard_map/pallas_call | solution.py:297
  15.6 0.1 shard_map.89
  15.7 0.1 collective-permute-start.3
  15.8 0.1 collective-permute-start.4
  15.9 0.7 %shard_map.90.keep_ref = f32[4,264,128]{2,1,0:T(8,128)S(1)} custom-call(f32[5,8,128]{2,1,0:T(8,128)S(1)} %copy-done.1, bf16[1024,256]{1,0:T(8,128)(2,1)S(1)} %get-tuple-element.35.x_ref, bf16[256,1024]{1,0:T(8,128)(2,1)S(1)} %get-tuple-element.36.weighted, f32[16,256]{1,0:T(8,128)S(1)} %get-tuple-element.37.moment_s, ...), custom_call_target="tpu_custom_call" | custom-call | flops 2147483648 | bytes 262144 | tf_op jit(solution)/shard_map/pallas_call | solution.py:297
  16.6 1.3 %collective-permute-start.5 = (f32[264,128]{1,0:T(8,128)S(1)}, f32[264,128]{1,0:T(8,128)S(1)}, u32[]{:S(2)}, u32[]{:S(2)}) collective-permute-start(f32[264,128]{1,0:T(8,128)S(1)} %get-tuple-element.44), channel_id=1, source_target_pairs={{0,2},{1,3},{2,0},{3,1},{4,6},{5,7},{6,4},{7,5},{8,10},{9,11},{10,... | collective-permute-start | bytes 405512 | tf_op jit(solution)/shard_map/ppermute | solution.py:517
  17.9 0.1 shard_map.92
  18.0 3.7 %collective-permute-start.7 = (f32[264,128]{1,0:T(8,128)S(1)}, f32[264,128]{1,0:T(8,128)S(1)}, u32[]{:S(2)}, u32[]{:S(2)}) collective-permute-start(f32[264,128]{1,0:T(8,128)S(1)} %get-tuple-element.45), channel_id=1, source_target_pairs={{0,14},{1,15},{2,12},{3,13},{4,10},{5,11},{6,8},{7,9},{8,6},{9,7},... | collective-permute-start | bytes 405512 | tf_op jit(solution)/shard_map/ppermute | solution.py:517
  21.7 0.9 %collective-permute-start.9 = (f32[264,128]{1,0:T(8,128)S(1)}, f32[264,128]{1,0:T(8,128)S(1)}, u32[]{:S(2)}, u32[]{:S(2)}) collective-permute-start(f32[264,128]{1,0:T(8,128)S(1)} %get-tuple-element.47), channel_id=1, source_target_pairs={{0,10},{1,11},{2,8},{3,9},{4,14},{5,15},{6,12},{7,13},{8,2},{9,3},... | collective-permute-start | bytes 405512 | tf_op jit(solution)/shard_map/ppermute | solution.py:517
  22.6 3.5 %collective-permute-start.10 = (f32[264,128]{1,0:T(8,128)S(1)}, f32[264,128]{1,0:T(8,128)S(1)}, u32[]{:S(2)}, u32[]{:S(2)}) collective-permute-start(f32[264,128]{1,0:T(8,128)S(1)} %get-tuple-element.48), channel_id=1, source_target_pairs={{0,6},{1,7},{2,4},{3,5},{4,2},{5,3},{6,0},{7,1},{8,14},{9,15},{10,... | collective-permute-start | bytes 405512 | tf_op jit(solution)/shard_map/ppermute | solution.py:517
  26.0 0.8 %collective-permute-done.7.refs_4_ = f32[264,128]{1,0:T(8,128)S(1)} collective-permute-done((f32[264,128]{1,0:T(8,128)S(1)}, f32[264,128]{1,0:T(8,128)S(1)}, u32[]{:S(2)}, u32[]{:S(2)}) %collective-permute-start.7) | collective-permute-done | bytes 135200 | tf_op jit(solution)/shard_map/ppermute | solution.py:517
  26.9 2.7 %collective-permute-done.8.refs_5_ = f32[264,128]{1,0:T(8,128)S(1)} collective-permute-done((f32[264,128]{1,0:T(8,128)S(1)}, f32[264,128]{1,0:T(8,128)S(1)}, u32[]{:S(2)}, u32[]{:S(2)}) %collective-permute-start.8) | collective-permute-done | bytes 135200 | tf_op jit(solution)/shard_map/ppermute | solution.py:517
  29.6 0.7 %collective-permute-done.9.refs_6_ = f32[264,128]{1,0:T(8,128)S(1)} collective-permute-done((f32[264,128]{1,0:T(8,128)S(1)}, f32[264,128]{1,0:T(8,128)S(1)}, u32[]{:S(2)}, u32[]{:S(2)}) %collective-permute-start.9) | collective-permute-done | bytes 135200 | tf_op jit(solution)/shard_map/ppermute | solution.py:517
  30.3 1.7 %collective-permute-done.10.refs_7_ = f32[264,128]{1,0:T(8,128)S(1)} collective-permute-done((f32[264,128]{1,0:T(8,128)S(1)}, f32[264,128]{1,0:T(8,128)S(1)}, u32[]{:S(2)}, u32[]{:S(2)}) %collective-permute-start.10) | collective-permute-done | bytes 135200 | tf_op jit(solution)/shard_map/ppermute | solution.py:517
  32.0 0.1 shard_map.93.refs_0_
  32.1 0.1 collective-permute-start.11
  32.2 8.7 %collective-permute-done.11.refs_1_ = f32[264,128]{1,0:T(8,128)S(1)} collective-permute-done((f32[264,128]{1,0:T(8,128)S(1)}, f32[264,128]{1,0:T(8,128)S(1)}, u32[]{:S(2)}, u32[]{:S(2)}) %collective-permute-start.11) | collective-permute-done | bytes 135200 | tf_op jit(solution)/shard_map/ppermute | solution.py:536
  40.8 7.6 %shard_map.94 = f32[32,4,128]{2,1,0:T(4,128)S(1)} custom-call(f32[264,128]{1,0:T(8,128)S(1)} %shard_map.93.refs_0_, f32[264,128]{1,0:T(8,128)S(1)} %collective-permute-done.11.refs_1_), custom_call_target="tpu_custom_call" | custom-call | tf_op jit(solution)/shard_map/pallas_call | solution.py:297
  48.5 9.1 %all_to_all.5.coef_ref = f32[32,4,128]{2,1,0:T(4,128)S(1)} all-to-all(f32[32,4,128]{2,1,0:T(4,128)S(1)} %shard_map.94), channel_id=1, replica_groups=mesh['doc'=8,'leaf'=4] {'doc','leaf'}, dimensions={0} | all-to-all | bytes 131072 | tf_op jit(solution)/shard_map/all_to_all | solution.py:542
  57.6 0.9 %shard_map.95 = (f32[8,128]{1,0:T(8,128)}, f32[8,128]{1,0:T(8,128)}) custom-call(f32[5,8,128]{2,1,0:T(8,128)S(1)} %copy-done.2, bf16[1024,256]{1,0:T(8,128)(2,1)S(1)} %copy-done, f32[32,4,128]{2,1,0:T(4,128)S(1)} %all_to_all.5.coef_ref), custom_call_target="tpu_custom_call" | custom-call | tf_op jit(solution)/shard_map/pallas_call | solution.py:297
  (12 shorter events, 0.0 us)
Async XLA Ops:
  2.0 0.7 %copy-start.3 = (f32[4,128]{1,0:T(4,128)S(1)}, f32[4,128]{1,0:T(4,128)}, u32[]{:S(2)}) copy-start(f32[4,128]{1,0:T(4,128)} %get-tuple-element.29) | copy-start | bytes 6148
  2.1 9.6 %collective-permute-start = (f32[4,128]{1,0:T(4,128)}, f32[4,128]{1,0:T(4,128)S(1)}, u32[]{:S(2)}, u32[]{:S(2)}) collective-permute-start(f32[4,128]{1,0:T(4,128)} %get-tuple-element.28), channel_id=1, source_target_pairs={{0,1},{1,0},{2,3},{3,2},{4,5},{5,4},{6,7},{7,6},{8,9},{9,8},{10,11... | collective-permute-start | bytes 6152 | tf_op jit(solution)/shard_map/ppermute | solution.py:517
  2.7 8.9 %collective-permute-start.1 = (f32[4,128]{1,0:T(4,128)S(1)}, f32[4,128]{1,0:T(4,128)S(1)}, u32[]{:S(2)}, u32[]{:S(2)}) collective-permute-start(f32[4,128]{1,0:T(4,128)S(1)} %copy-done.3), channel_id=1, source_target_pairs={{0,31},{1,2},{2,1},{3,4},{4,3},{5,6},{6,5},{7,8},{8,7},{9,10},{10,... | collective-permute-start | bytes 6152 | tf_op jit(solution)/shard_map/ppermute | solution.py:522
  9.2 0.7 %copy-start.1 = (f32[5,8,128]{2,1,0:T(8,128)S(1)}, f32[5,8,128]{2,1,0:T(8,128)}, u32[]{:S(2)}) copy-start(f32[5,8,128]{2,1,0:T(8,128)} %get-tuple-element.27.table) | copy-start | bytes 61444
  9.9 1.7 %copy-start = (bf16[1024,256]{1,0:T(8,128)(2,1)S(1)}, bf16[1024,256]{1,0:T(8,128)(2,1)}, u32[]{:S(2)}) copy-start(bf16[1024,256]{1,0:T(8,128)(2,1)} %x_ref.3) | copy-start | bytes 1572868
  13.6 2.0 %collective-permute-start.2 = (f32[4,264,128]{2,1,0:T(8,128)S(1)}, f32[4,264,128]{2,1,0:T(8,128)S(1)}, u32[]{:S(2)}, u32[]{:S(2)}) collective-permute-start(f32[4,264,128]{2,1,0:T(8,128)S(1)} %get-tuple-element.40), channel_id=1, source_target_pairs={{0,1},{1,0},{2,3},{3,2},{4,5},{5,4},{6,7},{7,6},{8,9},{9,8},{10,11... | collective-permute-start | bytes 1622024 | tf_op jit(solution)/shard_map/ppermute | solution.py:517
  14.3 3.6 %collective-permute-start.6 = (f32[4,264,128]{2,1,0:T(8,128)S(1)}, f32[4,264,128]{2,1,0:T(8,128)S(1)}, u32[]{:S(2)}, u32[]{:S(2)}) collective-permute-start(f32[4,264,128]{2,1,0:T(8,128)S(1)} %shard_map.91), channel_id=1, source_target_pairs={{0,1},{1,0},{2,3},{3,2},{4,5},{5,4},{6,7},{7,6},{8,9},{9,8},{10,11... | collective-permute-start | bytes 1622024 | tf_op jit(solution)/shard_map/ppermute | solution.py:517
  15.7 6.0 %collective-permute-start.3 = (f32[264,128]{1,0:T(8,128)S(1)}, f32[264,128]{1,0:T(8,128)S(1)}, u32[]{:S(2)}, u32[]{:S(2)}) collective-permute-start(f32[264,128]{1,0:T(8,128)S(1)} %get-tuple-element.42), channel_id=1, source_target_pairs={{0,8},{1,9},{2,10},{3,11},{4,12},{5,13},{6,14},{7,15},{8,0},{9,1},... | collective-permute-start | bytes 405512 | tf_op jit(solution)/shard_map/ppermute | solution.py:517
  15.8 6.8 %collective-permute-start.4 = (f32[264,128]{1,0:T(8,128)S(1)}, f32[264,128]{1,0:T(8,128)S(1)}, u32[]{:S(2)}, u32[]{:S(2)}) collective-permute-start(f32[264,128]{1,0:T(8,128)S(1)} %get-tuple-element.43), channel_id=1, source_target_pairs={{0,4},{1,5},{2,6},{3,7},{4,0},{5,1},{6,2},{7,3},{8,12},{9,13},{10,... | collective-permute-start | bytes 405512 | tf_op jit(solution)/shard_map/ppermute | solution.py:517
  16.6 9.5 %collective-permute-start.5 = (f32[264,128]{1,0:T(8,128)S(1)}, f32[264,128]{1,0:T(8,128)S(1)}, u32[]{:S(2)}, u32[]{:S(2)}) collective-permute-start(f32[264,128]{1,0:T(8,128)S(1)} %get-tuple-element.44), channel_id=1, source_target_pairs={{0,2},{1,3},{2,0},{3,1},{4,6},{5,7},{6,4},{7,5},{8,10},{9,11},{10,... | collective-permute-start | bytes 405512 | tf_op jit(solution)/shard_map/ppermute | solution.py:517
  18.0 8.9 %collective-permute-start.7 = (f32[264,128]{1,0:T(8,128)S(1)}, f32[264,128]{1,0:T(8,128)S(1)}, u32[]{:S(2)}, u32[]{:S(2)}) collective-permute-start(f32[264,128]{1,0:T(8,128)S(1)} %get-tuple-element.45), channel_id=1, source_target_pairs={{0,14},{1,15},{2,12},{3,13},{4,10},{5,11},{6,8},{7,9},{8,6},{9,7},... | collective-permute-start | bytes 405512 | tf_op jit(solution)/shard_map/ppermute | solution.py:517
  21.6 8.0 %collective-permute-start.8 = (f32[264,128]{1,0:T(8,128)S(1)}, f32[264,128]{1,0:T(8,128)S(1)}, u32[]{:S(2)}, u32[]{:S(2)}) collective-permute-start(f32[264,128]{1,0:T(8,128)S(1)} %get-tuple-element.46), channel_id=1, source_target_pairs={{0,12},{1,13},{2,14},{3,15},{4,8},{5,9},{6,10},{7,11},{8,4},{9,5},... | collective-permute-start | bytes 405512 | tf_op jit(solution)/shard_map/ppermute | solution.py:517
  21.7 8.7 %collective-permute-start.9 = (f32[264,128]{1,0:T(8,128)S(1)}, f32[264,128]{1,0:T(8,128)S(1)}, u32[]{:S(2)}, u32[]{:S(2)}) collective-permute-start(f32[264,128]{1,0:T(8,128)S(1)} %get-tuple-element.47), channel_id=1, source_target_pairs={{0,10},{1,11},{2,8},{3,9},{4,14},{5,15},{6,12},{7,13},{8,2},{9,3},... | collective-permute-start | bytes 405512 | tf_op jit(solution)/shard_map/ppermute | solution.py:517
  22.6 9.4 %collective-permute-start.10 = (f32[264,128]{1,0:T(8,128)S(1)}, f32[264,128]{1,0:T(8,128)S(1)}, u32[]{:S(2)}, u32[]{:S(2)}) collective-permute-start(f32[264,128]{1,0:T(8,128)S(1)} %get-tuple-element.48), channel_id=1, source_target_pairs={{0,6},{1,7},{2,4},{3,5},{4,2},{5,3},{6,0},{7,1},{8,14},{9,15},{10,... | collective-permute-start | bytes 405512 | tf_op jit(solution)/shard_map/ppermute | solution.py:517
  32.1 8.7 %collective-permute-start.11 = (f32[264,128]{1,0:T(8,128)S(1)}, f32[264,128]{1,0:T(8,128)S(1)}, u32[]{:S(2)}, u32[]{:S(2)}) collective-permute-start(f32[264,128]{1,0:T(8,128)S(1)} %shard_map.93.refs_0_), channel_id=1, source_target_pairs={{0,1},{1,17},{2,3},{3,19},{4,5},{5,21},{6,7},{7,23},{8,9},{9,25},{... | collective-permute-start | bytes 405512 | tf_op jit(solution)/shard_map/ppermute | solution.py:536
  48.4 9.1 %copy-start.2 = (f32[5,8,128]{2,1,0:T(8,128)S(1)}, f32[5,8,128]{2,1,0:T(8,128)}, u32[]{:S(2)}) copy-start(f32[5,8,128]{2,1,0:T(8,128)} %get-tuple-element.27.table) | copy-start | bytes 61444
